TPU v7x, 128 devices: a whole 4x4x4 slice. The times are simulated.
128 devices in a mesh: dp: 2 (over y_hi), seq: 16 (over x, y_lo, core), tp: 4 (over z).
Axes of the slice: x: 4, y: 4 (y_hi: 2, y_lo: 2; y = y_hi * 2 + y_lo), z: 4, core: 2. Of those that a mesh axis runs over, the one named last changes fastest.
Arguments:
- enc_context: bfloat16 [8, 512, 4096], P('dp', 'seq', 'tp'), may hold values from -6 to 6
- enc_residual: bfloat16 [8, 512, 4096], P('dp', 'seq', 'tp'), may hold values from -96 to 96
- out_weight: bfloat16 [4096, 4096], P('tp'), may hold values from -0.09375 to 0.09375
- norm_gain: float32 [4096], replicated, may hold values from 0.1 to 1.9
- kv_weight: bfloat16 [4096, 2, 4096], P(None, None, 'seq'), may hold values from -0.09375 to 0.09375
- caption_lengths: int32 [8], P(('dp', 'tp')), may hold values from 64 to 512, as said below
- streams: bfloat16 [4, 8, 2048, 4096], P(None, ('dp', 'tp'), 'seq'), may hold values from -96 to 96
- cotangents: bfloat16 [2, 8, 2048, 4096], P(None, ('dp', 'tp'), 'seq'), may hold values from -6 to 6
Outputs:
- self_ctx: bfloat16 [8, 2048, 4096], P(('dp', 'tp'), 'seq')
- cross_ctx: bfloat16 [8, 2048, 4096], P(('dp', 'tp'), 'seq')
- stream_grads: bfloat16 [4, 8, 2048, 4096], P(None, ('dp', 'tp'), 'seq')
- kv_weight_grad: float32 [4096, 2, 4096], P(('dp', 'tp'), None, 'seq')
Inputs may be any that keep to these rules, and one draw needn't show every extreme that they name: The first caption_lengths[c] caption tokens of clip c are valid; some caption uses all 512.
All inputs are finite; a program needn't handle non-finite values.
Results may differ from a plain program's by a relative error of at most 0.03035.
Values may be sent and summed in bfloat16 or wider, within the bound.
No kernel may reach another device: no remote copies, remote signals or barrier semaphores. Data moves between devices by JAX's collectives and lax.ppermute only.
A program may use at most 192 MiB of HBM per device.

v0:
```python
import math

import jax
import jax.numpy as jnp
from jax import lax
from jax.sharding import PartitionSpec as P

D_TEXT = 4096
HD = 128


def attend(queries, keys, values, cotangent, valid):
    total, heads_here, depth = queries.shape
    scale = 1.0 / math.sqrt(depth)
    block = max(min(512, total), total // 16)
    count = total // block

    def step(carry, pieces):
        grad_keys, grad_values = carry
        query_block, cot_block = pieces
        scores = (
            jnp.einsum("qhd,khd->hqk", query_block, keys, preferred_element_type=jnp.float32)
            * scale
        )
        scores = jnp.where(valid[None, None, :], scores, -1e30)
        top = jnp.max(scores, axis=2, keepdims=True)
        weights = jnp.exp(scores - top)
        probs = weights / jnp.sum(weights, axis=2, keepdims=True)
        rounded = probs.astype(jnp.bfloat16)
        context = jnp.einsum(
            "hqk,khd->qhd", rounded, values, preferred_element_type=jnp.float32
        ).astype(jnp.bfloat16)
        value_part = jnp.einsum(
            "hqk,qhd->khd", rounded, cot_block, preferred_element_type=jnp.float32
        )
        grad_probs = jnp.einsum(
            "qhd,khd->hqk", cot_block, values, preferred_element_type=jnp.float32
        )
        centre = jnp.sum(probs * grad_probs, axis=2, keepdims=True)
        grad_scores = (probs * (grad_probs - centre) * scale).astype(jnp.bfloat16)
        grad_query = jnp.einsum(
            "hqk,khd->qhd", grad_scores, keys, preferred_element_type=jnp.float32
        ).astype(jnp.bfloat16)
        key_part = jnp.einsum(
            "hqk,qhd->khd", grad_scores, query_block, preferred_element_type=jnp.float32
        )
        return ((grad_keys + key_part, grad_values + value_part), (context, grad_query))

    empty = jnp.zeros(keys.shape, jnp.float32)
    blocked = (
        queries.reshape(count, block, heads_here, depth),
        cotangent.reshape(count, block, heads_here, depth),
    )
    (grad_keys, grad_values), (context, grad_query) = lax.scan(step, (empty, empty), blocked)
    width = heads_here * depth
    return (
        context.reshape(total, width),
        grad_query.reshape(total, width),
        grad_keys.astype(jnp.bfloat16).reshape(keys.shape[0], width),
        grad_values.astype(jnp.bfloat16).reshape(keys.shape[0], width),
    )


def to_heads(array, depth):
    return array.reshape(array.shape[0], array.shape[1] // depth, depth)


def body(
    enc_context,
    enc_residual,
    out_weight,
    norm_gain,
    kv_weight,
    caption_lengths,
    streams,
    cotangents,
):
    owned, caption_rows, feature_part = enc_context.shape
    partial_value = jnp.dot(
        enc_context.reshape(owned * caption_rows, feature_part),
        out_weight,
        preferred_element_type=jnp.float32,
    ).reshape(owned, caption_rows, D_TEXT)
    summed = lax.psum_scatter(partial_value, "tp", scatter_dimension=2, tiled=True)
    hidden = summed + enc_residual.astype(jnp.float32)
    power = lax.psum(jnp.sum(hidden * hidden, axis=2, keepdims=True), "tp") / D_TEXT
    gain_part = lax.dynamic_slice_in_dim(
        norm_gain, lax.axis_index("tp") * feature_part, feature_part
    )
    normed = (hidden * lax.rsqrt(power + 1e-06) * gain_part).astype(jnp.bfloat16)
    mine = lax.all_to_all(normed, "tp", split_axis=0, concat_axis=2, tiled=True)
    states = lax.all_gather(mine, "seq", axis=1, tiled=True)[0]
    local_width = kv_weight.shape[2]
    caption_kv = jnp.dot(
        states, kv_weight.reshape(D_TEXT, 2 * local_width), preferred_element_type=jnp.float32
    ).astype(jnp.bfloat16)
    caption_keys = to_heads(caption_kv[:, :local_width], HD)
    caption_values = to_heads(caption_kv[:, local_width:], HD)
    head_in, head_cot = (
        lax.all_to_all(streams, "seq", split_axis=3, concat_axis=2, tiled=True),
        lax.all_to_all(cotangents, "seq", split_axis=3, concat_axis=2, tiled=True),
    )
    cross_query = head_in[3, 0]
    cross_cot = head_cot[1, 0]
    everything = jnp.arange(head_in.shape[2], dtype=jnp.int32) >= 0
    self_ctx, self_dq, self_dk, self_dv = attend(
        to_heads(head_in[0, 0], HD),
        to_heads(head_in[1, 0], HD),
        to_heads(head_in[2, 0], HD),
        to_heads(head_cot[0, 0], HD),
        everything,
    )
    valid = jnp.arange(states.shape[0], dtype=jnp.int32) < caption_lengths[0]
    cross_ctx, cross_dq, cross_dk, cross_dv = attend(
        to_heads(cross_query, HD), caption_keys, caption_values, to_heads(cross_cot, HD), valid
    )
    contexts = jnp.stack([self_ctx, cross_ctx])[:, None]
    grads = jnp.stack([self_dq, self_dk, self_dv, cross_dq])[:, None]
    token_contexts, token_grads = (
        lax.all_to_all(contexts, "seq", split_axis=2, concat_axis=3, tiled=True),
        lax.all_to_all(grads, "seq", split_axis=2, concat_axis=3, tiled=True),
    )
    caption_grads = jnp.concatenate([cross_dk, cross_dv], axis=1)
    grad = lax.psum_scatter(
        lax.dot_general(
            states, caption_grads, (((0,), (0,)), ((), ())), preferred_element_type=jnp.float32
        ),
        ("dp", "tp"),
        scatter_dimension=0,
        tiled=True,
    )
    weight_grad = grad.reshape(grad.shape[0], 2, local_width)
    return (token_contexts[0], token_contexts[1], token_grads, weight_grad)


def solution(mesh):
    placed = (
        P("dp", "seq", "tp"),
        P("dp", "seq", "tp"),
        P("tp", None),
        P(),
        P(None, None, "seq"),
        P(("dp", "tp")),
        P(None, ("dp", "tp"), "seq", None),
        P(None, ("dp", "tp"), "seq", None),
    )
    return jax.shard_map(
        body,
        mesh=mesh,
        in_specs=placed,
        out_specs=(
            P(("dp", "tp"), "seq", None),
            P(("dp", "tp"), "seq", None),
            P(None, ("dp", "tp"), "seq", None),
            P(("dp", "tp"), None, "seq"),
        ),
        check_vma=False,
    )
```

profile of v0, /device:TPU:9, one launch (start us, length us, event | category | flops | bytes accessed | tf_op | source)
XLA Modules:
  0.0 679.4 jit_solution(3980350477142792683)
XLA Ops:
  15.0 31.5 %reduce-scatter.3.cloned.1.call-done = f32[4,32,1024]{2,1,0:T(8,128)} async-done(((f32[4,32,4096]{2,1,0:T(8,128)}), f32[4,32,1024]{2,1,0:T(8,128)}) %reduce-scatter.3.cloned.1.call-update) | async-done | bytes 524304 | tf_op jit(solution)/shard_map/reduce_scatter | solution.py:84
  47.7 6.5 psum.7
  55.4 7.9 %all_to_all.81 = bf16[4,32,1024]{2,1,0:T(8,128)(2,1)S(1)} all-to-all(bf16[4,32,1024]{2,1,0:T(8,128)(2,1)S(1)} %multiply_convert_fusion.2), channel_id=1, replica_groups=mesh['dp'=2,'seq'=16,'tp'=4] {'tp'}, dimensions={0} | all-to-all | bytes 524288 | tf_op jit(solution)/shard_map/all_to_all | solution.py:91
  67.8 9.1 %all-to-all-start.1 = ((bf16[2,1,128,4096]{2,0,1,3:T(2,128)(2,1)}), bf16[2,1,128,4096]{2,0,1,3:T(2,128)(2,1)S(1)}, u32[]{:S(2)}, u32[]{:S(2)}) async-start(bf16[2,1,128,4096]{2,0,1,3:T(2,128)(2,1)} %copy.176), calls=%async_computation.1 | async-start | bytes 4194304 | tf_op jit(solution)/shard_map/all_to_all | solution.py:101
  77.0 7.4 %copy.172 = bf16[4,1,128,4096]{2,0,1,3:T(4,128)(2,1)} copy(bf16[4,1,128,4096]{3,2,1,0:T(8,128)(2,1)} %param.18) | data formatting | bytes 8388608 | tf_op args[6]
  84.4 33.5 %all-to-all-done.1 = bf16[2,1,128,4096]{2,0,1,3:T(2,128)(2,1)S(1)} async-done(((bf16[2,1,128,4096]{2,0,1,3:T(2,128)(2,1)}), bf16[2,1,128,4096]{2,0,1,3:T(2,128)(2,1)S(1)}, u32[]{:S(2)}, u32[]{:S(2)}) %all-to-all-start.1) | async-done | bytes 2097184 | tf_op jit(solution)/shard_map/all_to_all | solution.py:101
  130.7 48.6 %all-to-all-done = bf16[4,1,128,4096]{2,0,1,3:T(4,128)(2,1)} async-done(((bf16[4,1,128,4096]{2,0,1,3:T(4,128)(2,1)}), bf16[4,1,128,4096]{2,0,1,3:T(4,128)(2,1)}, u32[]{:S(2)}, u32[]{:S(2)}) %all-to-all-start) | async-done | bytes 4194336 | tf_op jit(solution)/shard_map/all_to_all | solution.py:100
  213.3 89.5 %while.36 = (s32[]{:T(128)}, f32[512,2,128]{0,2,1:T(8,128)}, f32[512,2,128]{0,2,1:T(8,128)}, bf16[4,512,2,128]{3,2,1,0:T(2,128)(2,1)}, bf16[4,512,2,128]{3,2,1,0...) while((s32[]{:T(128)}, f32[512,2,128]{0,2,1:T(8,128)}, ...), condition=%wide.region_12.13_spmd.clone, body=%wide.region_8.12_spmd.clone.sunk | while | flops 817631232 | bytes 42489152 | solution.py:54
  305.0 7.8 %fusion.91 = f32[4096,512]{1,0:T(8,128)} fusion(bf16[1,512,4096]{2,1,0:T(8,128)(2,1)} %all-gather.2.cloned.1.call-done, bf16[512,256]{0,1:T(8,128)(2,1)S(1)} %bitcast.198, bf16[512,256]{0,1:T(8,128)(2,1)S(1)} %bitcast.197), kind=kOutput, calls=%fused_computation.82 | convolution fusion | flops 2148532224 | bytes 13107200 | tf_op jit(solution)/shard_map/dot_general | solution.py:125
  314.9 221.9 %while.35 = (s32[]{:T(128)}, f32[2048,2,128]{0,2,1:T(8,128)}, f32[2048,2,128]{0,2,1:T(8,128)}, bf16[4,512,2,128]{3,2,1,0:T(2,128)(2,1)S(1)}, bf16[4,512,2,128]{3...) while((s32[]{:T(128)}, f32[2048,2,128]{0,2,1:T(8,128)}, ...), condition=%wide.region_4.5_spmd.clone, body=%wide.region_0.4_spmd.clone.sunk | while | flops 3267633152 | bytes 83382400 | solution.py:54
  321.8 7.4 %fusion.156 = (f32[2,512]{1,0:T(2,128)S(1)}, f32[2,512,2048]{2,1,0:T(8,128)}) fusion(bf16[2048,2,128]{2,0,1:T(8,128)(2,1)} %get-tuple-element.588, bf16[1,512,2,128]{3,2,1,0:T(2,128)(2,1)S(1)} %constant_dynamic-slice_fusion.9), kind=kOutput, calls=%fused_computation.96.clone.1 | convolution fusion | flops 543164416 | bytes 9703424 | tf_op jit(solution)/shard_map/while/body/eval_jaxpr/sub | solution.py:27
  333.9 13.6 %fusion.159 = bf16[1,512,2,128]{3,1,2,0:T(8,128)(2,1)S(1)} fusion(bf16[2048,2,128]{2,0,1:T(8,128)(2,1)} %get-tuple-element.588, f32[2,512,2048]{2,1,0:T(8,128)} %fusion.155, f32[2,512,2048]{2,1,0:T(8,128)} %get-tuple-element.506, f32[2,512]{1,0:T(2,128)S(1)} %get-tuple-element.507), kind=kOutput, calls=%fused_computation.22.clone.1 | convolution fusion | flops 551685120 | bytes 18092032 | tf_op jit(solution)/shard_map/while/body/eval_jaxpr/hqk,khd->qhd/dot_general | solution.py:41
  347.5 16.2 %fusion.157 = f32[2048,2,128]{0,2,1:T(8,128)} fusion(f32[2,512,2048]{2,1,0:T(8,128)} %fusion.155, f32[2048,2,128]{0,2,1:T(8,128)} %get-tuple-element.572, pred[]{:T(512)S(6)} %compare.6, bf16[1,512,2,128]{3,2,1,0:T(2,128)(2,1)S(1)} %constant_dynamic-slice_fusion.9, f32[2,512,2048]{2,1,0:T(8,128)} %get-tuple-element.506, ...), kind=kOutput, calls=%fused_computation.16.clone.1 | convolution fusion | flops 552602624 | bytes 21237760 | tf_op jit(solution)/shard_map/while/body/eval_jaxpr/hqk,qhd->khd/dot_general | solution.py:44
  377.6 7.1 %fusion.156 = (f32[2,512]{1,0:T(2,128)S(1)}, f32[2,512,2048]{2,1,0:T(8,128)}) fusion(bf16[2048,2,128]{2,0,1:T(8,128)(2,1)} %get-tuple-element.588, bf16[1,512,2,128]{3,2,1,0:T(2,128)(2,1)S(1)} %constant_dynamic-slice_fusion.9), kind=kOutput, calls=%fused_computation.96.clone.1 | convolution fusion | flops 543164416 | bytes 9703424 | tf_op jit(solution)/shard_map/while/body/eval_jaxpr/sub | solution.py:27
  389.4 13.2 %fusion.159 = bf16[1,512,2,128]{3,1,2,0:T(8,128)(2,1)S(1)} fusion(bf16[2048,2,128]{2,0,1:T(8,128)(2,1)} %get-tuple-element.588, f32[2,512,2048]{2,1,0:T(8,128)} %fusion.155, f32[2,512,2048]{2,1,0:T(8,128)} %get-tuple-element.506, f32[2,512]{1,0:T(2,128)S(1)} %get-tuple-element.507), kind=kOutput, calls=%fused_computation.22.clone.1 | convolution fusion | flops 551685120 | bytes 18092032 | tf_op jit(solution)/shard_map/while/body/eval_jaxpr/hqk,khd->qhd/dot_general | solution.py:41
  402.7 16.6 %fusion.157 = f32[2048,2,128]{0,2,1:T(8,128)} fusion(f32[2,512,2048]{2,1,0:T(8,128)} %fusion.155, f32[2048,2,128]{0,2,1:T(8,128)} %get-tuple-element.572, pred[]{:T(512)S(6)} %compare.6, bf16[1,512,2,128]{3,2,1,0:T(2,128)(2,1)S(1)} %constant_dynamic-slice_fusion.9, f32[2,512,2048]{2,1,0:T(8,128)} %get-tuple-element.506, ...), kind=kOutput, calls=%fused_computation.16.clone.1 | convolution fusion | flops 552602624 | bytes 21237760 | tf_op jit(solution)/shard_map/while/body/eval_jaxpr/hqk,qhd->khd/dot_general | solution.py:44
  419.2 6.5 fusion.158
  433.7 7.1 %fusion.156 = (f32[2,512]{1,0:T(2,128)S(1)}, f32[2,512,2048]{2,1,0:T(8,128)}) fusion(bf16[2048,2,128]{2,0,1:T(8,128)(2,1)} %get-tuple-element.588, bf16[1,512,2,128]{3,2,1,0:T(2,128)(2,1)S(1)} %constant_dynamic-slice_fusion.9), kind=kOutput, calls=%fused_computation.96.clone.1 | convolution fusion | flops 543164416 | bytes 9703424 | tf_op jit(solution)/shard_map/while/body/eval_jaxpr/sub | solution.py:27
  445.5 13.2 %fusion.159 = bf16[1,512,2,128]{3,1,2,0:T(8,128)(2,1)S(1)} fusion(bf16[2048,2,128]{2,0,1:T(8,128)(2,1)} %get-tuple-element.588, f32[2,512,2048]{2,1,0:T(8,128)} %fusion.155, f32[2,512,2048]{2,1,0:T(8,128)} %get-tuple-element.506, f32[2,512]{1,0:T(2,128)S(1)} %get-tuple-element.507), kind=kOutput, calls=%fused_computation.22.clone.1 | convolution fusion | flops 551685120 | bytes 18092032 | tf_op jit(solution)/shard_map/while/body/eval_jaxpr/hqk,khd->qhd/dot_general | solution.py:41
  458.7 15.8 %fusion.157 = f32[2048,2,128]{0,2,1:T(8,128)} fusion(f32[2,512,2048]{2,1,0:T(8,128)} %fusion.155, f32[2048,2,128]{0,2,1:T(8,128)} %get-tuple-element.572, pred[]{:T(512)S(6)} %compare.6, bf16[1,512,2,128]{3,2,1,0:T(2,128)(2,1)S(1)} %constant_dynamic-slice_fusion.9, f32[2,512,2048]{2,1,0:T(8,128)} %get-tuple-element.506, ...), kind=kOutput, calls=%fused_computation.16.clone.1 | convolution fusion | flops 552602624 | bytes 21237760 | tf_op jit(solution)/shard_map/while/body/eval_jaxpr/hqk,qhd->khd/dot_general | solution.py:44
  474.5 6.2 fusion.158
  488.7 7.1 %fusion.156 = (f32[2,512]{1,0:T(2,128)S(1)}, f32[2,512,2048]{2,1,0:T(8,128)}) fusion(bf16[2048,2,128]{2,0,1:T(8,128)(2,1)} %get-tuple-element.588, bf16[1,512,2,128]{3,2,1,0:T(2,128)(2,1)S(1)} %constant_dynamic-slice_fusion.9), kind=kOutput, calls=%fused_computation.96.clone.1 | convolution fusion | flops 543164416 | bytes 9703424 | tf_op jit(solution)/shard_map/while/body/eval_jaxpr/sub | solution.py:27
  500.4 13.2 %fusion.159 = bf16[1,512,2,128]{3,1,2,0:T(8,128)(2,1)S(1)} fusion(bf16[2048,2,128]{2,0,1:T(8,128)(2,1)} %get-tuple-element.588, f32[2,512,2048]{2,1,0:T(8,128)} %fusion.155, f32[2,512,2048]{2,1,0:T(8,128)} %get-tuple-element.506, f32[2,512]{1,0:T(2,128)S(1)} %get-tuple-element.507), kind=kOutput, calls=%fused_computation.22.clone.1 | convolution fusion | flops 551685120 | bytes 18092032 | tf_op jit(solution)/shard_map/while/body/eval_jaxpr/hqk,khd->qhd/dot_general | solution.py:41
  513.6 15.8 %fusion.157 = f32[2048,2,128]{0,2,1:T(8,128)} fusion(f32[2,512,2048]{2,1,0:T(8,128)} %fusion.155, f32[2048,2,128]{0,2,1:T(8,128)} %get-tuple-element.572, pred[]{:T(512)S(6)} %compare.6, bf16[1,512,2,128]{3,2,1,0:T(2,128)(2,1)S(1)} %constant_dynamic-slice_fusion.9, f32[2,512,2048]{2,1,0:T(8,128)} %get-tuple-element.506, ...), kind=kOutput, calls=%fused_computation.16.clone.1 | convolution fusion | flops 552602624 | bytes 21237760 | tf_op jit(solution)/shard_map/while/body/eval_jaxpr/hqk,qhd->khd/dot_general | solution.py:44
  529.4 6.2 fusion.158
  539.5 14.2 %copy.193 = bf16[2,1,2048,256]{3,0,1,2:T(2,128)(2,1)} copy(bf16[2,1,2048,256]{3,2,0,1:T(8,128)(2,1)S(1)} %maximum_bitcast_fusion.1) | data formatting | bytes 4194304 | tf_op jit(solution)/shard_map/broadcast_in_dim | solution.py:117
  553.7 6.4 all-to-all-start.3
  571.6 17.1 %copy.201 = bf16[4,1,2048,256]{3,0,1,2:T(4,128)(2,1)} copy(bf16[4,1,2048,256]{3,2,0,1:T(8,128)(2,1)S(1)} %maximum_bitcast_fusion) | data formatting | bytes 8388608 | tf_op jit(solution)/shard_map/broadcast_in_dim | solution.py:118
  588.7 6.1 all-to-all-start.4
  599.2 53.2 %all-to-all-done.4 = bf16[4,1,2048,256]{3,0,1,2:T(4,128)(2,1)} async-done(((bf16[4,1,2048,256]{3,0,1,2:T(4,128)(2,1)}), bf16[4,1,2048,256]{3,0,1,2:T(4,128)(2,1)}, u32[]{:S(2)}, u32[]{:S(2)}) %all-to-all-start.4) | async-done | bytes 4194336 | tf_op jit(solution)/shard_map/all_to_all | solution.py:121
  657.2 6.2 copy.203
  663.4 6.4 copy.206
  (187 shorter events, 236.9 us)
Async XLA Ops:
  7.2 39.3 %copy-start.10 = (bf16[4,32,1024]{2,1,0:T(8,128)(2,1)S(1)}, bf16[4,32,1024]{2,1,0:T(8,128)(2,1)}, u32[]{:S(2)}) copy-start(bf16[4,32,1024]{2,1,0:T(8,128)(2,1)} %param.13) | copy-start | bytes 786436
  7.2 39.3 %reduce-scatter.3.cloned.1.call-start = ((), (), s32[]{:S(2)}) async-start(), calls=%async_computation.7 | async-start | bytes 2621440 | tf_op jit(solution)/shard_map/reduce_scatter | solution.py:84
  14.1 50.0 %copy-start.9 = (bf16[2,1,128,4096]{3,2,1,0:T(8,128)(2,1)S(1)}, bf16[2,1,128,4096]{3,2,1,0:T(8,128)(2,1)}, u32[]{:S(2)}) copy-start(bf16[2,1,128,4096]{3,2,1,0:T(8,128)(2,1)} %param.19) | copy-start | bytes 6291460
  14.1 187.0 %all-gather.2.cloned.1.call-start = ((), (), s32[]{:S(2)}) async-start(), calls=%async_computation.8 | async-start | bytes 4456448 | tf_op jit(solution)/shard_map/all_gather | solution.py:92
  67.8 50.1 %all-to-all-start.1 = ((bf16[2,1,128,4096]{2,0,1,3:T(2,128)(2,1)}), bf16[2,1,128,4096]{2,0,1,3:T(2,128)(2,1)S(1)}, u32[]{:S(2)}, u32[]{:S(2)}) async-start(bf16[2,1,128,4096]{2,0,1,3:T(2,128)(2,1)} %copy.176), calls=%async_computation.1 | async-start | bytes 4194304 | tf_op jit(solution)/shard_map/all_to_all | solution.py:101
  117.9 61.3 %all-to-all-start = ((bf16[4,1,128,4096]{2,0,1,3:T(4,128)(2,1)}), bf16[4,1,128,4096]{2,0,1,3:T(4,128)(2,1)}, u32[]{:S(2)}, u32[]{:S(2)}) async-start(bf16[4,1,128,4096]{2,0,1,3:T(4,128)(2,1)} %copy.172), calls=%async_computation | async-start | bytes 8388608 | tf_op jit(solution)/shard_map/all_to_all | solution.py:100
  122.4 547.4 %reduce-scatter.5.cloned.1.call-start = ((), (), s32[]{:S(2)}) async-start(), calls=%async_computation.9 | async-start | bytes 9437184 | tf_op jit(solution)/shard_map/reduce_scatter | solution.py:124
  213.9 1.0 copy-start.4
  213.9 1.3 copy-start.6
  231.6 3.1 copy-start.2
  231.6 3.1 copy-start.3
  231.6 4.4 copy-start.5
  231.6 4.4 copy-start.7
  236.0 1.3 copy-start.6
  253.8 3.2 copy-start.2
  253.8 3.2 copy-start.3
  253.8 4.5 copy-start.5
  253.8 4.5 copy-start.7
  258.3 1.3 copy-start.6
  276.1 3.2 copy-start.2
  276.1 3.2 copy-start.3
  276.1 4.5 copy-start.5
  276.1 4.5 copy-start.7
  280.6 1.3 copy-start.6
  298.3 3.2 copy-start.2
  298.3 3.2 copy-start.3
  298.3 4.5 copy-start.5
  298.3 4.5 copy-start.7
  539.5 20.6 %copy-start.8 = (bf16[4,512,2,128]{3,2,1,0:T(2,128)(2,1)S(1)}, bf16[4,512,2,128]{3,2,1,0:T(2,128)(2,1)}, u32[]{:S(2)}) copy-start(bf16[4,512,2,128]{3,2,1,0:T(2,128)(2,1)} %get-tuple-element.143) | copy-start | bytes 3145732
  553.7 35.0 %all-to-all-start.3 = ((bf16[2,1,2048,256]{3,0,1,2:T(2,128)(2,1)}), bf16[2,1,2048,256]{3,0,1,2:T(2,128)(2,1)S(1)}, u32[]{:S(2)}, u32[]{:S(2)}) async-start(bf16[2,1,2048,256]{3,0,1,2:T(2,128)(2,1)} %copy.193), calls=%async_computation.4 | async-start | bytes 4194304 | tf_op jit(solution)/shard_map/all_to_all | solution.py:120
  588.7 63.7 %all-to-all-start.4 = ((bf16[4,1,2048,256]{3,0,1,2:T(4,128)(2,1)}), bf16[4,1,2048,256]{3,0,1,2:T(4,128)(2,1)}, u32[]{:S(2)}, u32[]{:S(2)}) async-start(bf16[4,1,2048,256]{3,0,1,2:T(4,128)(2,1)} %copy.201), calls=%async_computation.5 | async-start | bytes 8388608 | tf_op jit(solution)/shard_map/all_to_all | solution.py:121
  663.4 9.2 %copy-start.1 = (bf16[4,32,1024]{2,1,0:T(8,128)(2,1)S(1)}, bf16[4,32,1024]{2,1,0:T(8,128)(2,1)}, u32[]{:S(2)}) copy-start(bf16[4,32,1024]{2,1,0:T(8,128)(2,1)} %param.12) | copy-start | bytes 786436
  (4 other events, 3.9 us)
Sparse Core Ops, SparseCore 0:
  14.2 32.2 reduce-scatter.2
  64.2 61.8 all-gather.1
  313.0 118.7 reduce-scatter.4
where the time goes:
time: 692 us; the launch traced here: 679 us
  matrix products  302 us (44%)
  waiting for transfers between devices  167 us (24%)
  local copies, waits for them, and re-layouts  141 us (20%)
  starting transfers between devices  26.6 us (4%)
  blocking collectives  14.4 us (2%)
  between operations  14.3 us (2%)
  other arithmetic  13.1 us (2%)
    dot_general x8, matrix products, step(): jnp.einsum('hqk,qhd->khd', grad_scores, query_block, preferred_element_ty...  80.8 us
    dot_general x8, matrix products, step(): jnp.einsum('hqk,khd->qhd', grad_scores, keys, preferred_element_type=jnp....  69.3 us
    all_to_all x1, waiting for transfers between devices, body(): lax.all_to_all(grads, 'seq', split_axis=2, concat_axis=3, tiled=True)  53.2 us
    all_to_all x1, waiting for transfers between devices, body(): lax.all_to_all(streams, 'seq', split_axis=3, concat_axis=2, tiled=True)  48.6 us
    sub x8, matrix products, step(): weights = jnp.exp(scores - top)  41.4 us
    dot_general x8, matrix products, step(): jnp.einsum('hqk,qhd->khd', rounded, cot_block, preferred_element_type=jnp...  37.3 us
    all_to_all x1, waiting for transfers between devices, body(): lax.all_to_all(cotangents, 'seq', split_axis=3, concat_axis=2, tiled=True)  33.5 us
    unnamed x20, local copies, waits for them, and re-layouts  31.6 us
  transfers between devices with their start and end apart: 7, of which 4 were waited for; matrix products, arithmetic and copies ran while one was open for 49% of the time, Pallas kernels for 0%

commit v1 on v0

v1 whole, which is shorter than its diff:
```python
import functools
import math

import jax
import jax.numpy as jnp
from jax import lax
from jax.experimental import pallas as pl
from jax.experimental.pallas import tpu as pltpu
from jax.sharding import PartitionSpec as P

D_TEXT = 4096
HD = 128
SCALE = 1.0 / math.sqrt(HD)
LOG2E = math.log2(math.e)
VMEM = 56 * 2**20

NT = (((1,), (1,)), ((), ()))
NN = (((1,), (0,)), ((), ()))
TN = (((0,), (0,)), ((), ()))


def mm(a, b, dims):
    return lax.dot_general(a, b, dims, preferred_element_type=jnp.float32)


def attend_rows(queries, keys, values, cot, valid):
    scores = mm(queries, keys, NT)
    if valid is not None:
        scores = jnp.where(valid, scores, -1e30)
    top = jnp.max(scores, axis=1, keepdims=True)
    weights = jnp.exp2((scores - top) * (SCALE * LOG2E))
    inverse = 1.0 / jnp.sum(weights, axis=1, keepdims=True)
    rounded = weights.astype(jnp.bfloat16)
    context = mm(rounded, values, NN) * inverse
    products = weights * mm(cot, values, NT)
    centre = jnp.sum(products, axis=1, keepdims=True) * inverse
    grad_scores = (products - weights * centre).astype(jnp.bfloat16)
    grad_query = mm(grad_scores, keys, NN) * (inverse * SCALE)
    cot_scaled = (cot.astype(jnp.float32) * inverse).astype(jnp.bfloat16)
    query_scaled = (queries.astype(jnp.float32) * (inverse * SCALE)).astype(jnp.bfloat16)
    return (
        context,
        grad_query,
        mm(query_scaled, grad_scores, TN),
        mm(cot_scaled, rounded, TN),
    )


def self_kernel(q_ref, k_ref, v_ref, g_ref, y_ref, dk_acc, dv_acc, *, steps, per):
    step = pl.program_id(0)
    total = k_ref.shape[0] * k_ref.shape[2]

    @pl.when(step == 0)
    def _():
        dk_acc[...] = jnp.zeros_like(dk_acc)
        dv_acc[...] = jnp.zeros_like(dv_acc)

    rows = per * k_ref.shape[2]
    for head in range(k_ref.shape[3] // HD):
        cols = slice(head * HD, (head + 1) * HD)
        context, grad_query, dk, dv = attend_rows(
            q_ref[:, 0, :, cols].reshape(rows, HD),
            k_ref[:, 0, :, cols].reshape(total, HD),
            v_ref[:, 0, :, cols].reshape(total, HD),
            g_ref[:, 0, :, cols].reshape(rows, HD),
            None,
        )
        at = pl.ds(step * per, per)
        y_ref[at, 0, :, cols] = context.astype(jnp.bfloat16).reshape(per, -1, HD)
        y_ref[at, 1, :, cols] = grad_query.astype(jnp.bfloat16).reshape(per, -1, HD)
        dk_acc[head] += dk
        dv_acc[head] += dv

    @pl.when(step == steps - 1)
    def _():
        for head in range(k_ref.shape[3] // HD):
            cols = slice(head * HD, (head + 1) * HD)
            shape = (k_ref.shape[0], k_ref.shape[2], HD)
            y_ref[:, 2, :, cols] = dk_acc[head].T.astype(jnp.bfloat16).reshape(shape)
            y_ref[:, 3, :, cols] = dv_acc[head].T.astype(jnp.bfloat16).reshape(shape)


def self_attention(x):
    blocks, _, tokens, width = x.shape
    per = max(1, 512 // tokens)
    steps = blocks // per
    heads = width // HD
    total = blocks * tokens

    def rows(which):
        return pl.BlockSpec((per, 1, tokens, width), lambda i: (i, which, 0, 0))

    def whole(which):
        return pl.BlockSpec((blocks, 1, tokens, width), lambda i: (0, which, 0, 0))

    return pl.pallas_call(
        functools.partial(self_kernel, steps=steps, per=per),
        grid=(steps,),
        in_specs=[rows(0), whole(1), whole(2), rows(3)],
        out_specs=pl.BlockSpec((blocks, 4, tokens, width), lambda i: (0, 0, 0, 0)),
        out_shape=jax.ShapeDtypeStruct(x.shape, jnp.bfloat16),
        scratch_shapes=[pltpu.VMEM((heads, HD, total), jnp.float32)] * 2,
        compiler_params=pltpu.CompilerParams(vmem_limit_bytes=VMEM),
        cost_estimate=pl.CostEstimate(
            flops=24 * heads * total * total * HD,
            bytes_accessed=4 * x.size,
            transcendentals=heads * total * total,
        ),
        name="self_attention",
    )(x, x, x, x)


def cross_kernel(len_ref, q_ref, g_ref, k_ref, v_ref, y_ref, d_ref, dk_acc, dv_acc, *, steps, per):
    step = pl.program_id(0)
    total = k_ref.shape[0]

    @pl.when(step == 0)
    def _():
        dk_acc[...] = jnp.zeros_like(dk_acc)
        dv_acc[...] = jnp.zeros_like(dv_acc)

    rows = per * q_ref.shape[2]
    heads = q_ref.shape[3] // HD
    valid = lax.broadcasted_iota(jnp.int32, (rows, total), 1) < len_ref[0]
    for head in range(heads):
        cols = slice(head * HD, (head + 1) * HD)
        context, grad_query, dk, dv = attend_rows(
            q_ref[:, 0, :, cols].reshape(rows, HD),
            k_ref[:, cols],
            v_ref[:, cols],
            g_ref[:, 0, :, cols].reshape(rows, HD),
            valid,
        )
        y_ref[:, 0, :, cols] = context.astype(jnp.bfloat16).reshape(per, -1, HD)
        y_ref[:, 1, :, cols] = grad_query.astype(jnp.bfloat16).reshape(per, -1, HD)
        dk_acc[head] += dk
        dv_acc[head] += dv

    @pl.when(step == steps - 1)
    def _():
        for head in range(heads):
            cols = slice(head * HD, (head + 1) * HD)
            d_ref[:, cols] = dk_acc[head].T.astype(jnp.bfloat16)
            cols = slice((heads + head) * HD, (heads + head + 1) * HD)
            d_ref[:, cols] = dv_acc[head].T.astype(jnp.bfloat16)


def cross_attention(lengths, x, kv):
    blocks, _, tokens, width = x.shape
    captions = kv.shape[0]
    per = max(1, 512 // tokens)
    steps = blocks // per
    heads = width // HD
    total = blocks * tokens

    def rows(which):
        return pl.BlockSpec((per, 1, tokens, width), lambda i: (i, which, 0, 0))

    return pl.pallas_call(
        functools.partial(cross_kernel, steps=steps, per=per),
        grid=(steps,),
        in_specs=[
            pl.BlockSpec(memory_space=pltpu.SMEM),
            rows(0),
            rows(1),
            pl.BlockSpec((captions, width), lambda i: (0, 0)),
            pl.BlockSpec((captions, width), lambda i: (0, 1)),
        ],
        out_specs=[
            pl.BlockSpec((per, 2, tokens, width), lambda i: (i, 0, 0, 0)),
            pl.BlockSpec((captions, 2 * width), lambda i: (0, 0)),
        ],
        out_shape=[
            jax.ShapeDtypeStruct(x.shape, jnp.bfloat16),
            jax.ShapeDtypeStruct(kv.shape, jnp.bfloat16),
        ],
        scratch_shapes=[pltpu.VMEM((heads, HD, captions), jnp.float32)] * 2,
        compiler_params=pltpu.CompilerParams(vmem_limit_bytes=VMEM),
        cost_estimate=pl.CostEstimate(
            flops=24 * heads * total * captions * HD,
            bytes_accessed=4 * x.size + 4 * kv.size,
            transcendentals=heads * total * captions,
        ),
        name="cross_attention",
    )(lengths, x, x, kv, kv)


def pack_kernel(s_ref, c_ref, x_ref):
    count = s_ref.shape[0]
    x_ref[0, :count] = s_ref[:, 0]
    x_ref[0, count:] = c_ref[:, 0]


def pack(streams, cotangents, first, count, cot, parts):
    tokens, width = streams.shape[2], streams.shape[3] // parts
    return pl.pallas_call(
        pack_kernel,
        grid=(parts,),
        in_specs=[
            pl.BlockSpec((count, 1, tokens, width), lambda j: (first // count, 0, 0, j)),
            pl.BlockSpec((1, 1, tokens, width), lambda j: (cot, 0, 0, j)),
        ],
        out_specs=pl.BlockSpec((1, count + 1, tokens, width), lambda j: (j, 0, 0, 0)),
        out_shape=jax.ShapeDtypeStruct((parts, count + 1, tokens, width), jnp.bfloat16),
        cost_estimate=pl.CostEstimate(
            flops=0, bytes_accessed=4 * (count + 1) * tokens * width * parts, transcendentals=0
        ),
        name="pack",
    )(streams, cotangents)


def unpack_kernel(a_ref, b_ref, self_ref, cross_ref, grads_ref):
    self_ref[...] = a_ref[0, 0:1]
    cross_ref[...] = b_ref[0, 0:1]
    grads_ref[0:3, 0] = a_ref[0, 1:4]
    grads_ref[3:4, 0] = b_ref[0, 1:2]


def unpack(a, b):
    parts, _, tokens, width = a.shape
    return pl.pallas_call(
        unpack_kernel,
        grid=(parts,),
        in_specs=[
            pl.BlockSpec((1, 4, tokens, width), lambda j: (j, 0, 0, 0)),
            pl.BlockSpec((1, 2, tokens, width), lambda j: (j, 0, 0, 0)),
        ],
        out_specs=[
            pl.BlockSpec((1, tokens, width), lambda j: (0, 0, j)),
            pl.BlockSpec((1, tokens, width), lambda j: (0, 0, j)),
            pl.BlockSpec((4, 1, tokens, width), lambda j: (0, 0, 0, j)),
        ],
        out_shape=[
            jax.ShapeDtypeStruct((1, tokens, parts * width), jnp.bfloat16),
            jax.ShapeDtypeStruct((1, tokens, parts * width), jnp.bfloat16),
            jax.ShapeDtypeStruct((4, 1, tokens, parts * width), jnp.bfloat16),
        ],
        cost_estimate=pl.CostEstimate(
            flops=0, bytes_accessed=4 * (a.size + b.size), transcendentals=0
        ),
        name="unpack",
    )(a, b)


def project_kernel(own_ref, x_ref, w_ref, r_ref, y_ref, *, per):
    y = mm(x_ref[...], w_ref[...], NN)
    mine = (pl.program_id(0) // per) == own_ref[0]
    y_ref[...] = y + jnp.where(mine, r_ref[...].astype(jnp.float32), 0.0)


def project(context, weight, residual):
    rows, depth = context.shape
    block = 512
    per = depth // block
    own = lax.axis_index("tp").astype(jnp.int32).reshape(1)
    return pl.pallas_call(
        functools.partial(project_kernel, per=per),
        grid=(weight.shape[1] // block,),
        in_specs=[
            pl.BlockSpec(memory_space=pltpu.SMEM),
            pl.BlockSpec((rows, depth), lambda j: (0, 0)),
            pl.BlockSpec((depth, block), lambda j: (0, j)),
            pl.BlockSpec((rows, block), lambda j: (0, lax.rem(j, per))),
        ],
        out_specs=pl.BlockSpec((rows, block), lambda j: (0, j)),
        out_shape=jax.ShapeDtypeStruct((rows, weight.shape[1]), jnp.float32),
        cost_estimate=pl.CostEstimate(
            flops=2 * rows * depth * weight.shape[1],
            bytes_accessed=2 * weight.size,
            transcendentals=0,
        ),
        name="project",
    )(own, context, weight, residual)


def body(
    enc_context,
    enc_residual,
    out_weight,
    norm_gain,
    kv_weight,
    caption_lengths,
    streams,
    cotangents,
):
    owned, caption_rows, feature_part = enc_context.shape
    parts = lax.axis_size("seq")
    local_width = kv_weight.shape[2]

    cross_in = lax.all_to_all(
        pack(streams, cotangents, 3, 1, 1, parts), "seq", split_axis=0, concat_axis=0, tiled=True
    )
    self_in = lax.all_to_all(
        pack(streams, cotangents, 0, 3, 0, parts), "seq", split_axis=0, concat_axis=0, tiled=True
    )

    partial_value = project(
        enc_context.reshape(owned * caption_rows, feature_part),
        out_weight,
        enc_residual.reshape(owned * caption_rows, feature_part),
    )
    hidden = lax.psum_scatter(partial_value, "tp", scatter_dimension=0, tiled=True)
    power = jnp.mean(hidden * hidden, axis=1, keepdims=True)
    mine = (hidden * lax.rsqrt(power + 1e-06) * norm_gain).astype(jnp.bfloat16)
    states = lax.all_gather(mine, "seq", axis=0, tiled=True)
    caption_kv = jnp.dot(
        states, kv_weight.reshape(D_TEXT, 2 * local_width), preferred_element_type=jnp.float32
    ).astype(jnp.bfloat16)

    cross_out, caption_grads = cross_attention(caption_lengths, cross_in, caption_kv)
    cross_back = lax.all_to_all(cross_out, "seq", split_axis=0, concat_axis=0, tiled=True)
    product = lax.dot_general(states, caption_grads, TN, preferred_element_type=jnp.float32)
    grad = lax.psum_scatter(
        product.astype(jnp.bfloat16), ("dp", "tp"), scatter_dimension=0, tiled=True
    )
    weight_grad = grad.astype(jnp.float32).reshape(grad.shape[0], 2, local_width)

    self_out = self_attention(self_in)
    self_back = lax.all_to_all(self_out, "seq", split_axis=0, concat_axis=0, tiled=True)
    self_ctx, cross_ctx, stream_grads = unpack(self_back, cross_back)
    return (self_ctx, cross_ctx, stream_grads, weight_grad)


def solution(mesh):
    placed = (
        P("dp", "seq", "tp"),
        P("dp", "seq", "tp"),
        P("tp", None),
        P(),
        P(None, None, "seq"),
        P(("dp", "tp")),
        P(None, ("dp", "tp"), "seq", None),
        P(None, ("dp", "tp"), "seq", None),
    )
    return jax.shard_map(
        body,
        mesh=mesh,
        in_specs=placed,
        out_specs=(
            P(("dp", "tp"), "seq", None),
            P(("dp", "tp"), "seq", None),
            P(None, ("dp", "tp"), "seq", None),
            P(("dp", "tp"), None, "seq"),
        ),
        check_vma=False,
    )
```

time: 692 us -> 315 us (0.46); the launches traced: 679 us -> 312 us
  matrix products: 302 us -> 12 us
  local copies, waits for them, and re-layouts: 141 us -> 7.56 us
  Pallas kernels: 0 us -> 83 us
  waiting for transfers between devices: 167 us -> 89.6 us
  blocking collectives: 14.4 us -> 91.5 us
  starting transfers between devices: 26.6 us -> 10.6 us
  other arithmetic: 13.1 us -> 3.05 us
    dot_general x42 -> x1, matrix products: 255 us -> 5.38 us  [body(): lax.dot_general(states, caption_grads, TN, preferred_element_type=jnp.flo...]
    all_to_all x1 -> x2, blocking collectives: 7.92 us -> 91.5 us  [the longest x1 59.1 us: body(): lax.all_to_all(self_out, 'seq', split_axis=0, concat_axis=0, tiled=True)]
    pallas_call x0 -> x6, Pallas kernels: none -> 83 us  [the longest x1 33.9 us: self_attention(): pl.pallas_call(functools.partial(self_kernel, steps=steps, per=per), grid...]
    all_to_all x4 -> x2, waiting for transfers between devices: 135 us -> 57.2 us  [the longest x1 29.1 us: body(): lax.all_to_all(pack(streams, cotangents, 3, 1, 1, parts), 'seq', split_ax...]
    sub x8 -> x0, matrix products: 41.4 us -> none  [step(): weights = jnp.exp(scores - top)]
    broadcast_in_dim x2 -> x0, local copies, waits for them, and re-layouts: 31.3 us -> none  [the longest x1 17.1 us: body(): grads = jnp.stack([self_dq, self_dk, self_dv, cross_dq])[:, None]]
    unnamed x20 -> x9, local copies, waits for them, and re-layouts: 31.6 us -> 4.9 us
    another operation x16 -> x0, local copies, waits for them, and re-layouts: 21.1 us -> none  [the longest x4 5.84 us: body(): grads = jnp.stack([self_dq, self_dk, self_dv, cross_dq])[:, None]]
  transfers between devices with their start and end apart: 7 -> 5, of which waited for: 4 -> 3; matrix products, arithmetic and copies ran while one was open for 49% -> 5% of each run, Pallas kernels for 0% -> 24%
where the time goes in v1:
time: 315 us; the launch traced here: 312 us
  blocking collectives  91.5 us (29%)
  waiting for transfers between devices  89.6 us (28%)
  Pallas kernels  83 us (26%)
  between operations  14.4 us (5%)
  matrix products  12 us (4%)
  starting transfers between devices  10.6 us (3%)
  local copies, waits for them, and re-layouts  7.56 us (2%)
    all_to_all x1, blocking collectives, body(): lax.all_to_all(self_out, 'seq', split_axis=0, concat_axis=0, tiled=True)  59.1 us
    pallas_call x1, Pallas kernels, self_attention(): pl.pallas_call(functools.partial(self_kernel, steps=steps, per=per), grid...  33.9 us
    all_to_all x1, blocking collectives, body(): lax.all_to_all(cross_out, 'seq', split_axis=0, concat_axis=0, tiled=True)  32.4 us
    reduce_scatter x1, waiting for transfers between devices, body(): lax.psum_scatter(partial_value, 'tp', scatter_dimension=0, tiled=True)  32.3 us
    all_to_all x1, waiting for transfers between devices, body(): lax.all_to_all(pack(streams, cotangents, 3, 1, 1, parts), 'seq', split_ax...  29.1 us
    all_to_all x1, waiting for transfers between devices, body(): lax.all_to_all(pack(streams, cotangents, 0, 3, 0, parts), 'seq', split_ax...  28.1 us
    pallas_call x2, Pallas kernels, pack(): pl.pallas_call(pack_kernel, grid=(parts,), in_specs=[pl.BlockSpec((count,...  19.4 us
    pallas_call x1, Pallas kernels, unpack(): pl.pallas_call(unpack_kernel, grid=(parts,), in_specs=[pl.BlockSpec((1, 4...  10.8 us
  transfers between devices with their start and end apart: 5, of which 3 were waited for; matrix products, arithmetic and copies ran while one was open for 5% of the time, Pallas kernels for 24%

profile of v1, /device:TPU:9, one launch (start us, length us, event | category | flops | bytes accessed | tf_op | source)
XLA Modules:
  0.0 311.7 jit_solution(18090117320927946820)
XLA Ops:
  7.2 0.0 reduce-scatter.3.cloned.1.call-start
  7.2 0.0 copy-start.2
  7.2 8.2 %project.1 = f32[128,4096]{1,0:T(8,128)} custom-call(s32[1]{0:T(128)} %bitcast.own_ref, bf16[128,1024]{1,0:T(8,128)(2,1)} %bitcast.11, bf16[1024,4096]{1,0:T(8,128)(2,1)} %w_ref.1, bf16[128,1024]{1,0:T(8,128)(2,1)} %bitcast.12), custom_call_target="tpu_custom_call" | custom-call | flops 1073741824 | bytes 8388608 | tf_op jit(solution)/shard_map/project/pallas_call | solution.py:256
  15.4 0.0 reduce-scatter.3.cloned.1.call-update
  15.4 0.0 all-gather.2.cloned.1.call-start
  15.5 32.3 %reduce-scatter.3.cloned.1.call-done = f32[32,4096]{1,0:T(8,128)} async-done(((f32[128,4096]{1,0:T(8,128)}), f32[32,4096]{1,0:T(8,128)}) %reduce-scatter.3.cloned.1.call-update) | async-done | bytes 524304 | tf_op jit(solution)/shard_map/reduce_scatter | solution.py:302
  47.8 1.2 multiply_reduce_fusion
  49.0 0.0 copy-done.2
  49.0 1.9 multiply_convert_fusion
  50.9 0.0 all-gather.2.cloned.1.call-update
  50.9 9.3 %pack.3 = bf16[16,2,128,256]{3,2,1,0:T(8,128)(2,1)} custom-call(bf16[4,1,128,4096]{3,2,1,0:T(8,128)(2,1)} %s_ref.3, bf16[2,1,128,4096]{3,2,1,0:T(8,128)(2,1)} %c_ref.3), custom_call_target="tpu_custom_call" | custom-call | bytes 4194304 | tf_op jit(solution)/shard_map/pack/pallas_call | solution.py:196
  60.2 6.0 %all-to-all-start.2 = ((bf16[16,2,128,256]{3,2,1,0:T(8,128)(2,1)}), bf16[16,2,128,256]{3,2,1,0:T(8,128)(2,1)S(1)}, u32[]{:S(2)}, u32[]{:S(2)}) async-start(bf16[16,2,128,256]{3,2,1,0:T(8,128)(2,1)} %pack.3), calls=%async_computation.2 | async-start | bytes 4194304 | tf_op jit(solution)/shard_map/all_to_all | solution.py:290
  66.2 10.1 %pack.2 = bf16[16,4,128,256]{3,2,1,0:T(8,128)(2,1)} custom-call(bf16[4,1,128,4096]{3,2,1,0:T(8,128)(2,1)} %s_ref.3, bf16[2,1,128,4096]{3,2,1,0:T(8,128)(2,1)} %c_ref.3), custom_call_target="tpu_custom_call" | custom-call | bytes 8388608 | tf_op jit(solution)/shard_map/pack/pallas_call | solution.py:196
  76.4 29.1 %all-to-all-done.2.q_ref.g_ref = bf16[16,2,128,256]{3,2,1,0:T(8,128)(2,1)S(1)} async-done(((bf16[16,2,128,256]{3,2,1,0:T(8,128)(2,1)}), bf16[16,2,128,256]{3,2,1,0:T(8,128)(2,1)S(1)}, u32[]{:S(2)}, u32[]{:S(2)}) %all-to-all-start.2) | async-done | bytes 2097184 | tf_op jit(solution)/shard_map/all_to_all | solution.py:290
  105.5 0.0 copy-start
  105.5 4.5 %all-to-all-start = ((bf16[16,4,128,256]{3,2,1,0:T(8,128)(2,1)}), bf16[16,4,128,256]{3,2,1,0:T(8,128)(2,1)}, u32[]{:S(2)}, u32[]{:S(2)}) async-start(bf16[16,4,128,256]{3,2,1,0:T(8,128)(2,1)} %pack.2), calls=%async_computation | async-start | bytes 8388608 | tf_op jit(solution)/shard_map/all_to_all | solution.py:293
  109.9 0.0 reduce-scatter.5.cloned.1.call-start
  110.6 0.0 copy-done
  110.6 4.9 %copy.12 = bf16[512,8,2,256]{3,1,2,0:T(8,128)(2,1)} copy(bf16[512,8,2,256]{3,2,1,0:T(2,128)(2,1)} %bitcast.9) | data formatting | bytes 8388608
  115.5 0.0 all-gather.2.cloned.1.call-done
  115.5 6.6 %convolution_convert_fusion.1.k_ref.v_ref = bf16[512,512]{1,0:T(8,128)(2,1)} fusion(bf16[512,4096]{1,0:T(8,128)(2,1)} %all-gather.2.cloned.1.call-done, bf16[4096,512]{1,0:T(8,128)(2,1)} %bitcast.10), kind=kOutput, calls=%fused_computation.1 | convolution fusion | flops 2147745792 | bytes 8912896 | tf_op jit(solution)/shard_map/dot_general | solution.py:306
  122.1 10.7 %cross_attention.1 = (bf16[16,2,128,256]{3,2,1,0:T(8,128)(2,1)}, bf16[512,512]{1,0:T(8,128)(2,1)}) custom-call(s32[1]{0:T(128)S(6)} %copy.13.len_ref, bf16[16,2,128,256]{3,2,1,0:T(8,128)(2,1)} %copy-done, bf16[16,2,128,256]{3,2,1,0:T(8,128)(2,1)} %copy-done, bf16[512,512]{1,0:T(8,128)(2,1)} %convolution_convert_fusion.1.k_ref.v_ref, ...), custom_call_target="tpu_custom_call" | custom-call | flops 6442450944 | bytes 5242880 | tf_op jit(solution)/shard_map/cross_attention/pallas_call | solution.py:159
  132.9 0.0 copy-done.3
  132.9 5.4 %convolution_convert_fusion = bf16[4096,512]{1,0:T(8,128)(2,1)} fusion(bf16[512,4096]{1,0:T(8,128)(2,1)S(1)} %copy-done.3, bf16[512,512]{1,0:T(8,128)(2,1)} %get-tuple-element.13), kind=kOutput, calls=%fused_computation | convolution fusion | flops 2149580800 | bytes 8912896 | tf_op jit(solution)/shard_map/dot_general | solution.py:312
  138.2 0.0 reduce-scatter.5.cloned.1.call-update
  138.3 28.1 %all-to-all-done.q_ref.k_ref.v_ref.g_ref = bf16[16,4,128,256]{3,2,1,0:T(8,128)(2,1)} async-done(((bf16[16,4,128,256]{3,2,1,0:T(8,128)(2,1)}), bf16[16,4,128,256]{3,2,1,0:T(8,128)(2,1)}, u32[]{:S(2)}, u32[]{:S(2)}) %all-to-all-start) | async-done | bytes 4194336 | tf_op jit(solution)/shard_map/all_to_all | solution.py:293
  166.4 33.9 %self_attention.1 = bf16[16,4,128,256]{3,2,1,0:T(8,128)(2,1)} custom-call(bf16[16,4,128,256]{3,2,1,0:T(8,128)(2,1)} %all-to-all-done.q_ref.k_ref.v_ref.g_ref, bf16[16,4,128,256]{3,2,1,0:T(8,128)(2,1)} %all-to-all-done.q_ref.k_ref.v_ref.g_ref, bf16[16,4,128,256]{3,2,1,0:T(8,128)(2,1)} %all-to-all-done.q_ref.k_ref.v_ref.g_ref, ...), custom_call_target="tpu_custom_call" | custom-call | flops 25769803776 | bytes 8388608 | tf_op jit(solution)/shard_map/self_attention/pallas_call | solution.py:96
  200.2 59.1 %all_to_all.20.a_ref = bf16[16,4,128,256]{3,2,1,0:T(8,128)(2,1)} all-to-all(bf16[16,4,128,256]{3,2,1,0:T(8,128)(2,1)} %self_attention.1), channel_id=1, replica_groups=mesh['dp'=2,'seq'=16,'tp'=4] {'seq'}, dimensions={0} | all-to-all | bytes 8388608 | tf_op jit(solution)/shard_map/all_to_all | solution.py:319
  259.3 0.0 copy-done.1
  259.3 32.4 %all_to_all.21.b_ref = bf16[16,2,128,256]{3,2,1,0:T(8,128)(2,1)} all-to-all(bf16[16,2,128,256]{3,2,1,0:T(8,128)(2,1)S(1)} %copy-done.1), channel_id=1, replica_groups=mesh['dp'=2,'seq'=16,'tp'=4] {'seq'}, dimensions={0} | all-to-all | bytes 4194304 | tf_op jit(solution)/shard_map/all_to_all | solution.py:311
  291.7 10.8 %unpack.1 = (bf16[1,128,4096]{2,1,0:T(8,128)(2,1)}, bf16[1,128,4096]{2,1,0:T(8,128)(2,1)}, bf16[4,1,128,4096]{3,2,1,0:T(8,128)(2,1)}) custom-call(bf16[16,4,128,256]{3,2,1,0:T(8,128)(2,1)} %all_to_all.20.a_ref, bf16[16,2,128,256]{3,2,1,0:T(8,128)(2,1)} %all_to_all.21.b_ref), custom_call_target="tpu_custom_call" | custom-call | bytes 12582912 | tf_op jit(solution)/shard_map/unpack/pallas_call | solution.py:221
  302.5 2.7 reshape.42
  (4 shorter events, 0.0 us)
Async XLA Ops:
  7.2 40.7 %reduce-scatter.3.cloned.1.call-start = ((), (), s32[]{:S(2)}) async-start(), calls=%async_computation.6 | async-start | bytes 2621440 | tf_op jit(solution)/shard_map/reduce_scatter | solution.py:302
  7.2 41.8 %copy-start.2 = (f32[4096]{0:T(1024)S(1)}, f32[4096]{0:T(1024)}, u32[]{:S(2)}) copy-start(f32[4096]{0:T(1024)} %param.11) | copy-start | bytes 49156
  15.4 100.1 %all-gather.2.cloned.1.call-start = ((), (), s32[]{:S(2)}) async-start(), calls=%async_computation.7 | async-start | bytes 4456448 | tf_op jit(solution)/shard_map/all_gather | solution.py:305
  60.2 45.3 %all-to-all-start.2 = ((bf16[16,2,128,256]{3,2,1,0:T(8,128)(2,1)}), bf16[16,2,128,256]{3,2,1,0:T(8,128)(2,1)S(1)}, u32[]{:S(2)}, u32[]{:S(2)}) async-start(bf16[16,2,128,256]{3,2,1,0:T(8,128)(2,1)} %pack.3), calls=%async_computation.2 | async-start | bytes 4194304 | tf_op jit(solution)/shard_map/all_to_all | solution.py:290
  105.5 5.2 %copy-start = (bf16[16,2,128,256]{3,2,1,0:T(8,128)(2,1)}, bf16[16,2,128,256]{3,2,1,0:T(8,128)(2,1)S(1)}, u32[]{:S(2)}) copy-start(bf16[16,2,128,256]{3,2,1,0:T(8,128)(2,1)S(1)} %all-to-all-done.2.q_ref.g_ref) | copy-start | bytes 6291460
  105.5 60.9 %all-to-all-start = ((bf16[16,4,128,256]{3,2,1,0:T(8,128)(2,1)}), bf16[16,4,128,256]{3,2,1,0:T(8,128)(2,1)}, u32[]{:S(2)}, u32[]{:S(2)}) async-start(bf16[16,4,128,256]{3,2,1,0:T(8,128)(2,1)} %pack.2), calls=%async_computation | async-start | bytes 8388608 | tf_op jit(solution)/shard_map/all_to_all | solution.py:293
  109.9 192.6 %reduce-scatter.5.cloned.1.call-start = ((), (), s32[]{:S(2)}) async-start(), calls=%async_computation.8 | async-start | bytes 4718592 | tf_op jit(solution)/shard_map/reduce_scatter | solution.py:313
  122.1 10.7 %copy-start.3 = (bf16[512,4096]{1,0:T(8,128)(2,1)S(1)}, bf16[512,4096]{1,0:T(8,128)(2,1)}, u32[]{:S(2)}) copy-start(bf16[512,4096]{1,0:T(8,128)(2,1)} %all-gather.2.cloned.1.call-done) | copy-start | bytes 12582916
  200.2 59.1 %copy-start.1 = (bf16[16,2,128,256]{3,2,1,0:T(8,128)(2,1)S(1)}, bf16[16,2,128,256]{3,2,1,0:T(8,128)(2,1)}, u32[]{:S(2)}) copy-start(bf16[16,2,128,256]{3,2,1,0:T(8,128)(2,1)} %get-tuple-element.9) | copy-start | bytes 6291460
Sparse Core Ops, SparseCore 0:
  15.6 32.2 reduce-scatter.2
  51.0 58.6 all-gather.1
  138.4 128.0 reduce-scatter.4

commit v2 on v1

v2 whole, which is shorter than its diff:
```python
import functools
import math

import jax
import jax.numpy as jnp
from jax import lax
from jax.experimental import pallas as pl
from jax.experimental.pallas import tpu as pltpu
from jax.sharding import PartitionSpec as P

D_TEXT = 4096
HD = 128
SCALE = 1.0 / math.sqrt(HD)
LOG2E = math.log2(math.e)
VMEM = 56 * 2**20
ADD_COST = 2 * 10**10

NT = (((1,), (1,)), ((), ()))
NN = (((1,), (0,)), ((), ()))
TN = (((0,), (0,)), ((), ()))


def mm(a, b, dims):
    return lax.dot_general(a, b, dims, preferred_element_type=jnp.float32)


def attend_rows(queries, keys, values, cot, valid):
    scores = mm(queries, keys, NT)
    if valid is not None:
        scores = jnp.where(valid, scores, -1e30)
    top = jnp.max(scores, axis=1, keepdims=True)
    weights = jnp.exp2((scores - top) * (SCALE * LOG2E))
    inverse = 1.0 / jnp.sum(weights, axis=1, keepdims=True)
    rounded = weights.astype(jnp.bfloat16)
    context = mm(rounded, values, NN) * inverse
    products = weights * mm(cot, values, NT)
    centre = jnp.sum(products, axis=1, keepdims=True) * inverse
    grad_scores = (products - weights * centre).astype(jnp.bfloat16)
    grad_query = mm(grad_scores, keys, NN) * (inverse * SCALE)
    cot_scaled = (cot.astype(jnp.float32) * inverse).astype(jnp.bfloat16)
    query_scaled = (queries.astype(jnp.float32) * (inverse * SCALE)).astype(jnp.bfloat16)
    return (
        context,
        grad_query,
        mm(query_scaled, grad_scores, TN),
        mm(cot_scaled, rounded, TN),
    )


def self_kernel(q_ref, k_ref, v_ref, g_ref, *rest, steps, per):
    y_ref, dk_acc, dv_acc = rest[-3:]
    step = pl.program_id(0)
    blocks, _, tokens, _ = k_ref.shape
    total, rows = blocks * tokens, per * tokens

    @pl.when(step == 0)
    def _():
        dk_acc[...] = jnp.zeros_like(dk_acc)
        dv_acc[...] = jnp.zeros_like(dv_acc)

    context, grad_query, dk, dv = attend_rows(
        q_ref[...].reshape(rows, HD),
        k_ref[...].reshape(total, HD),
        v_ref[...].reshape(total, HD),
        g_ref[...].reshape(rows, HD),
        None,
    )
    at = pl.ds(step * per, per)
    y_ref[at, 0] = context.astype(jnp.bfloat16).reshape(per, tokens, HD)
    y_ref[at, 1] = grad_query.astype(jnp.bfloat16).reshape(per, tokens, HD)
    dk_acc[...] += dk
    dv_acc[...] += dv

    @pl.when(step == steps - 1)
    def _():
        y_ref[:, 2] = dk_acc[...].T.astype(jnp.bfloat16).reshape(blocks, tokens, HD)
        y_ref[:, 3] = dv_acc[...].T.astype(jnp.bfloat16).reshape(blocks, tokens, HD)


def self_attention(x, head, before):
    blocks, _, tokens, _ = x.shape
    per = max(1, 512 // tokens)
    steps = blocks // per
    total = blocks * tokens

    def rows(which):
        return pl.BlockSpec((per, 1, tokens, HD), lambda i: (i, which, 0, head))

    def whole(which):
        return pl.BlockSpec((blocks, 1, tokens, HD), lambda i: (0, which, 0, head))

    earlier = [] if before is None else [before]
    return pl.pallas_call(
        functools.partial(self_kernel, steps=steps, per=per),
        grid=(steps,),
        in_specs=[rows(0), whole(1), whole(2), rows(3)]
        + [pl.BlockSpec(memory_space=pl.ANY)] * len(earlier),
        out_specs=pl.BlockSpec((blocks, 4, tokens, HD), lambda i: (0, 0, 0, head)),
        out_shape=jax.ShapeDtypeStruct(x.shape, jnp.bfloat16),
        scratch_shapes=[pltpu.VMEM((HD, total), jnp.float32)] * 2,
        input_output_aliases={4: 0} if earlier else {},
        compiler_params=pltpu.CompilerParams(vmem_limit_bytes=VMEM),
        cost_estimate=pl.CostEstimate(
            flops=24 * total * total * HD,
            bytes_accessed=16 * total * HD,
            transcendentals=total * total,
        ),
        name="self_attention",
    )(x, x, x, x, *earlier)


def cross_kernel(len_ref, pos_ref, q_ref, g_ref, k_ref, v_ref, y_ref, d_ref, dk_acc, dv_acc, *, steps, per):
    step = pl.program_id(0)
    total = k_ref.shape[0]

    @pl.when(step == 0)
    def _():
        dk_acc[...] = jnp.zeros_like(dk_acc)
        dv_acc[...] = jnp.zeros_like(dv_acc)

    rows = per * q_ref.shape[2]
    heads = q_ref.shape[3] // HD
    valid = jnp.broadcast_to(pos_ref[...], (rows, total)) < len_ref[0]
    for head in range(heads):
        cols = slice(head * HD, (head + 1) * HD)
        context, grad_query, dk, dv = attend_rows(
            q_ref[:, 0, :, cols].reshape(rows, HD),
            k_ref[:, cols],
            v_ref[:, cols],
            g_ref[:, 0, :, cols].reshape(rows, HD),
            valid,
        )
        y_ref[:, 0, :, cols] = context.astype(jnp.bfloat16).reshape(per, -1, HD)
        y_ref[:, 1, :, cols] = grad_query.astype(jnp.bfloat16).reshape(per, -1, HD)
        dk_acc[head] += dk
        dv_acc[head] += dv

    @pl.when(step == steps - 1)
    def _():
        for head in range(heads):
            cols = slice(head * HD, (head + 1) * HD)
            d_ref[:, cols] = dk_acc[head].T.astype(jnp.bfloat16)
            cols = slice((heads + head) * HD, (heads + head + 1) * HD)
            d_ref[:, cols] = dv_acc[head].T.astype(jnp.bfloat16)


def cross_attention(lengths, positions, x, kv):
    blocks, _, tokens, width = x.shape
    captions = kv.shape[0]
    per = max(1, 512 // tokens)
    steps = blocks // per
    heads = width // HD
    total = blocks * tokens

    def rows(which):
        return pl.BlockSpec((per, 1, tokens, width), lambda i: (i, which, 0, 0))

    return pl.pallas_call(
        functools.partial(cross_kernel, steps=steps, per=per),
        grid=(steps,),
        in_specs=[
            pl.BlockSpec(memory_space=pltpu.SMEM),
            pl.BlockSpec((1, captions), lambda i: (0, 0)),
            rows(0),
            rows(1),
            pl.BlockSpec((captions, width), lambda i: (0, 0)),
            pl.BlockSpec((captions, width), lambda i: (0, 1)),
        ],
        out_specs=[
            pl.BlockSpec((per, 2, tokens, width), lambda i: (i, 0, 0, 0)),
            pl.BlockSpec((captions, 2 * width), lambda i: (0, 0)),
        ],
        out_shape=[
            jax.ShapeDtypeStruct(x.shape, jnp.bfloat16),
            jax.ShapeDtypeStruct(kv.shape, jnp.bfloat16),
        ],
        scratch_shapes=[pltpu.VMEM((heads, HD, captions), jnp.float32)] * 2,
        compiler_params=pltpu.CompilerParams(vmem_limit_bytes=VMEM),
        cost_estimate=pl.CostEstimate(
            flops=24 * heads * total * captions * HD,
            bytes_accessed=4 * x.size + 4 * kv.size,
            transcendentals=heads * total * captions,
        ),
        name="cross_attention",
    )(lengths, positions.reshape(1, captions), x, x, kv, kv)


def pack_kernel(s_ref, c_ref, x_ref):
    count, width = s_ref.shape[0], x_ref.shape[3]
    for part in range(x_ref.shape[0]):
        cols = slice(part * width, (part + 1) * width)
        x_ref[part, :count] = s_ref[:, 0, :, cols]
        x_ref[part, count:] = c_ref[:, 0, :, cols]


def pack(streams, cotangents, first, count, cot, parts):
    tokens, width = streams.shape[2], streams.shape[3] // parts
    per = 4
    return pl.pallas_call(
        pack_kernel,
        grid=(parts // per,),
        in_specs=[
            pl.BlockSpec((count, 1, tokens, per * width), lambda j: (first // count, 0, 0, j)),
            pl.BlockSpec((1, 1, tokens, per * width), lambda j: (cot, 0, 0, j)),
        ],
        out_specs=pl.BlockSpec((per, count + 1, tokens, width), lambda j: (j, 0, 0, 0)),
        out_shape=jax.ShapeDtypeStruct((parts, count + 1, tokens, width), jnp.bfloat16),
        cost_estimate=pl.CostEstimate(
            flops=0, bytes_accessed=4 * (count + 1) * tokens * width * parts, transcendentals=0
        ),
        compiler_params=pltpu.CompilerParams(vmem_limit_bytes=VMEM),
        name="pack",
    )(streams, cotangents)


def unpack_self_kernel(x_ref, ctx_ref, grads_ref):
    width = x_ref.shape[3]
    for part in range(x_ref.shape[0]):
        cols = slice(part * width, (part + 1) * width)
        ctx_ref[0, :, cols] = x_ref[part, 0]
        grads_ref[:, 0, :, cols] = x_ref[part, 1:]


def unpack_self(x):
    parts, _, tokens, width = x.shape
    per = 4
    return pl.pallas_call(
        unpack_self_kernel,
        grid=(parts // per,),
        in_specs=[pl.BlockSpec((per, 4, tokens, width), lambda j: (j, 0, 0, 0))],
        out_specs=[
            pl.BlockSpec((1, tokens, per * width), lambda j: (0, 0, j)),
            pl.BlockSpec((3, 1, tokens, per * width), lambda j: (0, 0, 0, j)),
        ],
        out_shape=[
            jax.ShapeDtypeStruct((1, tokens, parts * width), jnp.bfloat16),
            jax.ShapeDtypeStruct((4, 1, tokens, parts * width), jnp.bfloat16),
        ],
        cost_estimate=pl.CostEstimate(flops=0, bytes_accessed=4 * x.size, transcendentals=0),
        compiler_params=pltpu.CompilerParams(vmem_limit_bytes=VMEM),
        name="unpack_self",
    )(x)


def unpack_cross_kernel(x_ref, _, ctx_ref, grads_ref):
    width = x_ref.shape[3]
    for part in range(x_ref.shape[0]):
        cols = slice(part * width, (part + 1) * width)
        ctx_ref[0, :, cols] = x_ref[part, 0]
        grads_ref[0, 0, :, cols] = x_ref[part, 1]


def unpack_cross(x, grads):
    parts, _, tokens, width = x.shape
    per = 4
    return pl.pallas_call(
        unpack_cross_kernel,
        grid=(parts // per,),
        in_specs=[
            pl.BlockSpec((per, 2, tokens, width), lambda j: (j, 0, 0, 0)),
            pl.BlockSpec(memory_space=pl.ANY),
        ],
        out_specs=[
            pl.BlockSpec((1, tokens, per * width), lambda j: (0, 0, j)),
            pl.BlockSpec((1, 1, tokens, per * width), lambda j: (3, 0, 0, j)),
        ],
        out_shape=[
            jax.ShapeDtypeStruct((1, tokens, parts * width), jnp.bfloat16),
            jax.ShapeDtypeStruct(grads.shape, jnp.bfloat16),
        ],
        input_output_aliases={1: 1},
        cost_estimate=pl.CostEstimate(flops=0, bytes_accessed=4 * x.size, transcendentals=0),
        compiler_params=pltpu.CompilerParams(vmem_limit_bytes=VMEM),
        name="unpack_cross",
    )(x, grads)


def project_kernel(own_ref, x_ref, w_ref, r_ref, *rest, per):
    terms, y_ref = rest[:-1], rest[-1]
    own = own_ref[0]
    y = mm(x_ref[...], w_ref[...], NN)
    mine = (pl.program_id(0) // per) == own
    y = y + jnp.where(mine, r_ref[...].astype(jnp.float32), 0.0)
    y_ref[...] = y.reshape(y_ref.shape)
    for offset, term in enumerate(terms):
        term[...] = y_ref[lax.rem(own + offset, len(terms))]


def project(context, weight, residual):
    owned, rows, depth = context.shape
    block = 512
    per = depth // block
    own = lax.axis_index("tp").astype(jnp.int32).reshape(1)
    return pl.pallas_call(
        functools.partial(project_kernel, per=per),
        grid=(weight.shape[1] // block,),
        in_specs=[
            pl.BlockSpec(memory_space=pltpu.SMEM),
            pl.BlockSpec((owned * rows, depth), lambda j: (0, 0)),
            pl.BlockSpec((depth, block), lambda j: (0, j)),
            pl.BlockSpec((owned * rows, block), lambda j: (0, lax.rem(j, per))),
        ],
        out_specs=[pl.BlockSpec((rows, block), lambda j: (0, j))] * owned,
        out_shape=[jax.ShapeDtypeStruct((rows, weight.shape[1]), jnp.float32)] * owned,
        scratch_shapes=[pltpu.VMEM((owned, rows, block), jnp.float32)],
        cost_estimate=pl.CostEstimate(
            flops=2 * owned * rows * depth * weight.shape[1],
            bytes_accessed=2 * weight.size,
            transcendentals=0,
        ),
        name="project",
    )(own, context.reshape(owned * rows, depth), weight, residual.reshape(owned * rows, depth))


def norm_kernel(*refs):
    terms, gain_ref, y_ref = refs[:-2], refs[-2], refs[-1]
    hidden = sum(term[...] for term in terms)
    power = jnp.mean(hidden * hidden, axis=1, keepdims=True)
    y = (hidden * lax.rsqrt(power + 1e-06) * gain_ref[...]).astype(jnp.bfloat16)
    for copy in range(y_ref.shape[0]):
        y_ref[copy] = y


def norm(terms, gain, copies):
    return pl.pallas_call(
        norm_kernel,
        out_shape=jax.ShapeDtypeStruct((copies,) + terms[0].shape, jnp.bfloat16),
        name="norm",
    )(*terms, gain.reshape(1, -1))


def caption_kernel(near_ref, far_ref, w_ref, kv_ref, acc):
    step = pl.program_id(0)
    half = near_ref.shape[0]
    for at, ref in ((0, near_ref), (half, far_ref)):
        terms = mm(ref[...], w_ref[...], NN)
        rows = slice(at, at + half)

        @pl.when(step == 0)
        def _():
            acc[rows] = terms

        @pl.when(step > 0)
        def _():
            acc[rows] += terms

    @pl.when(step == pl.num_programs(0) - 1)
    def _():
        kv_ref[...] = acc[...].astype(jnp.bfloat16)


def caption_projection(near, far, weight):
    half, depth = near.shape
    rows, width = 2 * half, weight.shape[1]
    block = 512
    return pl.pallas_call(
        caption_kernel,
        grid=(depth // block,),
        in_specs=[
            pl.BlockSpec((half, block), lambda j: (0, j)),
            pl.BlockSpec((half, block), lambda j: (0, j)),
            pl.BlockSpec((block, width), lambda j: (j, 0)),
        ],
        out_specs=pl.BlockSpec((rows, width), lambda j: (0, 0)),
        out_shape=jax.ShapeDtypeStruct((rows, width), jnp.bfloat16),
        scratch_shapes=[pltpu.VMEM((rows, width), jnp.float32)],
        compiler_params=pltpu.CompilerParams(vmem_limit_bytes=VMEM),
        cost_estimate=pl.CostEstimate(
            flops=2 * rows * depth * width,
            bytes_accessed=2 * rows * depth + 2 * depth * width,
            transcendentals=0,
        ),
        name="caption_projection",
    )(near, far, weight)


def split_kernel(own_ref, x_ref, *outs):
    block = x_ref.shape[1] // len(outs)
    for clip in range(len(outs)):
        for offset, out in enumerate(outs):

            @pl.when(lax.rem(own_ref[0] + offset, len(outs)) == clip)
            def _():
                out[...] = x_ref[:, clip * block : (clip + 1) * block]


def split_features(rows, groups, clips):
    count, depth = rows.shape
    own = lax.axis_index("tp").astype(jnp.int32).reshape(1)
    return pl.pallas_call(
        split_kernel,
        grid=(groups,),
        in_specs=[
            pl.BlockSpec(memory_space=pltpu.SMEM),
            pl.BlockSpec((count, depth // groups), lambda d: (0, d)),
        ],
        out_specs=[pl.BlockSpec((count, depth // (groups * clips)), lambda d: (0, d))] * clips,
        out_shape=[jax.ShapeDtypeStruct((count, depth // clips), rows.dtype)] * clips,
        cost_estimate=pl.CostEstimate(
            flops=0, bytes_accessed=4 * rows.size, transcendentals=0
        ),
        name="split_features",
    )(own, rows)


def weight_kernel(own_ref, *refs, clips):
    near, far, grads = refs[:clips], refs[clips : 2 * clips], refs[2 * clips : 3 * clips]
    kept_ref, sent_ref = refs[-2:]
    half = near[0].shape[0]
    total = sum(
        mm(x[...], g[:half], TN) + mm(y[...], g[half:], TN) for x, y, g in zip(near, far, grads)
    )
    mine = pl.program_id(0) == own_ref[0]

    @pl.when(mine)
    def _():
        kept_ref[...] = total

    @pl.when(jnp.logical_not(mine))
    def _():
        sent_ref[...] = total.astype(jnp.bfloat16)


def weight_terms(near, far, grads, groups):
    clips = len(near)
    rows, width = grads[0].shape
    block = near[0].shape[1] // groups
    own = lax.axis_index("dp").astype(jnp.int32).reshape(1)
    return pl.pallas_call(
        functools.partial(weight_kernel, clips=clips),
        grid=(groups,),
        in_specs=[pl.BlockSpec(memory_space=pltpu.SMEM)]
        + [pl.BlockSpec((rows // 2, block), lambda d: (0, d))] * (2 * clips)
        + [pl.BlockSpec((rows, width), lambda d: (0, 0))] * clips,
        out_specs=[pl.BlockSpec((block, width), lambda d: (0, 0))] * 2,
        out_shape=[
            jax.ShapeDtypeStruct((block, width), jnp.float32),
            jax.ShapeDtypeStruct((block, width), jnp.bfloat16),
        ],
        compiler_params=pltpu.CompilerParams(vmem_limit_bytes=VMEM),
        cost_estimate=pl.CostEstimate(
            flops=2 * clips * groups * rows * block * width,
            bytes_accessed=2 * clips * rows * (groups * block + width),
            transcendentals=0,
        ),
        name="weight_terms",
    )(own, *near, *far, *grads)


def add_kernel(kept_ref, taken_ref, y_ref):
    y_ref[...] = kept_ref[...] + taken_ref[...].astype(jnp.float32)


def add_taken(kept, taken):
    rows, width = kept.shape
    block = pl.BlockSpec((rows // 4, width), lambda j: (j, 0))
    return pl.pallas_call(
        add_kernel,
        grid=(4,),
        in_specs=[block, block],
        out_specs=block,
        out_shape=jax.ShapeDtypeStruct(kept.shape, jnp.float32),
        cost_estimate=pl.CostEstimate(
            flops=ADD_COST, bytes_accessed=10 * kept.size, transcendentals=0
        ),
        name="add_taken",
    )(kept, taken)


def shifts(size, offset):
    return [(at, (at + offset) % size) for at in range(size)]


def seq_exchange(x):
    return lax.all_to_all(x, "seq", split_axis=0, concat_axis=0, tiled=True)


def tp_terms(terms):
    size = len(terms)
    return [terms[0]] + [
        lax.ppermute(terms[offset], "tp", shifts(size, offset)) for offset in range(1, size)
    ]


CORES = 2


def gather_captions(copies):
    size = lax.axis_size("seq")
    groups = [list(range(core, size, CORES)) for core in range(CORES)]
    rows = lax.all_to_all(
        copies, "seq", split_axis=0, concat_axis=0, tiled=True, axis_index_groups=groups
    )
    return rows.reshape(-1, copies.shape[2])


def other_core(x):
    size = lax.axis_size("seq")
    return lax.ppermute(x, "seq", [(source, source ^ 1) for source in range(size)])


def caption_order(rows):
    size, core = lax.axis_size("seq"), lax.axis_index("seq") % CORES
    chips = jnp.arange(0, size, CORES, dtype=jnp.int32)
    places = jnp.concatenate([chips + core, chips + (1 - core)])
    return (places[:, None] * rows + jnp.arange(rows, dtype=jnp.int32)[None, :]).reshape(-1)


def body(
    enc_context,
    enc_residual,
    out_weight,
    norm_gain,
    kv_weight,
    caption_lengths,
    streams,
    cotangents,
):
    parts = lax.axis_size("seq")
    groups, clips = lax.axis_size("dp"), lax.axis_size("tp")
    local_width = kv_weight.shape[2]

    self_packed = pack(streams, cotangents, 0, 3, 0, parts)
    self_in = seq_exchange(self_packed)
    streams, cotangents, enc_context, _ = lax.optimization_barrier(
        (streams, cotangents, enc_context, self_packed)
    )
    terms = tp_terms(project(enc_context, out_weight, enc_residual))
    cross_packed = pack(streams, cotangents, 3, 1, 1, parts)
    kv_flat = kv_weight.reshape(kv_weight.shape[0], 2 * local_width)
    terms, kv_flat, cross_packed, _ = lax.optimization_barrier(
        (terms, kv_flat, cross_packed, self_in)
    )
    near = gather_captions(norm(terms, norm_gain, parts // CORES))
    self_out = None
    for head in range(local_width // HD):
        self_out = self_attention(self_in, head, self_out)

    near, cross_packed, _ = lax.optimization_barrier((near, cross_packed, self_out))
    cross_in = seq_exchange(cross_packed)
    far = other_core(near)
    near_terms = tp_terms(split_features(near, groups, clips))
    caption_kv = caption_projection(near, far, kv_flat)

    self_out, _, _, near_terms = lax.optimization_barrier(
        (self_out, cross_in, caption_kv, near_terms)
    )
    self_back = seq_exchange(self_out)
    far_terms = [other_core(x) for x in near_terms]
    order = caption_order(enc_context.shape[1])
    cross_out, caption_grads = cross_attention(caption_lengths, order, cross_in, caption_kv)
    caption_grads, far_terms = lax.optimization_barrier((caption_grads, far_terms))
    grads = tp_terms([caption_grads] * clips)
    kept, sent = weight_terms(near_terms, far_terms, grads, groups)

    cross_out, _, _ = lax.optimization_barrier((cross_out, self_back, sent))
    cross_back = seq_exchange(cross_out)
    self_ctx, stream_grads = unpack_self(self_back)
    taken = lax.ppermute(sent, "dp", shifts(groups, 1))
    kept, _ = lax.optimization_barrier((kept, self_ctx))
    grad = add_taken(kept, taken)
    weight_grad = grad.reshape(grad.shape[0], 2, local_width)
    cross_ctx, stream_grads = unpack_cross(cross_back, stream_grads)
    return (self_ctx, cross_ctx, stream_grads, weight_grad)


def solution(mesh):
    placed = (
        P("dp", "seq", "tp"),
        P("dp", "seq", "tp"),
        P("tp", None),
        P(),
        P(None, None, "seq"),
        P(("dp", "tp")),
        P(None, ("dp", "tp"), "seq", None),
        P(None, ("dp", "tp"), "seq", None),
    )
    return jax.shard_map(
        body,
        mesh=mesh,
        in_specs=placed,
        out_specs=(
            P(("dp", "tp"), "seq", None),
            P(("dp", "tp"), "seq", None),
            P(None, ("dp", "tp"), "seq", None),
            P(("dp", "tp"), None, "seq"),
        ),
        check_vma=False,
    )
```

time: 315 us -> 258 us (0.82)
  blocking collectives: 91.5 us -> 0 us
  starting transfers between devices: 10.6 us -> 49.1 us
  Pallas kernels: 83 us -> 97.1 us
  between operations: 14.4 us -> 1.4 us
  matrix products: 12 us -> 0 us
  waiting for transfers between devices: 89.6 us -> 95.6 us
  local copies, waits for them, and re-layouts: 7.56 us -> 13.1 us
    all_to_all x2 -> x0, blocking collectives: 91.5 us -> none  [the longest x1 59.1 us: body(): lax.all_to_all(self_out, 'seq', split_axis=0, concat_axis=0, tiled=True)]
    ppermute x0 -> x15, waiting for transfers between devices: none -> 52.7 us  [the longest x9 52.7 us: tp_terms(): lax.ppermute(terms[offset], 'tp', shifts(size, offset))]
    reduce_scatter x2 -> x0, waiting for transfers between devices: 32.3 us -> none  [the longest x1 32.3 us: body(): lax.psum_scatter(partial_value, 'tp', scatter_dimension=0, tiled=True)]
    all_to_all x2 -> x5, starting transfers between devices: 10.5 us -> 30.9 us  [the longest x4 24.8 us: seq_exchange(): return lax.all_to_all(x, 'seq', split_axis=0, concat_axis=0, tiled=True)]
    ppermute x0 -> x15, starting transfers between devices: none -> 18.1 us  [the longest x9 14.2 us: tp_terms(): lax.ppermute(terms[offset], 'tp', shifts(size, offset))]
    all_to_all x2 -> x5, waiting for transfers between devices: 57.2 us -> 43 us  [the longest x4 43 us: seq_exchange(): return lax.all_to_all(x, 'seq', split_axis=0, concat_axis=0, tiled=True)]
    dot_general x2 -> x0, matrix products: 12 us -> none  [the longest x1 6.59 us: body(): jnp.dot(states, kv_weight.reshape(D_TEXT, 2 * local_width), preferred_ele...]
    pallas_call x3 -> x9, Pallas kernels: 30.2 us -> 42.2 us  [the longest x1 9.38 us: caption_projection(): pl.pallas_call(caption_kernel, grid=(depth // block,), in_specs=[pl.Block...]
  transfers between devices with their start and end apart: 5 -> 20, of which waited for: 3 -> 10; matrix products, arithmetic and copies ran while one was open for 5% -> 3% of each run, Pallas kernels for 24% -> 33%
where the time goes in v2:
time: 258 us; the launch traced here: 256 us
  Pallas kernels  97.1 us (38%)
  waiting for transfers between devices  95.6 us (37%)
  starting transfers between devices  49.1 us (19%)
  local copies, waits for them, and re-layouts  13.1 us (5%)
    ppermute x9, waiting for transfers between devices, tp_terms(): lax.ppermute(terms[offset], 'tp', shifts(size, offset))  52.7 us
    all_to_all x4, waiting for transfers between devices, seq_exchange(): return lax.all_to_all(x, 'seq', split_axis=0, concat_axis=0, tiled=True)  43 us
    pallas_call x2, Pallas kernels, self_attention(): pl.pallas_call(functools.partial(self_kernel, steps=steps, per=per), grid...  36.1 us
    all_to_all x4, starting transfers between devices, seq_exchange(): return lax.all_to_all(x, 'seq', split_axis=0, concat_axis=0, tiled=True)  24.8 us
    ppermute x9, starting transfers between devices, tp_terms(): lax.ppermute(terms[offset], 'tp', shifts(size, offset))  14.2 us
    pallas_call x1, Pallas kernels, cross_attention(): pl.pallas_call(functools.partial(cross_kernel, steps=steps, per=per), gri...  10.6 us
    unnamed x33, local copies, waits for them, and re-layouts  9.56 us
    pallas_call x1, Pallas kernels, caption_projection(): pl.pallas_call(caption_kernel, grid=(depth // block,), in_specs=[pl.Block...  9.38 us
  transfers between devices with their start and end apart: 20, of which 10 were waited for; matrix products, arithmetic and copies ran while one was open for 3% of the time, Pallas kernels for 33%

profile of v2, /device:TPU:9, one launch (start us, length us, event | category | flops | bytes accessed | tf_op | source)
XLA Modules:
  0.0 256.5 jit_solution(11245671549078609910)
XLA Ops:
  0.6 4.7 %pack.2 = bf16[16,4,128,256]{3,2,1,0:T(8,128)(2,1)} custom-call(bf16[4,1,128,4096]{3,2,1,0:T(8,128)(2,1)} %s_ref.2, bf16[2,1,128,4096]{3,2,1,0:T(8,128)(2,1)} %c_ref.2), custom_call_target="tpu_custom_call" | custom-call | bytes 8388608 | tf_op jit(solution)/shard_map/pack/pallas_call | solution.py:199
  5.3 6.1 %all-to-all-start = ((bf16[16,4,128,256]{3,2,1,0:T(8,128)(2,1)}), bf16[16,4,128,256]{3,2,1,0:T(8,128)(2,1)}, u32[]{:S(2)}, u32[]{:S(2)}) async-start(bf16[16,4,128,256]{3,2,1,0:T(8,128)(2,1)} %pack.2), calls=%async_computation | async-start | bytes 8388608 | tf_op jit(solution)/shard_map/all_to_all | solution.py:475
  11.4 8.3 %project.1 = (f32[32,4096]{1,0:T(8,128)}, f32[32,4096]{1,0:T(8,128)}, f32[32,4096]{1,0:T(8,128)}, f32[32,4096]{1,0:T(8,128)}) custom-call(s32[1]{0:T(128)} %bitcast.own_ref, bf16[128,1024]{1,0:T(8,128)(2,1)} %bitcast.13, bf16[1024,4096]{1,0:T(8,128)(2,1)} %w_ref.1, bf16[128,1024]{1,0:T(8,128)(2,1)} %bitcast.14), custom_call_target="tpu_custom_call" | custom-call | flops 1073741824 | bytes 8388608 | tf_op jit(solution)/shard_map/project/pallas_call | solution.py:294
  21.3 3.3 %collective-permute-start.1 = (f32[32,4096]{1,0:T(8,128)}, f32[32,4096]{1,0:T(8,128)S(1)}, u32[]{:S(2)}, u32[]{:S(2)}) collective-permute-start(f32[32,4096]{1,0:T(8,128)} %get-tuple-element.46), channel_id=1, source_target_pairs={{0,2},{1,3},{2,0},{3,1},{4,6},{5,7},{6,4},{7,5},{8,10},{9,11},{10,... | collective-permute-start | bytes 1572872 | tf_op jit(solution)/shard_map/ppermute | solution.py:481
  25.4 4.9 %copy.14 = bf16[512,8,2,256]{3,1,2,0:T(8,128)(2,1)} copy(bf16[512,8,2,256]{3,2,1,0:T(2,128)(2,1)} %bitcast.12) | data formatting | bytes 8388608
  30.2 3.8 %pack.3 = bf16[16,2,128,256]{3,2,1,0:T(8,128)(2,1)} custom-call(bf16[4,1,128,4096]{3,2,1,0:T(8,128)(2,1)} %s_ref.2, bf16[2,1,128,4096]{3,2,1,0:T(8,128)(2,1)} %c_ref.2), custom_call_target="tpu_custom_call" | custom-call | bytes 4194304 | tf_op jit(solution)/shard_map/pack/pallas_call | solution.py:199
  35.8 12.1 %collective-permute-done.1.refs_2_ = f32[32,4096]{1,0:T(8,128)S(1)} collective-permute-done((f32[32,4096]{1,0:T(8,128)}, f32[32,4096]{1,0:T(8,128)S(1)}, u32[]{:S(2)}, u32[]{:S(2)}) %collective-permute-start.1) | collective-permute-done | bytes 524320 | tf_op jit(solution)/shard_map/ppermute | solution.py:481
  47.9 21.2 %all-to-all-done.q_ref.k_ref.v_ref.g_ref = bf16[16,4,128,256]{3,2,1,0:T(8,128)(2,1)} async-done(((bf16[16,4,128,256]{3,2,1,0:T(8,128)(2,1)}), bf16[16,4,128,256]{3,2,1,0:T(8,128)(2,1)}, u32[]{:S(2)}, u32[]{:S(2)}) %all-to-all-start) | async-done | bytes 4194336 | tf_op jit(solution)/shard_map/all_to_all | solution.py:475
  69.1 3.2 %norm.1 = bf16[8,32,4096]{2,1,0:T(8,128)(2,1)} custom-call(f32[32,4096]{1,0:T(8,128)} %get-tuple-element.50.refs_0_, f32[32,4096]{1,0:T(8,128)} %copy-done.2, f32[32,4096]{1,0:T(8,128)} %copy-done.3, f32[32,4096]{1,0:T(8,128)} %copy-done.4, f32[1,4096]{1,0:T(1,128)} %bitcast.15), custom_call_target="tpu_custom_call" | custom-call | tf_op jit(solution)/shard_map/norm/pallas_call | solution.py:325
  72.3 6.1 %all-to-all-start.1 = ((bf16[8,32,4096]{2,1,0:T(8,128)(2,1)}), bf16[8,32,4096]{2,1,0:T(8,128)(2,1)S(1)}, u32[]{:S(2)}, u32[]{:S(2)}) async-start(bf16[8,32,4096]{2,1,0:T(8,128)(2,1)} %norm.1), calls=%async_computation.1 | async-start | bytes 4194304 | tf_op jit(solution)/shard_map/all_to_all | solution.py:491
  78.3 18.1 %self_attention.2.rest_0_ = bf16[16,4,128,256]{3,2,1,0:T(8,128)(2,1)} custom-call(bf16[16,4,128,256]{3,2,1,0:T(8,128)(2,1)} %all-to-all-done.q_ref.k_ref.v_ref.g_ref, bf16[16,4,128,256]{3,2,1,0:T(8,128)(2,1)} %all-to-all-done.q_ref.k_ref.v_ref.g_ref, bf16[16,4,128,256]{3,2,1,0:T(8,128)(2,1)} %all-to-all-done.q_ref.k_ref.v_ref.g_ref, ...), custom_call_target="tpu_custom_call" | custom-call | flops 12884901888 | bytes 4194304 | tf_op jit(solution)/shard_map/self_attention/pallas_call | solution.py:93
  96.4 18.1 %self_attention.3 = bf16[16,4,128,256]{3,2,1,0:T(8,128)(2,1)} custom-call(bf16[16,4,128,256]{3,2,1,0:T(8,128)(2,1)} %all-to-all-done.q_ref.k_ref.v_ref.g_ref, bf16[16,4,128,256]{3,2,1,0:T(8,128)(2,1)} %all-to-all-done.q_ref.k_ref.v_ref.g_ref, bf16[16,4,128,256]{3,2,1,0:T(8,128)(2,1)} %all-to-all-done.q_ref.k_ref.v_ref.g_ref, ...), custom_call_target="tpu_custom_call", output_to_operand_aliasing={{}: (4, {})} | custom-call | flops 12884901888 | bytes 4194304 | tf_op jit(solution)/shard_map/self_attention/pallas_call | solution.py:93
  115.3 5.5 %all-to-all-start.2 = ((bf16[16,2,128,256]{3,2,1,0:T(8,128)(2,1)}), bf16[16,2,128,256]{3,2,1,0:T(8,128)(2,1)}, u32[]{:S(2)}, u32[]{:S(2)}) async-start(bf16[16,2,128,256]{3,2,1,0:T(8,128)(2,1)} %pack.3), calls=%async_computation.2 | async-start | bytes 4194304 | tf_op jit(solution)/shard_map/all_to_all | solution.py:475
  120.8 2.8 %split_features.1 = (bf16[256,1024]{1,0:T(8,128)(2,1)}, bf16[256,1024]{1,0:T(8,128)(2,1)}, bf16[256,1024]{1,0:T(8,128)(2,1)}, bf16[256,1024]{1,0:T(8,128)(2,1)}) custom-call(s32[1]{0:T(128)} %bitcast.own_ref, bf16[256,4096]{1,0:T(8,128)(2,1)} %bitcast.9), custom_call_target="tpu_custom_call" | custom-call | bytes 4194304 | tf_op jit(solution)/shard_map/split_features/pallas_call | solution.py:390
  125.2 3.3 %collective-permute-start.5 = (bf16[256,1024]{1,0:T(8,128)(2,1)}, bf16[256,1024]{1,0:T(8,128)(2,1)S(1)}, u32[]{:S(2)}, u32[]{:S(2)}) collective-permute-start(bf16[256,1024]{1,0:T(8,128)(2,1)} %get-tuple-element.60), channel_id=1, source_target_pairs={{0,2},{1,3},{2,0},{3,1},{4,6},{5,7},{6,4},{7,5},{8,10},{9,11},{10,... | collective-permute-start | bytes 1572872 | tf_op jit(solution)/shard_map/ppermute | solution.py:481
  129.2 9.4 %caption_projection.1.k_ref.v_ref = bf16[512,512]{1,0:T(8,128)(2,1)} custom-call(bf16[256,4096]{1,0:T(8,128)(2,1)} %bitcast.10, bf16[256,4096]{1,0:T(8,128)(2,1)} %collective-permute-done.3.far_ref, bf16[4096,512]{1,0:T(8,128)(2,1)} %bitcast.11), custom_call_target="tpu_custom_call" | custom-call | flops 2147483648 | bytes 8388608 | tf_op jit(solution)/shard_map/caption_projection/pallas_call | solution.py:356
  139.7 12.0 %collective-permute-done.5.refs_2_ = bf16[256,1024]{1,0:T(8,128)(2,1)S(1)} collective-permute-done((bf16[256,1024]{1,0:T(8,128)(2,1)}, bf16[256,1024]{1,0:T(8,128)(2,1)S(1)}, u32[]{:S(2)}, u32[]{:S(2)}) %collective-permute-start.5) | collective-permute-done | bytes 524320 | tf_op jit(solution)/shard_map/ppermute | solution.py:481
  151.7 6.7 %all-to-all-start.3 = ((bf16[16,4,128,256]{3,2,1,0:T(8,128)(2,1)}), bf16[16,4,128,256]{3,2,1,0:T(8,128)(2,1)}, u32[]{:S(2)}, u32[]{:S(2)}) async-start(bf16[16,4,128,256]{3,2,1,0:T(8,128)(2,1)} %self_attention.3), calls=%async_computation.3 | async-start | bytes 8388608 | tf_op jit(solution)/shard_map/all_to_all | solution.py:475
  160.9 10.6 %cross_attention.1 = (bf16[16,2,128,256]{3,2,1,0:T(8,128)(2,1)}, bf16[512,512]{1,0:T(8,128)(2,1)}) custom-call(s32[1]{0:T(128)S(6)} %copy.17.len_ref, s32[1,512]{1,0:T(1,128)} %add.51.pos_ref, bf16[16,2,128,256]{3,2,1,0:T(8,128)(2,1)} %all-to-all-done.2.q_ref.g_ref, bf16[16,2,128,256]{3,2,1,0:T(8,128)(2,1)} %all-to-all-done.2.q_ref.g_ref, ...), custom_call_target="tpu_custom_call" | custom-call | flops 6442450944 | bytes 5242880 | tf_op jit(solution)/shard_map/cross_attention/pallas_call | solution.py:158
  173.2 1.9 collective-permute-start.13
  176.1 10.6 %collective-permute-done.13.refs_11_ = bf16[512,512]{1,0:T(8,128)(2,1)S(1)} collective-permute-done((bf16[512,512]{1,0:T(8,128)(2,1)}, bf16[512,512]{1,0:T(8,128)(2,1)S(1)}, u32[]{:S(2)}, u32[]{:S(2)}) %collective-permute-start.13) | collective-permute-done | bytes 524320 | tf_op jit(solution)/shard_map/ppermute | solution.py:481
  186.7 3.1 %collective-permute-done.12.refs_10_ = bf16[512,512]{1,0:T(8,128)(2,1)S(1)} collective-permute-done((bf16[512,512]{1,0:T(8,128)(2,1)}, bf16[512,512]{1,0:T(8,128)(2,1)S(1)}, u32[]{:S(2)}, u32[]{:S(2)}) %collective-permute-start.12) | collective-permute-done | bytes 524320 | tf_op jit(solution)/shard_map/ppermute | solution.py:481
  189.8 12.1 %collective-permute-done.11.refs_9_ = bf16[512,512]{1,0:T(8,128)(2,1)S(1)} collective-permute-done((bf16[512,512]{1,0:T(8,128)(2,1)}, bf16[512,512]{1,0:T(8,128)(2,1)S(1)}, u32[]{:S(2)}, u32[]{:S(2)}) %collective-permute-start.11) | collective-permute-done | bytes 524320 | tf_op jit(solution)/shard_map/ppermute | solution.py:481
  202.8 6.2 %weight_terms.1 = (f32[512,512]{1,0:T(8,128)}, bf16[512,512]{1,0:T(8,128)(2,1)}) custom-call(s32[1]{0:T(128)} %bitcast.5.own_ref, bf16[256,1024]{1,0:T(8,128)(2,1)} %get-tuple-element.65.refs_0_, bf16[256,1024]{1,0:T(8,128)(2,1)} %copy-done.6, bf16[256,1024]{1,0:T(8,128)(2,1)} %copy-done.7, bf16[256,1024]{1,0:T(8,128)(2,1)} %collective-permute-done.6.refs_3_, ...), custom_call_target="tpu_custom_call" | custom-call | flops 2147483648 | bytes 6291456 | tf_op jit(solution)/shard_map/weight_terms/pallas_call | solution.py:429
  209.0 2.0 collective-permute-start.14
  211.0 5.1 %all-to-all-done.3.x_ref = bf16[16,4,128,256]{3,2,1,0:T(8,128)(2,1)} async-done(((bf16[16,4,128,256]{3,2,1,0:T(8,128)(2,1)}), bf16[16,4,128,256]{3,2,1,0:T(8,128)(2,1)}, u32[]{:S(2)}, u32[]{:S(2)}) %all-to-all-start.3) | async-done | bytes 4194336 | tf_op jit(solution)/shard_map/all_to_all | solution.py:475
  216.1 6.6 %all-to-all-start.4 = ((bf16[16,2,128,256]{3,2,1,0:T(8,128)(2,1)}), bf16[16,2,128,256]{3,2,1,0:T(8,128)(2,1)S(1)}, u32[]{:S(2)}, u32[]{:S(2)}) async-start(bf16[16,2,128,256]{3,2,1,0:T(8,128)(2,1)} %get-tuple-element.76), calls=%async_computation.4 | async-start | bytes 4194304 | tf_op jit(solution)/shard_map/all_to_all | solution.py:475
  222.7 4.9 %unpack_self.1 = (bf16[1,128,4096]{2,1,0:T(8,128)(2,1)}, bf16[4,1,128,4096]{3,2,1,0:T(8,128)(2,1)}) custom-call(bf16[16,4,128,256]{3,2,1,0:T(8,128)(2,1)} %all-to-all-done.3.x_ref), custom_call_target="tpu_custom_call" | custom-call | bytes 8388608 | tf_op jit(solution)/shard_map/unpack_self/pallas_call | solution.py:227
  228.3 3.4 %add_taken.1 = f32[512,512]{1,0:T(8,128)} custom-call(f32[512,512]{1,0:T(8,128)} %get-tuple-element.81.kept_ref, bf16[512,512]{1,0:T(8,128)(2,1)} %copy-done.15), custom_call_target="tpu_custom_call" | custom-call | flops 20000000000 | bytes 2621440 | tf_op jit(solution)/shard_map/add_taken/pallas_call | solution.py:457
  231.8 2.8 %reshape.76 = f32[512,2,256]{2,1,0:T(2,128)} reshape(f32[512,512]{1,0:T(8,128)} %add_taken.1) | data formatting | bytes 2097152 | tf_op jit(solution)/shard_map/reshape | solution.py:562
  234.6 16.7 %all-to-all-done.4.x_ref = bf16[16,2,128,256]{3,2,1,0:T(8,128)(2,1)S(1)} async-done(((bf16[16,2,128,256]{3,2,1,0:T(8,128)(2,1)}), bf16[16,2,128,256]{3,2,1,0:T(8,128)(2,1)S(1)}, u32[]{:S(2)}, u32[]{:S(2)}) %all-to-all-start.4) | async-done | bytes 2097184 | tf_op jit(solution)/shard_map/all_to_all | solution.py:475
  252.7 3.8 %unpack_cross.1 = (bf16[1,128,4096]{2,1,0:T(8,128)(2,1)}, bf16[4,1,128,4096]{3,2,1,0:T(8,128)(2,1)}) custom-call(bf16[16,2,128,256]{3,2,1,0:T(8,128)(2,1)} %copy-done.1, bf16[4,1,128,4096]{3,2,1,0:T(8,128)(2,1)} %get-tuple-element.77._), custom_call_target="tpu_custom_call", output_to_operand_aliasing={{1}: (1, {})} | custom-call | bytes 4194304 | tf_op jit(solution)/shard_map/unpack_cross/pallas_call | solution.py:256
  (59 shorter events, 15.9 us)
Async XLA Ops:
  5.3 63.8 %all-to-all-start = ((bf16[16,4,128,256]{3,2,1,0:T(8,128)(2,1)}), bf16[16,4,128,256]{3,2,1,0:T(8,128)(2,1)}, u32[]{:S(2)}, u32[]{:S(2)}) async-start(bf16[16,4,128,256]{3,2,1,0:T(8,128)(2,1)} %pack.2), calls=%async_computation | async-start | bytes 8388608 | tf_op jit(solution)/shard_map/all_to_all | solution.py:475
  19.7 16.1 %collective-permute-start = (f32[32,4096]{1,0:T(8,128)}, f32[32,4096]{1,0:T(8,128)S(1)}, u32[]{:S(2)}, u32[]{:S(2)}) collective-permute-start(f32[32,4096]{1,0:T(8,128)} %get-tuple-element.45), channel_id=1, source_target_pairs={{0,1},{1,2},{2,3},{3,0},{4,5},{5,6},{6,7},{7,4},{8,9},{9,10},{10,1... | collective-permute-start | bytes 1572872 | tf_op jit(solution)/shard_map/ppermute | solution.py:481
  21.3 26.5 %collective-permute-start.1 = (f32[32,4096]{1,0:T(8,128)}, f32[32,4096]{1,0:T(8,128)S(1)}, u32[]{:S(2)}, u32[]{:S(2)}) collective-permute-start(f32[32,4096]{1,0:T(8,128)} %get-tuple-element.46), channel_id=1, source_target_pairs={{0,2},{1,3},{2,0},{3,1},{4,6},{5,7},{6,4},{7,5},{8,10},{9,11},{10,... | collective-permute-start | bytes 1572872 | tf_op jit(solution)/shard_map/ppermute | solution.py:481
  24.6 23.2 %collective-permute-start.2 = (f32[32,4096]{1,0:T(8,128)}, f32[32,4096]{1,0:T(8,128)S(1)}, u32[]{:S(2)}, u32[]{:S(2)}) collective-permute-start(f32[32,4096]{1,0:T(8,128)} %get-tuple-element.47), channel_id=1, source_target_pairs={{0,3},{1,0},{2,1},{3,2},{4,7},{5,4},{6,5},{7,6},{8,11},{9,8},{10,9... | collective-permute-start | bytes 1572872 | tf_op jit(solution)/shard_map/ppermute | solution.py:481
  35.8 33.3 %copy-start.2 = (f32[32,4096]{1,0:T(8,128)}, f32[32,4096]{1,0:T(8,128)S(1)}, u32[]{:S(2)}) copy-start(f32[32,4096]{1,0:T(8,128)S(1)} %collective-permute-done.refs_1_) | copy-start | bytes 1572868
  47.9 21.2 %copy-start.3 = (f32[32,4096]{1,0:T(8,128)}, f32[32,4096]{1,0:T(8,128)S(1)}, u32[]{:S(2)}) copy-start(f32[32,4096]{1,0:T(8,128)S(1)} %collective-permute-done.1.refs_2_) | copy-start | bytes 1572868
  47.9 21.2 %copy-start.4 = (f32[32,4096]{1,0:T(8,128)}, f32[32,4096]{1,0:T(8,128)S(1)}, u32[]{:S(2)}) copy-start(f32[32,4096]{1,0:T(8,128)S(1)} %collective-permute-done.2.refs_3_) | copy-start | bytes 1572868
  72.3 42.2 %all-to-all-start.1 = ((bf16[8,32,4096]{2,1,0:T(8,128)(2,1)}), bf16[8,32,4096]{2,1,0:T(8,128)(2,1)S(1)}, u32[]{:S(2)}, u32[]{:S(2)}) async-start(bf16[8,32,4096]{2,1,0:T(8,128)(2,1)} %norm.1), calls=%async_computation.1 | async-start | bytes 4194304 | tf_op jit(solution)/shard_map/all_to_all | solution.py:491
  114.5 6.3 %copy-start = (bf16[8,32,4096]{2,1,0:T(8,128)(2,1)}, bf16[8,32,4096]{2,1,0:T(8,128)(2,1)S(1)}, u32[]{:S(2)}) copy-start(bf16[8,32,4096]{2,1,0:T(8,128)(2,1)S(1)} %all-to-all-done.1) | copy-start | bytes 6291460
  114.5 14.8 %collective-permute-start.3 = (bf16[256,4096]{1,0:T(8,128)(2,1)S(1)}, bf16[256,4096]{1,0:T(8,128)(2,1)}, u32[]{:S(2)}, u32[]{:S(2)}) collective-permute-start(bf16[256,4096]{1,0:T(8,128)(2,1)S(1)} %bitcast.8), channel_id=1, source_target_pairs={{0,4},{4,0},{8,12},{12,8},{16,20},{20,16},{24,28},{28,24},{32,36},... | collective-permute-start | bytes 6291464 | tf_op jit(solution)/shard_map/ppermute | solution.py:499
  115.3 36.3 %all-to-all-start.2 = ((bf16[16,2,128,256]{3,2,1,0:T(8,128)(2,1)}), bf16[16,2,128,256]{3,2,1,0:T(8,128)(2,1)}, u32[]{:S(2)}, u32[]{:S(2)}) async-start(bf16[16,2,128,256]{3,2,1,0:T(8,128)(2,1)} %pack.3), calls=%async_computation.2 | async-start | bytes 4194304 | tf_op jit(solution)/shard_map/all_to_all | solution.py:475
  123.6 16.1 %collective-permute-start.4 = (bf16[256,1024]{1,0:T(8,128)(2,1)}, bf16[256,1024]{1,0:T(8,128)(2,1)S(1)}, u32[]{:S(2)}, u32[]{:S(2)}) collective-permute-start(bf16[256,1024]{1,0:T(8,128)(2,1)} %get-tuple-element.59), channel_id=1, source_target_pairs={{0,1},{1,2},{2,3},{3,0},{4,5},{5,6},{6,7},{7,4},{8,9},{9,10},{10,1... | collective-permute-start | bytes 1572872 | tf_op jit(solution)/shard_map/ppermute | solution.py:481
  125.2 26.5 %collective-permute-start.5 = (bf16[256,1024]{1,0:T(8,128)(2,1)}, bf16[256,1024]{1,0:T(8,128)(2,1)S(1)}, u32[]{:S(2)}, u32[]{:S(2)}) collective-permute-start(bf16[256,1024]{1,0:T(8,128)(2,1)} %get-tuple-element.60), channel_id=1, source_target_pairs={{0,2},{1,3},{2,0},{3,1},{4,6},{5,7},{6,4},{7,5},{8,10},{9,11},{10,... | collective-permute-start | bytes 1572872 | tf_op jit(solution)/shard_map/ppermute | solution.py:481
  128.5 23.1 %collective-permute-start.6 = (bf16[256,1024]{1,0:T(8,128)(2,1)}, bf16[256,1024]{1,0:T(8,128)(2,1)}, u32[]{:S(2)}, u32[]{:S(2)}) collective-permute-start(bf16[256,1024]{1,0:T(8,128)(2,1)} %get-tuple-element.61), channel_id=1, source_target_pairs={{0,3},{1,0},{2,1},{3,2},{4,7},{5,4},{6,5},{7,6},{8,11},{9,8},{10,9... | collective-permute-start | bytes 1572872 | tf_op jit(solution)/shard_map/ppermute | solution.py:481
  139.7 20.6 %copy-start.6 = (bf16[256,1024]{1,0:T(8,128)(2,1)}, bf16[256,1024]{1,0:T(8,128)(2,1)S(1)}, u32[]{:S(2)}) copy-start(bf16[256,1024]{1,0:T(8,128)(2,1)S(1)} %collective-permute-done.4.refs_1_) | copy-start | bytes 1572868
  151.6 8.7 %copy-start.7 = (bf16[256,1024]{1,0:T(8,128)(2,1)}, bf16[256,1024]{1,0:T(8,128)(2,1)S(1)}, u32[]{:S(2)}) copy-start(bf16[256,1024]{1,0:T(8,128)(2,1)S(1)} %collective-permute-done.5.refs_2_) | copy-start | bytes 1572868
  151.7 8.2 %copy-start.5 = (bf16[256,1024]{1,0:T(8,128)(2,1)S(1)}, bf16[256,1024]{1,0:T(8,128)(2,1)}, u32[]{:S(2)}) copy-start(bf16[256,1024]{1,0:T(8,128)(2,1)} %get-tuple-element.65.refs_0_) | copy-start | bytes 1572868
  151.7 64.5 %all-to-all-start.3 = ((bf16[16,4,128,256]{3,2,1,0:T(8,128)(2,1)}), bf16[16,4,128,256]{3,2,1,0:T(8,128)(2,1)}, u32[]{:S(2)}, u32[]{:S(2)}) async-start(bf16[16,4,128,256]{3,2,1,0:T(8,128)(2,1)} %self_attention.3), calls=%async_computation.3 | async-start | bytes 8388608 | tf_op jit(solution)/shard_map/all_to_all | solution.py:475
  159.9 11.6 %collective-permute-start.7 = (bf16[256,1024]{1,0:T(8,128)(2,1)S(1)}, bf16[256,1024]{1,0:T(8,128)(2,1)S(1)}, u32[]{:S(2)}, u32[]{:S(2)}) collective-permute-start(bf16[256,1024]{1,0:T(8,128)(2,1)S(1)} %copy-done.5), channel_id=1, source_target_pairs={{0,4},{4,0},{8,12},{12,8},{16,20},{20,16},{24,28},{28,24},{32,36},... | collective-permute-start | bytes 1572872 | tf_op jit(solution)/shard_map/ppermute | solution.py:499
  160.2 11.3 %collective-permute-start.8 = (bf16[256,1024]{1,0:T(8,128)(2,1)S(1)}, bf16[256,1024]{1,0:T(8,128)(2,1)S(1)}, u32[]{:S(2)}, u32[]{:S(2)}) collective-permute-start(bf16[256,1024]{1,0:T(8,128)(2,1)S(1)} %collective-permute-done.4.refs_1_), channel_id=1, source_target_pairs={{0,4},{4,0},{8,12},{12,8},{16,20},{20,16},{24,28},{28,24},{32,36},... | collective-permute-start | bytes 1572872 | tf_op jit(solution)/shard_map/ppermute | solution.py:499
  160.4 11.1 %collective-permute-start.9 = (bf16[256,1024]{1,0:T(8,128)(2,1)S(1)}, bf16[256,1024]{1,0:T(8,128)(2,1)S(1)}, u32[]{:S(2)}, u32[]{:S(2)}) collective-permute-start(bf16[256,1024]{1,0:T(8,128)(2,1)S(1)} %collective-permute-done.5.refs_2_), channel_id=1, source_target_pairs={{0,4},{4,0},{8,12},{12,8},{16,20},{20,16},{24,28},{28,24},{32,36},... | collective-permute-start | bytes 1572872 | tf_op jit(solution)/shard_map/ppermute | solution.py:499
  160.7 11.6 %collective-permute-start.10 = (bf16[256,1024]{1,0:T(8,128)(2,1)}, bf16[256,1024]{1,0:T(8,128)(2,1)S(1)}, u32[]{:S(2)}, u32[]{:S(2)}) collective-permute-start(bf16[256,1024]{1,0:T(8,128)(2,1)} %collective-permute-done.6.refs_3_), channel_id=1, source_target_pairs={{0,4},{4,0},{8,12},{12,8},{16,20},{20,16},{24,28},{28,24},{32,36},... | collective-permute-start | bytes 1572872 | tf_op jit(solution)/shard_map/ppermute | solution.py:499
  171.5 30.4 %copy-start.8 = (bf16[256,1024]{1,0:T(8,128)(2,1)}, bf16[256,1024]{1,0:T(8,128)(2,1)S(1)}, u32[]{:S(2)}) copy-start(bf16[256,1024]{1,0:T(8,128)(2,1)S(1)} %collective-permute-done.7.refs_4_) | copy-start | bytes 1572868
  171.5 30.4 %copy-start.9 = (bf16[256,1024]{1,0:T(8,128)(2,1)}, bf16[256,1024]{1,0:T(8,128)(2,1)S(1)}, u32[]{:S(2)}) copy-start(bf16[256,1024]{1,0:T(8,128)(2,1)S(1)} %collective-permute-done.8.refs_5_) | copy-start | bytes 1572868
  173.2 13.5 %collective-permute-start.13 = (bf16[512,512]{1,0:T(8,128)(2,1)}, bf16[512,512]{1,0:T(8,128)(2,1)S(1)}, u32[]{:S(2)}, u32[]{:S(2)}) collective-permute-start(bf16[512,512]{1,0:T(8,128)(2,1)} %get-tuple-element.74.refs_8_), channel_id=1, source_target_pairs={{0,3},{1,0},{2,1},{3,2},{4,7},{5,4},{6,5},{7,6},{8,11},{9,8},{10,9... | collective-permute-start | bytes 1572872 | tf_op jit(solution)/shard_map/ppermute | solution.py:481
  175.1 14.7 %collective-permute-start.12 = (bf16[512,512]{1,0:T(8,128)(2,1)}, bf16[512,512]{1,0:T(8,128)(2,1)S(1)}, u32[]{:S(2)}, u32[]{:S(2)}) collective-permute-start(bf16[512,512]{1,0:T(8,128)(2,1)} %get-tuple-element.74.refs_8_), channel_id=1, source_target_pairs={{0,2},{1,3},{2,0},{3,1},{4,6},{5,7},{6,4},{7,5},{8,10},{9,11},{10,... | collective-permute-start | bytes 1572872 | tf_op jit(solution)/shard_map/ppermute | solution.py:481
  176.0 25.9 %collective-permute-start.11 = (bf16[512,512]{1,0:T(8,128)(2,1)}, bf16[512,512]{1,0:T(8,128)(2,1)S(1)}, u32[]{:S(2)}, u32[]{:S(2)}) collective-permute-start(bf16[512,512]{1,0:T(8,128)(2,1)} %get-tuple-element.74.refs_8_), channel_id=1, source_target_pairs={{0,1},{1,2},{2,3},{3,0},{4,5},{5,6},{6,7},{7,4},{8,9},{9,10},{10,1... | collective-permute-start | bytes 1572872 | tf_op jit(solution)/shard_map/ppermute | solution.py:481
  186.7 15.2 %copy-start.12 = (bf16[512,512]{1,0:T(8,128)(2,1)}, bf16[512,512]{1,0:T(8,128)(2,1)S(1)}, u32[]{:S(2)}) copy-start(bf16[512,512]{1,0:T(8,128)(2,1)S(1)} %collective-permute-done.13.refs_11_) | copy-start | bytes 1572868
  189.8 12.1 %copy-start.13 = (bf16[512,512]{1,0:T(8,128)(2,1)}, bf16[512,512]{1,0:T(8,128)(2,1)S(1)}, u32[]{:S(2)}) copy-start(bf16[512,512]{1,0:T(8,128)(2,1)S(1)} %collective-permute-done.12.refs_10_) | copy-start | bytes 1572868
  209.0 18.6 %collective-permute-start.14 = (bf16[512,512]{1,0:T(8,128)(2,1)}, bf16[512,512]{1,0:T(8,128)(2,1)S(1)}, u32[]{:S(2)}, u32[]{:S(2)}) collective-permute-start(bf16[512,512]{1,0:T(8,128)(2,1)} %get-tuple-element.75), channel_id=1, source_target_pairs={{0,64},{64,0},{1,65},{65,1},{2,66},{66,2},{3,67},{67,3},{4,68},{68... | collective-permute-start | bytes 1572872 | tf_op jit(solution)/shard_map/ppermute | solution.py:559
  216.1 35.2 %all-to-all-start.4 = ((bf16[16,2,128,256]{3,2,1,0:T(8,128)(2,1)}), bf16[16,2,128,256]{3,2,1,0:T(8,128)(2,1)S(1)}, u32[]{:S(2)}, u32[]{:S(2)}) async-start(bf16[16,2,128,256]{3,2,1,0:T(8,128)(2,1)} %get-tuple-element.76), calls=%async_computation.4 | async-start | bytes 4194304 | tf_op jit(solution)/shard_map/all_to_all | solution.py:475
  251.3 1.3 copy-start.1
  (4 other events, 3.3 us)

commit v3 on v2

--- a/solution.py
+++ b/solution.py
@@ -13,7 +13,12 @@
 SCALE = 1.0 / math.sqrt(HD)
 LOG2E = math.log2(math.e)
 VMEM = 56 * 2**20
+SMALL = 12 * 2**20
+MIDDLE = 28 * 2**20
+VMEM_SELF = 36 * 2**20
 ADD_COST = 2 * 10**10
+CROSS_COST = 6 * 10**9
+CORES = 2
 
 NT = (((1,), (1,)), ((), ()))
 NN = (((1,), (0,)), ((), ()))
@@ -99,7 +104,7 @@
         out_shape=jax.ShapeDtypeStruct(x.shape, jnp.bfloat16),
         scratch_shapes=[pltpu.VMEM((HD, total), jnp.float32)] * 2,
         input_output_aliases={4: 0} if earlier else {},
-        compiler_params=pltpu.CompilerParams(vmem_limit_bytes=VMEM),
+        compiler_params=pltpu.CompilerParams(vmem_limit_bytes=VMEM_SELF),
         cost_estimate=pl.CostEstimate(
             flops=24 * total * total * HD,
             bytes_accessed=16 * total * HD,
@@ -109,7 +114,7 @@
     )(x, x, x, x, *earlier)
 
 
-def cross_kernel(len_ref, pos_ref, q_ref, g_ref, k_ref, v_ref, y_ref, d_ref, dk_acc, dv_acc, *, steps, per):
+def cross_kernel(core_ref, len_ref, pos_ref, x_ref, k_ref, v_ref, y_ref, d_ref, dk_acc, dv_acc):
     step = pl.program_id(0)
     total = k_ref.shape[0]
 
@@ -118,24 +123,31 @@
         dk_acc[...] = jnp.zeros_like(dk_acc)
         dv_acc[...] = jnp.zeros_like(dv_acc)
 
-    rows = per * q_ref.shape[2]
-    heads = q_ref.shape[3] // HD
+    chips, _, tokens, width = x_ref.shape
+    rows = chips * CORES * tokens
+    heads = width // HD
     valid = jnp.broadcast_to(pos_ref[...], (rows, total)) < len_ref[0]
     for head in range(heads):
         cols = slice(head * HD, (head + 1) * HD)
         context, grad_query, dk, dv = attend_rows(
-            q_ref[:, 0, :, cols].reshape(rows, HD),
+            jnp.concatenate([x_ref[:, 0, :, cols], x_ref[:, 2, :, cols]]).reshape(rows, HD),
             k_ref[:, cols],
             v_ref[:, cols],
-            g_ref[:, 0, :, cols].reshape(rows, HD),
+            jnp.concatenate([x_ref[:, 1, :, cols], x_ref[:, 3, :, cols]]).reshape(rows, HD),
             valid,
         )
-        y_ref[:, 0, :, cols] = context.astype(jnp.bfloat16).reshape(per, -1, HD)
-        y_ref[:, 1, :, cols] = grad_query.astype(jnp.bfloat16).reshape(per, -1, HD)
+        shape = (CORES, chips, tokens, HD)
+        context = context.astype(jnp.bfloat16).reshape(shape)
+        grad_query = grad_query.astype(jnp.bfloat16).reshape(shape)
+        for chip in range(chips):
+            for other in range(CORES):
+                at = CORES * chip + lax.rem(core_ref[0] + other, CORES)
+                y_ref[at, 0, :, cols] = context[other, chip]
+                y_ref[at, 1, :, cols] = grad_query[other, chip]
         dk_acc[head] += dk
         dv_acc[head] += dv
 
-    @pl.when(step == steps - 1)
+    @pl.when(step == pl.num_programs(0) - 1)
     def _():
         for head in range(heads):
             cols = slice(head * HD, (head + 1) * HD)
@@ -144,45 +156,40 @@
             d_ref[:, cols] = dv_acc[head].T.astype(jnp.bfloat16)
 
 
-def cross_attention(lengths, positions, x, kv):
-    blocks, _, tokens, width = x.shape
+def cross_attention(core, lengths, positions, x, kv):
+    chips, _, tokens, width = x.shape
     captions = kv.shape[0]
-    per = max(1, 512 // tokens)
-    steps = blocks // per
+    per = max(1, 512 // (CORES * tokens))
     heads = width // HD
-    total = blocks * tokens
-
-    def rows(which):
-        return pl.BlockSpec((per, 1, tokens, width), lambda i: (i, which, 0, 0))
-
-    return pl.pallas_call(
-        functools.partial(cross_kernel, steps=steps, per=per),
-        grid=(steps,),
+    total = chips * CORES * tokens
+    return pl.pallas_call(
+        cross_kernel,
+        grid=(chips // per,),
         in_specs=[
             pl.BlockSpec(memory_space=pltpu.SMEM),
+            pl.BlockSpec(memory_space=pltpu.SMEM),
             pl.BlockSpec((1, captions), lambda i: (0, 0)),
-            rows(0),
-            rows(1),
+            pl.BlockSpec((per, 2 * CORES, tokens, width), lambda i: (i, 0, 0, 0)),
             pl.BlockSpec((captions, width), lambda i: (0, 0)),
             pl.BlockSpec((captions, width), lambda i: (0, 1)),
         ],
         out_specs=[
-            pl.BlockSpec((per, 2, tokens, width), lambda i: (i, 0, 0, 0)),
+            pl.BlockSpec((CORES * per, 2, tokens, width), lambda i: (i, 0, 0, 0)),
             pl.BlockSpec((captions, 2 * width), lambda i: (0, 0)),
         ],
         out_shape=[
-            jax.ShapeDtypeStruct(x.shape, jnp.bfloat16),
+            jax.ShapeDtypeStruct((CORES * chips, 2, tokens, width), jnp.bfloat16),
             jax.ShapeDtypeStruct(kv.shape, jnp.bfloat16),
         ],
         scratch_shapes=[pltpu.VMEM((heads, HD, captions), jnp.float32)] * 2,
-        compiler_params=pltpu.CompilerParams(vmem_limit_bytes=VMEM),
-        cost_estimate=pl.CostEstimate(
-            flops=24 * heads * total * captions * HD,
-            bytes_accessed=4 * x.size + 4 * kv.size,
+        compiler_params=pltpu.CompilerParams(vmem_limit_bytes=MIDDLE),
+        cost_estimate=pl.CostEstimate(
+            flops=CROSS_COST,
+            bytes_accessed=8 * total * width + 4 * kv.size,
             transcendentals=heads * total * captions,
         ),
         name="cross_attention",
-    )(lengths, positions.reshape(1, captions), x, x, kv, kv)
+    )(core, lengths, positions.reshape(1, captions), x, kv, kv)
 
 
 def pack_kernel(s_ref, c_ref, x_ref):
@@ -213,6 +220,44 @@
     )(streams, cotangents)
 
 
+def pack_cores_kernel(core_ref, s_ref, c_ref, keep_ref, give_ref):
+    width = keep_ref.shape[3]
+    for core in range(CORES):
+        cols = slice(core * width, (core + 1) * width)
+
+        @pl.when(core_ref[0] == core)
+        def _():
+            keep_ref[0, 0] = s_ref[0, 0, :, cols]
+            keep_ref[0, 1] = c_ref[0, 0, :, cols]
+
+        @pl.when(core_ref[0] != core)
+        def _():
+            give_ref[0, 0] = s_ref[0, 0, :, cols]
+            give_ref[0, 1] = c_ref[0, 0, :, cols]
+
+
+def pack_cores(core, streams, cotangents, stream, cot, parts):
+    tokens, width = streams.shape[2], streams.shape[3] // parts
+    chips = parts // CORES
+    slab = pl.BlockSpec((1, 2, tokens, width), lambda j: (j, 0, 0, 0))
+    return pl.pallas_call(
+        pack_cores_kernel,
+        grid=(chips,),
+        in_specs=[
+            pl.BlockSpec(memory_space=pltpu.SMEM),
+            pl.BlockSpec((1, 1, tokens, CORES * width), lambda j: (stream, 0, 0, j)),
+            pl.BlockSpec((1, 1, tokens, CORES * width), lambda j: (cot, 0, 0, j)),
+        ],
+        out_specs=[slab, slab],
+        out_shape=[jax.ShapeDtypeStruct((chips, 2, tokens, width), jnp.bfloat16)] * 2,
+        compiler_params=pltpu.CompilerParams(vmem_limit_bytes=VMEM),
+        cost_estimate=pl.CostEstimate(
+            flops=0, bytes_accessed=8 * tokens * width * parts, transcendentals=0
+        ),
+        name="pack_cores",
+    )(core, streams, cotangents)
+
+
 def unpack_self_kernel(x_ref, ctx_ref, grads_ref):
     width = x_ref.shape[3]
     for part in range(x_ref.shape[0]):
@@ -237,7 +282,7 @@
             jax.ShapeDtypeStruct((4, 1, tokens, parts * width), jnp.bfloat16),
         ],
         cost_estimate=pl.CostEstimate(flops=0, bytes_accessed=4 * x.size, transcendentals=0),
-        compiler_params=pltpu.CompilerParams(vmem_limit_bytes=VMEM),
+        compiler_params=pltpu.CompilerParams(vmem_limit_bytes=SMALL),
         name="unpack_self",
     )(x)
 
@@ -270,7 +315,7 @@
         ],
         input_output_aliases={1: 1},
         cost_estimate=pl.CostEstimate(flops=0, bytes_accessed=4 * x.size, transcendentals=0),
-        compiler_params=pltpu.CompilerParams(vmem_limit_bytes=VMEM),
+        compiler_params=pltpu.CompilerParams(vmem_limit_bytes=SMALL),
         name="unpack_cross",
     )(x, grads)
 
@@ -312,95 +357,154 @@
     )(own, context.reshape(owned * rows, depth), weight, residual.reshape(owned * rows, depth))
 
 
+def join_kernel(own_ref, other_ref, y_ref):
+    y_ref[:, :2] = own_ref[...]
+    y_ref[:, 2:] = other_ref[...]
+
+
+def join_cores(own, other, blocks):
+    chips, count, tokens, width = own.shape
+    per = 2
+    slab = pl.BlockSpec((per, count, tokens, width), lambda j: (j, 0, 0, 0))
+    return pl.pallas_call(
+        join_kernel,
+        grid=(chips // per,),
+        in_specs=[slab, slab],
+        out_specs=pl.BlockSpec((per, 2 * count, tokens, width), lambda j: (j, 0, 0, 0)),
+        out_shape=jax.ShapeDtypeStruct((chips, 2 * count + blocks, tokens, width), jnp.bfloat16),
+        compiler_params=pltpu.CompilerParams(vmem_limit_bytes=SMALL),
+        name="join_cores",
+    )(own, other)
+
+
 def norm_kernel(*refs):
-    terms, gain_ref, y_ref = refs[:-2], refs[-2], refs[-1]
-    hidden = sum(term[...] for term in terms)
-    power = jnp.mean(hidden * hidden, axis=1, keepdims=True)
-    y = (hidden * lax.rsqrt(power + 1e-06) * gain_ref[...]).astype(jnp.bfloat16)
-    for copy in range(y_ref.shape[0]):
-        y_ref[copy] = y
-
-
-def norm(terms, gain, copies):
+    terms, (gain_ref, _, y_ref, states) = refs[:-4], refs[-4:]
+    blocks, rows, width = states.shape
+
+    @pl.when(pl.program_id(0) == 0)
+    def _():
+        hidden = sum(term[...] for term in terms)
+        power = jnp.mean(hidden * hidden, axis=1, keepdims=True)
+        normed = (hidden * lax.rsqrt(power + 1e-06) * gain_ref[...]).astype(jnp.bfloat16)
+        held = terms[0].shape[0]
+        per = rows // held
+        for at in range(blocks * per):
+            to = pl.ds(at % per * held, held)
+            states[at // per, to] = normed[:, at * width : (at + 1) * width]
+
+    for chip in range(y_ref.shape[0]):
+        y_ref[chip] = states[...]
+
+
+def norm_into(terms, gain, packed, blocks):
+    chips, total, tokens, width = packed.shape
+    rows, depth = terms[0].shape
+    per = 2
     return pl.pallas_call(
         norm_kernel,
-        out_shape=jax.ShapeDtypeStruct((copies,) + terms[0].shape, jnp.bfloat16),
-        name="norm",
-    )(*terms, gain.reshape(1, -1))
-
-
-def caption_kernel(near_ref, far_ref, w_ref, kv_ref, acc):
+        grid=(chips // per,),
+        in_specs=[pl.BlockSpec((rows, depth), lambda j: (0, 0))] * len(terms)
+        + [pl.BlockSpec((1, depth), lambda j: (0, 0)), pl.BlockSpec(memory_space=pl.ANY)],
+        out_specs=pl.BlockSpec(
+            (per, blocks, tokens, width), lambda j: (j, total // blocks - 1, 0, 0)
+        ),
+        out_shape=jax.ShapeDtypeStruct(packed.shape, jnp.bfloat16),
+        scratch_shapes=[pltpu.VMEM((blocks, tokens, width), jnp.bfloat16)],
+        input_output_aliases={len(terms) + 1: 0},
+        compiler_params=pltpu.CompilerParams(vmem_limit_bytes=SMALL),
+        name="norm_into",
+    )(*terms, gain.reshape(1, -1), packed)
+
+
+def caption_kernel(near_ref, far_ref, w_ref, kv_ref, acc, *, held):
     step = pl.program_id(0)
-    half = near_ref.shape[0]
+    chips, _, rows, width = near_ref.shape
+    half = chips * held
     for at, ref in ((0, near_ref), (half, far_ref)):
-        terms = mm(ref[...], w_ref[...], NN)
-        rows = slice(at, at + half)
+        terms = sum(
+            mm(
+                ref[:, 0, block * held : (block + 1) * held].reshape(half, width),
+                w_ref[block * width : (block + 1) * width],
+                NN,
+            )
+            for block in range(rows // held)
+        )
+        to = slice(at, at + half)
 
         @pl.when(step == 0)
         def _():
-            acc[rows] = terms
+            acc[to] = terms
 
         @pl.when(step > 0)
         def _():
-            acc[rows] += terms
+            acc[to] += terms
 
     @pl.when(step == pl.num_programs(0) - 1)
     def _():
         kv_ref[...] = acc[...].astype(jnp.bfloat16)
 
 
-def caption_projection(near, far, weight):
-    half, depth = near.shape
-    rows, width = 2 * half, weight.shape[1]
-    block = 512
-    return pl.pallas_call(
-        caption_kernel,
-        grid=(depth // block,),
+def caption_projection(near, skip, far, weight, held):
+    chips, blocks, rows, columns = far.shape
+    blocks -= skip
+    captions, width = CORES * chips * held, weight.shape[1]
+    depth = columns * rows // held
+    return pl.pallas_call(
+        functools.partial(caption_kernel, held=held),
+        grid=(blocks,),
         in_specs=[
-            pl.BlockSpec((half, block), lambda j: (0, j)),
-            pl.BlockSpec((half, block), lambda j: (0, j)),
-            pl.BlockSpec((block, width), lambda j: (j, 0)),
-        ],
-        out_specs=pl.BlockSpec((rows, width), lambda j: (0, 0)),
-        out_shape=jax.ShapeDtypeStruct((rows, width), jnp.bfloat16),
-        scratch_shapes=[pltpu.VMEM((rows, width), jnp.float32)],
-        compiler_params=pltpu.CompilerParams(vmem_limit_bytes=VMEM),
-        cost_estimate=pl.CostEstimate(
-            flops=2 * rows * depth * width,
-            bytes_accessed=2 * rows * depth + 2 * depth * width,
+            pl.BlockSpec((chips, 1, rows, columns), lambda j: (0, skip + j, 0, 0)),
+            pl.BlockSpec((chips, 1, rows, columns), lambda j: (0, skip + j, 0, 0)),
+            pl.BlockSpec((depth, width), lambda j: (j, 0)),
+        ],
+        out_specs=pl.BlockSpec((captions, width), lambda j: (0, 0)),
+        out_shape=jax.ShapeDtypeStruct((captions, width), jnp.bfloat16),
+        scratch_shapes=[pltpu.VMEM((captions, width), jnp.float32)],
+        compiler_params=pltpu.CompilerParams(vmem_limit_bytes=MIDDLE),
+        cost_estimate=pl.CostEstimate(
+            flops=2 * captions * blocks * depth * width,
+            bytes_accessed=4 * far.size + 2 * weight.size,
             transcendentals=0,
         ),
         name="caption_projection",
     )(near, far, weight)
 
 
-def split_kernel(own_ref, x_ref, *outs):
-    block = x_ref.shape[1] // len(outs)
+def split_kernel(own_ref, x_ref, *outs, held):
+    chips, blocks, rows, columns = x_ref.shape
+    per = rows // held
+    count = blocks * per // len(outs)
     for clip in range(len(outs)):
         for offset, out in enumerate(outs):
 
             @pl.when(lax.rem(own_ref[0] + offset, len(outs)) == clip)
             def _():
-                out[...] = x_ref[:, clip * block : (clip + 1) * block]
-
-
-def split_features(rows, groups, clips):
-    count, depth = rows.shape
+                for at in range(count):
+                    block, place = divmod(clip * count + at, per)
+                    piece = x_ref[:, block, place * held : (place + 1) * held]
+                    out[:, at * columns : (at + 1) * columns] = piece.reshape(-1, columns)
+
+
+def split_features(x, skip, groups, clips, held):
+    chips, blocks, rows, columns = x.shape
+    blocks = (blocks - skip) // groups
+    depth = blocks * columns * rows // held // clips
     own = lax.axis_index("tp").astype(jnp.int32).reshape(1)
     return pl.pallas_call(
-        split_kernel,
+        functools.partial(split_kernel, held=held),
         grid=(groups,),
         in_specs=[
             pl.BlockSpec(memory_space=pltpu.SMEM),
-            pl.BlockSpec((count, depth // groups), lambda d: (0, d)),
-        ],
-        out_specs=[pl.BlockSpec((count, depth // (groups * clips)), lambda d: (0, d))] * clips,
-        out_shape=[jax.ShapeDtypeStruct((count, depth // clips), rows.dtype)] * clips,
-        cost_estimate=pl.CostEstimate(
-            flops=0, bytes_accessed=4 * rows.size, transcendentals=0
+            pl.BlockSpec((chips, blocks, rows, columns), lambda d: (0, skip // blocks + d, 0, 0)),
+        ],
+        out_specs=[pl.BlockSpec((chips * held, depth), lambda d: (0, d))] * clips,
+        out_shape=[jax.ShapeDtypeStruct((chips * held, groups * depth), x.dtype)] * clips,
+        compiler_params=pltpu.CompilerParams(vmem_limit_bytes=SMALL),
+        cost_estimate=pl.CostEstimate(
+            flops=0, bytes_accessed=2 * x.size, transcendentals=0
         ),
         name="split_features",
-    )(own, rows)
+    )(own, x)
 
 
 def weight_kernel(own_ref, *refs, clips):
@@ -437,7 +541,7 @@
             jax.ShapeDtypeStruct((block, width), jnp.float32),
             jax.ShapeDtypeStruct((block, width), jnp.bfloat16),
         ],
-        compiler_params=pltpu.CompilerParams(vmem_limit_bytes=VMEM),
+        compiler_params=pltpu.CompilerParams(vmem_limit_bytes=MIDDLE),
         cost_estimate=pl.CostEstimate(
             flops=2 * clips * groups * rows * block * width,
             bytes_accessed=2 * clips * rows * (groups * block + width),
@@ -482,16 +586,12 @@
     ]
 
 
-CORES = 2
-
-
-def gather_captions(copies):
+def core_exchange(x):
     size = lax.axis_size("seq")
     groups = [list(range(core, size, CORES)) for core in range(CORES)]
-    rows = lax.all_to_all(
-        copies, "seq", split_axis=0, concat_axis=0, tiled=True, axis_index_groups=groups
-    )
-    return rows.reshape(-1, copies.shape[2])
+    return lax.all_to_all(
+        x, "seq", split_axis=0, concat_axis=0, tiled=True, axis_index_groups=groups
+    )
 
 
 def other_core(x):
@@ -520,37 +620,42 @@
     groups, clips = lax.axis_size("dp"), lax.axis_size("tp")
     local_width = kv_weight.shape[2]
 
+    held = enc_context.shape[1]
+    core = (lax.axis_index("seq") % CORES).astype(jnp.int32).reshape(1)
+
     self_packed = pack(streams, cotangents, 0, 3, 0, parts)
     self_in = seq_exchange(self_packed)
     streams, cotangents, enc_context, _ = lax.optimization_barrier(
         (streams, cotangents, enc_context, self_packed)
     )
     terms = tp_terms(project(enc_context, out_weight, enc_residual))
-    cross_packed = pack(streams, cotangents, 3, 1, 1, parts)
+    keep, give = pack_cores(core, streams, cotangents, 3, 1, parts)
+    blocks = terms[0].size // (keep.shape[2] * keep.shape[3])
+    packed = join_cores(keep, other_core(give), blocks)
     kv_flat = kv_weight.reshape(kv_weight.shape[0], 2 * local_width)
-    terms, kv_flat, cross_packed, _ = lax.optimization_barrier(
-        (terms, kv_flat, cross_packed, self_in)
-    )
-    near = gather_captions(norm(terms, norm_gain, parts // CORES))
+    packed, kv_flat, _ = lax.optimization_barrier(
+        (norm_into(terms, norm_gain, packed, blocks), kv_flat, self_in)
+    )
+    mixed = core_exchange(packed)
     self_out = None
     for head in range(local_width // HD):
         self_out = self_attention(self_in, head, self_out)
 
-    near, cross_packed, _ = lax.optimization_barrier((near, cross_packed, self_out))
-    cross_in = seq_exchange(cross_packed)
-    far = other_core(near)
-    near_terms = tp_terms(split_features(near, groups, clips))
-    caption_kv = caption_projection(near, far, kv_flat)
-
-    self_out, _, _, near_terms = lax.optimization_barrier(
-        (self_out, cross_in, caption_kv, near_terms)
-    )
+    self_out, mixed = lax.optimization_barrier((self_out, mixed))
     self_back = seq_exchange(self_out)
+    skip = 2 * CORES
+    near_terms = tp_terms(split_features(mixed, skip, groups, clips, held))
+    far = other_core(mixed)
+    caption_kv = caption_projection(mixed, skip, far, kv_flat, held)
+    cross_out, caption_grads = cross_attention(
+        core, caption_lengths, caption_order(held), mixed, caption_kv
+    )
+    near_terms[1], near_terms[3], caption_grads = lax.optimization_barrier(
+        (near_terms[1], near_terms[3], caption_grads)
+    )
+    grads = tp_terms([caption_grads] * clips)
+    near_terms, _ = lax.optimization_barrier((near_terms, grads[1]))
     far_terms = [other_core(x) for x in near_terms]
-    order = caption_order(enc_context.shape[1])
-    cross_out, caption_grads = cross_attention(caption_lengths, order, cross_in, caption_kv)
-    caption_grads, far_terms = lax.optimization_barrier((caption_grads, far_terms))
-    grads = tp_terms([caption_grads] * clips)
     kept, sent = weight_terms(near_terms, far_terms, grads, groups)
 
     cross_out, _, _ = lax.optimization_barrier((cross_out, self_back, sent))

time: 258 us -> 246 us (0.953)
  Pallas kernels: 97.1 us -> 85.9 us
  waiting for transfers between devices: 95.6 us -> 84.4 us
  starting transfers between devices: 49.1 us -> 55.5 us
  local copies, waits for them, and re-layouts: 13.1 us -> 16.9 us
    ppermute x9, waiting for transfers between devices: 52.7 us -> 29.9 us  [tp_terms(): lax.ppermute(terms[offset], 'tp', shifts(size, offset))]
    all_to_all x1, waiting for transfers between devices: 0.01 us -> 22.2 us  [core_exchange(): lax.all_to_all(x, 'seq', split_axis=0, concat_axis=0, tiled=True, axis_in...]
    ppermute x5 -> x6, starting transfers between devices: 1.87 us -> 14.2 us  [other_core(): lax.ppermute(x, 'seq', [(source, source ^ 1) for source in range(size)])]
    all_to_all x4 -> x3, waiting for transfers between devices: 43 us -> 30.7 us  [seq_exchange(): return lax.all_to_all(x, 'seq', split_axis=0, concat_axis=0, tiled=True)]
    all_to_all x4 -> x3, starting transfers between devices: 24.8 us -> 19.2 us  [seq_exchange(): return lax.all_to_all(x, 'seq', split_axis=0, concat_axis=0, tiled=True)]
    unnamed x33 -> x23, local copies, waits for them, and re-layouts: 9.56 us -> 13.9 us
    pallas_call x2 -> x1, Pallas kernels: 8.45 us -> 4.68 us  [pack(): pl.pallas_call(pack_kernel, grid=(parts // per,), in_specs=[pl.BlockSpec(...]
    pallas_call x4 -> x6, Pallas kernels: 25.9 us -> 23.7 us  [the longest x1 9.51 us: cross_attention(): pl.pallas_call(cross_kernel, grid=(chips // per,), in_specs=[pl.BlockSpec...]
  transfers between devices with their start and end apart: 20 -> 20, of which waited for: 10 -> 8; matrix products, arithmetic and copies ran while one was open for 3% -> 3% of each run, Pallas kernels for 33% -> 32%
where the time goes in v3:
time: 246 us; the launch traced here: 244 us
  Pallas kernels  85.9 us (35%)
  waiting for transfers between devices  84.4 us (34%)
  starting transfers between devices  55.5 us (23%)
  local copies, waits for them, and re-layouts  16.9 us (7%)
    pallas_call x2, Pallas kernels, self_attention(): pl.pallas_call(functools.partial(self_kernel, steps=steps, per=per), grid...  34.3 us
    all_to_all x3, waiting for transfers between devices, seq_exchange(): return lax.all_to_all(x, 'seq', split_axis=0, concat_axis=0, tiled=True)  30.7 us
    ppermute x9, waiting for transfers between devices, tp_terms(): lax.ppermute(terms[offset], 'tp', shifts(size, offset))  29.9 us
    all_to_all x1, waiting for transfers between devices, core_exchange(): lax.all_to_all(x, 'seq', split_axis=0, concat_axis=0, tiled=True, axis_in...  22.2 us
    all_to_all x3, starting transfers between devices, seq_exchange(): return lax.all_to_all(x, 'seq', split_axis=0, concat_axis=0, tiled=True)  19.2 us
    ppermute x6, starting transfers between devices, other_core(): lax.ppermute(x, 'seq', [(source, source ^ 1) for source in range(size)])  14.2 us
    ppermute x9, starting transfers between devices, tp_terms(): lax.ppermute(terms[offset], 'tp', shifts(size, offset))  14 us
    unnamed x23, local copies, waits for them, and re-layouts  13.9 us
  transfers between devices with their start and end apart: 20, of which 8 were waited for; matrix products, arithmetic and copies ran while one was open for 3% of the time, Pallas kernels for 32%

profile of v3, /device:TPU:9, one launch (start us, length us, event | category | flops | bytes accessed | tf_op | source)
XLA Modules:
  0.0 244.3 jit_solution(13809082365816320625)
XLA Ops:
  0.6 4.7 %pack.1 = bf16[16,4,128,256]{3,2,1,0:T(8,128)(2,1)} custom-call(bf16[4,1,128,4096]{3,2,1,0:T(8,128)(2,1)} %s_ref.2, bf16[2,1,128,4096]{3,2,1,0:T(8,128)(2,1)} %c_ref.2), custom_call_target="tpu_custom_call" | custom-call | bytes 8388608 | tf_op jit(solution)/shard_map/pack/pallas_call | solution.py:206
  5.3 6.1 %all-to-all-start = ((bf16[16,4,128,256]{3,2,1,0:T(8,128)(2,1)}), bf16[16,4,128,256]{3,2,1,0:T(8,128)(2,1)}, u32[]{:S(2)}, u32[]{:S(2)}) async-start(bf16[16,4,128,256]{3,2,1,0:T(8,128)(2,1)} %pack.1), calls=%async_computation | async-start | bytes 8388608 | tf_op jit(solution)/shard_map/all_to_all | solution.py:579
  11.4 5.8 %pack_cores.1 = (bf16[8,2,128,256]{3,2,1,0:T(8,128)(2,1)}, bf16[8,2,128,256]{3,2,1,0:T(8,128)(2,1)}) custom-call(s32[1]{0:T(128)} %bitcast.4.core_ref, bf16[4,1,128,4096]{3,2,1,0:T(8,128)(2,1)} %s_ref.2, bf16[2,1,128,4096]{3,2,1,0:T(8,128)(2,1)} %c_ref.2), custom_call_target="tpu_custom_call" | custom-call | bytes 4194304 | tf_op jit(solution)/shard_map/pack_cores/pallas_call | solution.py:243
  17.5 8.2 %project.1 = (f32[32,4096]{1,0:T(8,128)}, f32[32,4096]{1,0:T(8,128)}, f32[32,4096]{1,0:T(8,128)}, f32[32,4096]{1,0:T(8,128)}) custom-call(s32[1]{0:T(128)} %bitcast.own_ref, bf16[128,1024]{1,0:T(8,128)(2,1)} %bitcast.11, bf16[1024,4096]{1,0:T(8,128)(2,1)} %w_ref.1, bf16[128,1024]{1,0:T(8,128)(2,1)} %bitcast.12), custom_call_target="tpu_custom_call" | custom-call | flops 1073741824 | bytes 8388608 | tf_op jit(solution)/shard_map/project/pallas_call | solution.py:339
  27.4 3.3 %collective-permute-start.1 = (f32[32,4096]{1,0:T(8,128)}, f32[32,4096]{1,0:T(8,128)S(1)}, u32[]{:S(2)}, u32[]{:S(2)}) collective-permute-start(f32[32,4096]{1,0:T(8,128)} %get-tuple-element.41), channel_id=1, source_target_pairs={{0,2},{1,3},{2,0},{3,1},{4,6},{5,7},{6,4},{7,5},{8,10},{9,11},{10,... | collective-permute-start | bytes 1572872 | tf_op jit(solution)/shard_map/ppermute | solution.py:585
  31.4 5.0 %copy.15 = bf16[512,8,2,256]{3,1,2,0:T(8,128)(2,1)} copy(bf16[512,8,2,256]{3,2,1,0:T(2,128)(2,1)} %bitcast.10) | data formatting | bytes 8388608
  36.9 5.2 %collective-permute-done.refs_1_ = f32[32,4096]{1,0:T(8,128)S(1)} collective-permute-done((f32[32,4096]{1,0:T(8,128)}, f32[32,4096]{1,0:T(8,128)S(1)}, u32[]{:S(2)}, u32[]{:S(2)}) %collective-permute-start) | collective-permute-done | bytes 524320 | tf_op jit(solution)/shard_map/ppermute | solution.py:585
  42.1 12.1 %collective-permute-done.1.refs_2_ = f32[32,4096]{1,0:T(8,128)S(1)} collective-permute-done((f32[32,4096]{1,0:T(8,128)}, f32[32,4096]{1,0:T(8,128)S(1)}, u32[]{:S(2)}, u32[]{:S(2)}) %collective-permute-start.1) | collective-permute-done | bytes 524320 | tf_op jit(solution)/shard_map/ppermute | solution.py:585
  54.8 1.9 copy-done
  56.7 12.3 %all-to-all-done.q_ref.k_ref.v_ref.g_ref = bf16[16,4,128,256]{3,2,1,0:T(8,128)(2,1)} async-done(((bf16[16,4,128,256]{3,2,1,0:T(8,128)(2,1)}), bf16[16,4,128,256]{3,2,1,0:T(8,128)(2,1)}, u32[]{:S(2)}, u32[]{:S(2)}) %all-to-all-start) | async-done | bytes 4194336 | tf_op jit(solution)/shard_map/all_to_all | solution.py:579
  69.1 6.1 %all-to-all-start.1 = ((bf16[8,8,128,256]{3,2,1,0:T(8,128)(2,1)}), bf16[8,8,128,256]{3,2,1,0:T(8,128)(2,1)}, u32[]{:S(2)}, u32[]{:S(2)}) async-start(bf16[8,8,128,256]{3,2,1,0:T(8,128)(2,1)} %copy-done), calls=%async_computation.1 | async-start | bytes 8388608 | tf_op jit(solution)/shard_map/all_to_all | solution.py:592
  75.1 17.1 %self_attention.2.rest_0_ = bf16[16,4,128,256]{3,2,1,0:T(8,128)(2,1)S(1)} custom-call(bf16[16,4,128,256]{3,2,1,0:T(8,128)(2,1)} %all-to-all-done.q_ref.k_ref.v_ref.g_ref, bf16[16,4,128,256]{3,2,1,0:T(8,128)(2,1)} %all-to-all-done.q_ref.k_ref.v_ref.g_ref, bf16[16,4,128,256]{3,2,1,0:T(8,128)(2,1)} %all-to-all-done.q_ref.k_ref.v_ref.g_ref, ...), custom_call_target="tpu_custom_call" | custom-call | flops 12884901888 | bytes 4194304 | tf_op jit(solution)/shard_map/self_attention/pallas_call | solution.py:98
  92.3 17.1 %self_attention.3 = bf16[16,4,128,256]{3,2,1,0:T(8,128)(2,1)S(1)} custom-call(bf16[16,4,128,256]{3,2,1,0:T(8,128)(2,1)} %all-to-all-done.q_ref.k_ref.v_ref.g_ref, bf16[16,4,128,256]{3,2,1,0:T(8,128)(2,1)} %all-to-all-done.q_ref.k_ref.v_ref.g_ref, bf16[16,4,128,256]{3,2,1,0:T(8,128)(2,1)} %all-to-all-done.q_ref.k_ref.v_ref.g_ref, ...), custom_call_target="tpu_custom_call", output_to_operand_aliasing={{}: (4, {})} | custom-call | flops 12884901888 | bytes 4194304 | tf_op jit(solution)/shard_map/self_attention/pallas_call | solution.py:98
  109.4 2.0 copy-done.2
  111.4 22.2 %all-to-all-done.1.near_ref.x_ref = bf16[8,8,128,256]{3,2,1,0:T(8,128)(2,1)} async-done(((bf16[8,8,128,256]{3,2,1,0:T(8,128)(2,1)}), bf16[8,8,128,256]{3,2,1,0:T(8,128)(2,1)}, u32[]{:S(2)}, u32[]{:S(2)}) %all-to-all-start.1) | async-done | bytes 4194336 | tf_op jit(solution)/shard_map/all_to_all | solution.py:592
  135.0 5.0 %all-to-all-start.2 = ((bf16[16,4,128,256]{3,2,1,0:T(8,128)(2,1)}), bf16[16,4,128,256]{3,2,1,0:T(8,128)(2,1)}, u32[]{:S(2)}, u32[]{:S(2)}) async-start(bf16[16,4,128,256]{3,2,1,0:T(8,128)(2,1)} %copy-done.2), calls=%async_computation.2 | async-start | bytes 8388608 | tf_op jit(solution)/shard_map/all_to_all | solution.py:579
  140.8 2.0 split_features.1
  144.5 2.2 collective-permute-start.6
  148.0 5.4 %caption_projection.1.k_ref.v_ref = bf16[512,512]{1,0:T(8,128)(2,1)S(1)} custom-call(bf16[8,8,128,256]{3,2,1,0:T(8,128)(2,1)} %all-to-all-done.1.near_ref.x_ref, bf16[8,8,128,256]{3,2,1,0:T(8,128)(2,1)} %collective-permute-done.4.far_ref, bf16[4096,512]{1,0:T(8,128)(2,1)S(1)} %bitcast.8), custom_call_target="tpu_custom_call" | custom-call | flops 2147483648 | bytes 12582912 | tf_op jit(solution)/shard_map/caption_projection/pallas_call | solution.py:452
  153.4 9.5 %cross_attention.1 = (bf16[16,2,128,256]{3,2,1,0:T(8,128)(2,1)S(1)}, bf16[512,512]{1,0:T(8,128)(2,1)S(1)}) custom-call(s32[1]{0:T(128)} %bitcast.4.core_ref, s32[1]{0:T(128)S(6)} %copy.19.len_ref, s32[1,512]{1,0:T(1,128)S(1)} %add.52.pos_ref, bf16[8,8,128,256]{3,2,1,0:T(8,128)(2,1)} %all-to-all-done.1.near_ref.x_ref, ...), custom_call_target="tpu_custom_call" | custom-call | flops 6000000000 | bytes 5242880 | tf_op jit(solution)/shard_map/cross_attention/pallas_call | solution.py:165
  165.0 1.9 collective-permute-start.14
  167.5 3.4 %collective-permute-done.7.refs_2_ = bf16[256,1024]{1,0:T(8,128)(2,1)S(1)} collective-permute-done((bf16[256,1024]{1,0:T(8,128)(2,1)S(1)}, bf16[256,1024]{1,0:T(8,128)(2,1)S(1)}, u32[]{:S(2)}, u32[]{:S(2)}) %collective-permute-start.7) | collective-permute-done | bytes 524320 | tf_op jit(solution)/shard_map/ppermute | solution.py:585
  170.9 9.2 %collective-permute-done.8.refs_9_ = bf16[512,512]{1,0:T(8,128)(2,1)S(1)} collective-permute-done((bf16[512,512]{1,0:T(8,128)(2,1)S(1)}, bf16[512,512]{1,0:T(8,128)(2,1)S(1)}, u32[]{:S(2)}, u32[]{:S(2)}) %collective-permute-start.8) | collective-permute-done | bytes 524320 | tf_op jit(solution)/shard_map/ppermute | solution.py:585
  180.1 8.6 %collective-permute-start.9 = (bf16[256,1024]{1,0:T(8,128)(2,1)S(1)}, bf16[256,1024]{1,0:T(8,128)(2,1)}, u32[]{:S(2)}, u32[]{:S(2)}) collective-permute-start(bf16[256,1024]{1,0:T(8,128)(2,1)S(1)} %get-tuple-element.61.refs_0_), channel_id=1, source_target_pairs={{0,4},{4,0},{8,12},{12,8},{16,20},{20,16},{24,28},{28,24},{32,36},... | collective-permute-start | bytes 1572872 | tf_op jit(solution)/shard_map/ppermute | solution.py:599
  190.0 3.4 %collective-permute-start.12 = (bf16[256,1024]{1,0:T(8,128)(2,1)S(1)}, bf16[256,1024]{1,0:T(8,128)(2,1)}, u32[]{:S(2)}, u32[]{:S(2)}) collective-permute-start(bf16[256,1024]{1,0:T(8,128)(2,1)S(1)} %collective-permute-done.6.refs_3_), channel_id=1, source_target_pairs={{0,4},{4,0},{8,12},{12,8},{16,20},{20,16},{24,28},{28,24},{32,36},... | collective-permute-start | bytes 1572872 | tf_op jit(solution)/shard_map/ppermute | solution.py:599
  196.1 4.9 %weight_terms.1 = (f32[512,512]{1,0:T(8,128)S(1)}, bf16[512,512]{1,0:T(8,128)(2,1)}) custom-call(s32[1]{0:T(128)} %bitcast.5.own_ref, bf16[256,1024]{1,0:T(8,128)(2,1)S(1)} %get-tuple-element.61.refs_0_, bf16[256,1024]{1,0:T(8,128)(2,1)S(1)} %collective-permute-done.5.refs_1_, bf16[256,1024]{1,0:T(8,128)(2,1)S(1)} %collective-permute-done.7.refs_2_, ...), custom_call_target="tpu_custom_call" | custom-call | flops 2147483648 | bytes 6291456 | tf_op jit(solution)/shard_map/weight_terms/pallas_call | solution.py:533
  202.0 2.0 collective-permute-start.15
  204.0 8.1 %all-to-all-start.3 = ((bf16[16,2,128,256]{3,2,1,0:T(8,128)(2,1)}), bf16[16,2,128,256]{3,2,1,0:T(8,128)(2,1)S(1)}, u32[]{:S(2)}, u32[]{:S(2)}) async-start(bf16[16,2,128,256]{3,2,1,0:T(8,128)(2,1)} %copy-done.3), calls=%async_computation.3 | async-start | bytes 4194304 | tf_op jit(solution)/shard_map/all_to_all | solution.py:579
  212.1 4.9 %unpack_self.1 = (bf16[1,128,4096]{2,1,0:T(8,128)(2,1)}, bf16[4,1,128,4096]{3,2,1,0:T(8,128)(2,1)}) custom-call(bf16[16,4,128,256]{3,2,1,0:T(8,128)(2,1)} %all-to-all-done.2.x_ref), custom_call_target="tpu_custom_call" | custom-call | bytes 8388608 | tf_op jit(solution)/shard_map/unpack_self/pallas_call | solution.py:272
  217.8 3.4 %add_taken.1 = f32[512,512]{1,0:T(8,128)} custom-call(f32[512,512]{1,0:T(8,128)} %copy-done.9, bf16[512,512]{1,0:T(8,128)(2,1)} %copy-done.10), custom_call_target="tpu_custom_call" | custom-call | flops 20000000000 | bytes 2621440 | tf_op jit(solution)/shard_map/add_taken/pallas_call | solution.py:561
  221.2 2.8 %reshape.76 = f32[512,2,256]{2,1,0:T(2,128)} reshape(f32[512,512]{1,0:T(8,128)} %add_taken.1) | data formatting | bytes 2097152 | tf_op jit(solution)/shard_map/reshape | solution.py:667
  224.1 18.3 %all-to-all-done.3.x_ref = bf16[16,2,128,256]{3,2,1,0:T(8,128)(2,1)S(1)} async-done(((bf16[16,2,128,256]{3,2,1,0:T(8,128)(2,1)}), bf16[16,2,128,256]{3,2,1,0:T(8,128)(2,1)S(1)}, u32[]{:S(2)}, u32[]{:S(2)}) %all-to-all-start.3) | async-done | bytes 2097184 | tf_op jit(solution)/shard_map/all_to_all | solution.py:579
  (50 shorter events, 18.5 us)
Async XLA Ops:
  5.3 63.8 %all-to-all-start = ((bf16[16,4,128,256]{3,2,1,0:T(8,128)(2,1)}), bf16[16,4,128,256]{3,2,1,0:T(8,128)(2,1)}, u32[]{:S(2)}, u32[]{:S(2)}) async-start(bf16[16,4,128,256]{3,2,1,0:T(8,128)(2,1)} %pack.1), calls=%async_computation | async-start | bytes 8388608 | tf_op jit(solution)/shard_map/all_to_all | solution.py:579
  17.2 19.3 %collective-permute-start.3 = (bf16[8,2,128,256]{3,2,1,0:T(8,128)(2,1)}, bf16[8,2,128,256]{3,2,1,0:T(8,128)(2,1)S(1)}, u32[]{:S(2)}, u32[]{:S(2)}) collective-permute-start(bf16[8,2,128,256]{3,2,1,0:T(8,128)(2,1)} %get-tuple-element.46), channel_id=1, source_target_pairs={{0,4},{4,0},{8,12},{12,8},{16,20},{20,16},{24,28},{28,24},{32,36},... | collective-permute-start | bytes 3145736 | tf_op jit(solution)/shard_map/ppermute | solution.py:599
  25.7 16.3 %collective-permute-start = (f32[32,4096]{1,0:T(8,128)}, f32[32,4096]{1,0:T(8,128)S(1)}, u32[]{:S(2)}, u32[]{:S(2)}) collective-permute-start(f32[32,4096]{1,0:T(8,128)} %get-tuple-element.40), channel_id=1, source_target_pairs={{0,1},{1,2},{2,3},{3,0},{4,5},{5,6},{6,7},{7,4},{8,9},{9,10},{10,1... | collective-permute-start | bytes 1572872 | tf_op jit(solution)/shard_map/ppermute | solution.py:585
  27.4 26.8 %collective-permute-start.1 = (f32[32,4096]{1,0:T(8,128)}, f32[32,4096]{1,0:T(8,128)S(1)}, u32[]{:S(2)}, u32[]{:S(2)}) collective-permute-start(f32[32,4096]{1,0:T(8,128)} %get-tuple-element.41), channel_id=1, source_target_pairs={{0,2},{1,3},{2,0},{3,1},{4,6},{5,7},{6,4},{7,5},{8,10},{9,11},{10,... | collective-permute-start | bytes 1572872 | tf_op jit(solution)/shard_map/ppermute | solution.py:585
  30.7 23.4 %collective-permute-start.2 = (f32[32,4096]{1,0:T(8,128)}, f32[32,4096]{1,0:T(8,128)S(1)}, u32[]{:S(2)}, u32[]{:S(2)}) collective-permute-start(f32[32,4096]{1,0:T(8,128)} %get-tuple-element.42), channel_id=1, source_target_pairs={{0,3},{1,0},{2,1},{3,2},{4,7},{5,4},{6,5},{7,6},{8,11},{9,8},{10,9... | collective-permute-start | bytes 1572872 | tf_op jit(solution)/shard_map/ppermute | solution.py:585
  31.4 5.1 %copy-start.4 = (bf16[8,2,128,256]{3,2,1,0:T(8,128)(2,1)S(1)}, bf16[8,2,128,256]{3,2,1,0:T(8,128)(2,1)}, u32[]{:S(2)}) copy-start(bf16[8,2,128,256]{3,2,1,0:T(8,128)(2,1)} %get-tuple-element.45.own_ref) | copy-start | bytes 3145732
  36.5 17.7 %copy-start.5 = (f32[32,4096]{1,0:T(8,128)S(1)}, f32[32,4096]{1,0:T(8,128)}, u32[]{:S(2)}) copy-start(f32[32,4096]{1,0:T(8,128)} %get-tuple-element.39.refs_0_) | copy-start | bytes 1572868
  36.5 17.7 %copy-start.6 = (f32[4096]{0:T(1024)S(1)}, f32[4096]{0:T(1024)}, u32[]{:S(2)}) copy-start(f32[4096]{0:T(1024)} %param.11) | copy-start | bytes 49156
  54.8 1.9 copy-start
  69.1 64.6 %all-to-all-start.1 = ((bf16[8,8,128,256]{3,2,1,0:T(8,128)(2,1)}), bf16[8,8,128,256]{3,2,1,0:T(8,128)(2,1)}, u32[]{:S(2)}, u32[]{:S(2)}) async-start(bf16[8,8,128,256]{3,2,1,0:T(8,128)(2,1)} %copy-done), calls=%async_computation.1 | async-start | bytes 8388608 | tf_op jit(solution)/shard_map/all_to_all | solution.py:592
  109.4 2.0 copy-start.2
  133.6 14.3 %collective-permute-start.4 = (bf16[8,8,128,256]{3,2,1,0:T(8,128)(2,1)}, bf16[8,8,128,256]{3,2,1,0:T(8,128)(2,1)}, u32[]{:S(2)}, u32[]{:S(2)}) collective-permute-start(bf16[8,8,128,256]{3,2,1,0:T(8,128)(2,1)} %all-to-all-done.1.near_ref.x_ref), channel_id=1, source_target_pairs={{0,4},{4,0},{8,12},{12,8},{16,20},{20,16},{24,28},{28,24},{32,36},... | collective-permute-start | bytes 12582920 | tf_op jit(solution)/shard_map/ppermute | solution.py:599
  135.0 69.1 %all-to-all-start.2 = ((bf16[16,4,128,256]{3,2,1,0:T(8,128)(2,1)}), bf16[16,4,128,256]{3,2,1,0:T(8,128)(2,1)}, u32[]{:S(2)}, u32[]{:S(2)}) async-start(bf16[16,4,128,256]{3,2,1,0:T(8,128)(2,1)} %copy-done.2), calls=%async_computation.2 | async-start | bytes 8388608 | tf_op jit(solution)/shard_map/all_to_all | solution.py:579
  140.8 7.2 %copy-start.1 = (bf16[512,8,2,256]{3,1,2,0:T(8,128)(2,1)S(1)}, bf16[512,8,2,256]{3,1,2,0:T(8,128)(2,1)}, u32[]{:S(2)}) copy-start(bf16[512,8,2,256]{3,1,2,0:T(8,128)(2,1)} %copy.15) | copy-start | bytes 12582916
  142.8 21.4 %collective-permute-start.5 = (bf16[256,1024]{1,0:T(8,128)(2,1)S(1)}, bf16[256,1024]{1,0:T(8,128)(2,1)S(1)}, u32[]{:S(2)}, u32[]{:S(2)}) collective-permute-start(bf16[256,1024]{1,0:T(8,128)(2,1)S(1)} %get-tuple-element.54), channel_id=1, source_target_pairs={{0,1},{1,2},{2,3},{3,0},{4,5},{5,6},{6,7},{7,4},{8,9},{9,10},{10,1... | collective-permute-start | bytes 1572872 | tf_op jit(solution)/shard_map/ppermute | solution.py:585
  144.5 19.8 %collective-permute-start.6 = (bf16[256,1024]{1,0:T(8,128)(2,1)S(1)}, bf16[256,1024]{1,0:T(8,128)(2,1)S(1)}, u32[]{:S(2)}, u32[]{:S(2)}) collective-permute-start(bf16[256,1024]{1,0:T(8,128)(2,1)S(1)} %get-tuple-element.55), channel_id=1, source_target_pairs={{0,3},{1,0},{2,1},{3,2},{4,7},{5,4},{6,5},{7,6},{8,11},{9,8},{10,9... | collective-permute-start | bytes 1572872 | tf_op jit(solution)/shard_map/ppermute | solution.py:585
  146.7 24.2 %collective-permute-start.7 = (bf16[256,1024]{1,0:T(8,128)(2,1)S(1)}, bf16[256,1024]{1,0:T(8,128)(2,1)S(1)}, u32[]{:S(2)}, u32[]{:S(2)}) collective-permute-start(bf16[256,1024]{1,0:T(8,128)(2,1)S(1)} %get-tuple-element.58), channel_id=1, source_target_pairs={{0,2},{1,3},{2,0},{3,1},{4,6},{5,7},{6,4},{7,5},{8,10},{9,11},{10,... | collective-permute-start | bytes 1572872 | tf_op jit(solution)/shard_map/ppermute | solution.py:585
  162.9 1.4 copy-start.3
  164.3 15.8 %collective-permute-start.8 = (bf16[512,512]{1,0:T(8,128)(2,1)S(1)}, bf16[512,512]{1,0:T(8,128)(2,1)S(1)}, u32[]{:S(2)}, u32[]{:S(2)}) collective-permute-start(bf16[512,512]{1,0:T(8,128)(2,1)S(1)} %get-tuple-element.60.refs_8_), channel_id=1, source_target_pairs={{0,1},{1,2},{2,3},{3,0},{4,5},{5,6},{6,7},{7,4},{8,9},{9,10},{10,1... | collective-permute-start | bytes 1572872 | tf_op jit(solution)/shard_map/ppermute | solution.py:585
  165.0 24.2 %collective-permute-start.14 = (bf16[512,512]{1,0:T(8,128)(2,1)S(1)}, bf16[512,512]{1,0:T(8,128)(2,1)S(1)}, u32[]{:S(2)}, u32[]{:S(2)}) collective-permute-start(bf16[512,512]{1,0:T(8,128)(2,1)S(1)} %get-tuple-element.60.refs_8_), channel_id=1, source_target_pairs={{0,3},{1,0},{2,1},{3,2},{4,7},{5,4},{6,5},{7,6},{8,11},{9,8},{10,9... | collective-permute-start | bytes 1572872 | tf_op jit(solution)/shard_map/ppermute | solution.py:585
  167.0 26.4 %collective-permute-start.13 = (bf16[512,512]{1,0:T(8,128)(2,1)S(1)}, bf16[512,512]{1,0:T(8,128)(2,1)}, u32[]{:S(2)}, u32[]{:S(2)}) collective-permute-start(bf16[512,512]{1,0:T(8,128)(2,1)S(1)} %get-tuple-element.60.refs_8_), channel_id=1, source_target_pairs={{0,2},{1,3},{2,0},{3,1},{4,6},{5,7},{6,4},{7,5},{8,10},{9,11},{10,... | collective-permute-start | bytes 1572872 | tf_op jit(solution)/shard_map/ppermute | solution.py:585
  180.1 13.3 %collective-permute-start.9 = (bf16[256,1024]{1,0:T(8,128)(2,1)S(1)}, bf16[256,1024]{1,0:T(8,128)(2,1)}, u32[]{:S(2)}, u32[]{:S(2)}) collective-permute-start(bf16[256,1024]{1,0:T(8,128)(2,1)S(1)} %get-tuple-element.61.refs_0_), channel_id=1, source_target_pairs={{0,4},{4,0},{8,12},{12,8},{16,20},{20,16},{24,28},{28,24},{32,36},... | collective-permute-start | bytes 1572872 | tf_op jit(solution)/shard_map/ppermute | solution.py:599
  188.7 4.7 %collective-permute-start.10 = (bf16[256,1024]{1,0:T(8,128)(2,1)S(1)}, bf16[256,1024]{1,0:T(8,128)(2,1)}, u32[]{:S(2)}, u32[]{:S(2)}) collective-permute-start(bf16[256,1024]{1,0:T(8,128)(2,1)S(1)} %collective-permute-done.5.refs_1_), channel_id=1, source_target_pairs={{0,4},{4,0},{8,12},{12,8},{16,20},{20,16},{24,28},{28,24},{32,36},... | collective-permute-start | bytes 1572872 | tf_op jit(solution)/shard_map/ppermute | solution.py:599
  188.7 4.7 %collective-permute-start.11 = (bf16[256,1024]{1,0:T(8,128)(2,1)S(1)}, bf16[256,1024]{1,0:T(8,128)(2,1)}, u32[]{:S(2)}, u32[]{:S(2)}) collective-permute-start(bf16[256,1024]{1,0:T(8,128)(2,1)S(1)} %collective-permute-done.7.refs_2_), channel_id=1, source_target_pairs={{0,4},{4,0},{8,12},{12,8},{16,20},{20,16},{24,28},{28,24},{32,36},... | collective-permute-start | bytes 1572872 | tf_op jit(solution)/shard_map/ppermute | solution.py:599
  189.2 0.8 copy-start.7
  190.0 5.1 %collective-permute-start.12 = (bf16[256,1024]{1,0:T(8,128)(2,1)S(1)}, bf16[256,1024]{1,0:T(8,128)(2,1)}, u32[]{:S(2)}, u32[]{:S(2)}) collective-permute-start(bf16[256,1024]{1,0:T(8,128)(2,1)S(1)} %collective-permute-done.6.refs_3_), channel_id=1, source_target_pairs={{0,4},{4,0},{8,12},{12,8},{16,20},{20,16},{24,28},{28,24},{32,36},... | collective-permute-start | bytes 1572872 | tf_op jit(solution)/shard_map/ppermute | solution.py:599
  195.1 1.0 copy-start.8
  201.0 1.0 copy-start.9
  202.0 15.0 %collective-permute-start.15 = (bf16[512,512]{1,0:T(8,128)(2,1)}, bf16[512,512]{1,0:T(8,128)(2,1)S(1)}, u32[]{:S(2)}, u32[]{:S(2)}) collective-permute-start(bf16[512,512]{1,0:T(8,128)(2,1)} %get-tuple-element.65), channel_id=1, source_target_pairs={{0,64},{64,0},{1,65},{65,1},{2,66},{66,2},{3,67},{67,3},{4,68},{68... | collective-permute-start | bytes 1572872 | tf_op jit(solution)/shard_map/ppermute | solution.py:664
  204.0 38.4 %all-to-all-start.3 = ((bf16[16,2,128,256]{3,2,1,0:T(8,128)(2,1)}), bf16[16,2,128,256]{3,2,1,0:T(8,128)(2,1)S(1)}, u32[]{:S(2)}, u32[]{:S(2)}) async-start(bf16[16,2,128,256]{3,2,1,0:T(8,128)(2,1)} %copy-done.3), calls=%async_computation.3 | async-start | bytes 4194304 | tf_op jit(solution)/shard_map/all_to_all | solution.py:579
  217.0 0.8 copy-start.10

commit v4 on v3

--- a/solution.py
+++ b/solution.py
@@ -192,30 +192,43 @@
     )(core, lengths, positions.reshape(1, captions), x, kv, kv)
 
 
-def pack_kernel(s_ref, c_ref, x_ref):
-    count, width = s_ref.shape[0], x_ref.shape[3]
-    for part in range(x_ref.shape[0]):
-        cols = slice(part * width, (part + 1) * width)
-        x_ref[part, :count] = s_ref[:, 0, :, cols]
-        x_ref[part, count:] = c_ref[:, 0, :, cols]
-
-
-def pack(streams, cotangents, first, count, cot, parts):
+def pack_kernel(s_ref, c_ref, x_ref, held, in_sems, out_sems):
+    parts, count, _, width = x_ref.shape
+    fetches, stores = [], []
+    for which in range(count):
+        given = s_ref.at[which, 0] if which < count - 1 else c_ref.at[0, 0]
+        fetches.append(pltpu.make_async_copy(given, held.at[which], in_sems.at[which]))
+        fetches[-1].start()
+    for which in range(count):
+        fetches[which].wait()
+        for part in range(parts):
+            cols = pl.ds(part * width, width)
+            stores.append(
+                pltpu.make_async_copy(
+                    held.at[which, :, cols], x_ref.at[part, which], out_sems.at[part, which]
+                )
+            )
+            stores[-1].start()
+    for store in stores:
+        store.wait()
+
+
+def pack(streams, cotangents, count, parts):
     tokens, width = streams.shape[2], streams.shape[3] // parts
-    per = 4
     return pl.pallas_call(
         pack_kernel,
-        grid=(parts // per,),
-        in_specs=[
-            pl.BlockSpec((count, 1, tokens, per * width), lambda j: (first // count, 0, 0, j)),
-            pl.BlockSpec((1, 1, tokens, per * width), lambda j: (cot, 0, 0, j)),
-        ],
-        out_specs=pl.BlockSpec((per, count + 1, tokens, width), lambda j: (j, 0, 0, 0)),
+        in_specs=[pl.BlockSpec(memory_space=pl.ANY)] * 2,
+        out_specs=pl.BlockSpec(memory_space=pl.ANY),
         out_shape=jax.ShapeDtypeStruct((parts, count + 1, tokens, width), jnp.bfloat16),
+        scratch_shapes=[
+            pltpu.VMEM((count + 1, tokens, parts * width), jnp.bfloat16),
+            pltpu.SemaphoreType.DMA((count + 1,)),
+            pltpu.SemaphoreType.DMA((parts, count + 1)),
+        ],
+        compiler_params=pltpu.CompilerParams(vmem_limit_bytes=VMEM),
         cost_estimate=pl.CostEstimate(
             flops=0, bytes_accessed=4 * (count + 1) * tokens * width * parts, transcendentals=0
         ),
-        compiler_params=pltpu.CompilerParams(vmem_limit_bytes=VMEM),
         name="pack",
     )(streams, cotangents)
 
@@ -552,18 +565,23 @@
 
 
 def add_kernel(kept_ref, taken_ref, y_ref):
-    y_ref[...] = kept_ref[...] + taken_ref[...].astype(jnp.float32)
-
-
-def add_taken(kept, taken):
+    width = y_ref.shape[2]
+    for at in range(y_ref.shape[1]):
+        cols = slice(at * width, (at + 1) * width)
+        y_ref[:, at] = kept_ref[:, cols] + taken_ref[:, cols].astype(jnp.float32)
+
+
+def add_taken(kept, taken, parts):
     rows, width = kept.shape
-    block = pl.BlockSpec((rows // 4, width), lambda j: (j, 0))
+    steps = 4
+    block = pl.BlockSpec((rows // steps, width), lambda j: (j, 0))
     return pl.pallas_call(
         add_kernel,
-        grid=(4,),
+        grid=(steps,),
         in_specs=[block, block],
-        out_specs=block,
-        out_shape=jax.ShapeDtypeStruct(kept.shape, jnp.float32),
+        out_specs=pl.BlockSpec((rows // steps, parts, width // parts), lambda j: (j, 0, 0)),
+        out_shape=jax.ShapeDtypeStruct((rows, parts, width // parts), jnp.float32),
+        compiler_params=pltpu.CompilerParams(vmem_limit_bytes=SMALL),
         cost_estimate=pl.CostEstimate(
             flops=ADD_COST, bytes_accessed=10 * kept.size, transcendentals=0
         ),
@@ -623,7 +641,7 @@
     held = enc_context.shape[1]
     core = (lax.axis_index("seq") % CORES).astype(jnp.int32).reshape(1)
 
-    self_packed = pack(streams, cotangents, 0, 3, 0, parts)
+    self_packed = pack(streams, cotangents, 3, parts)
     self_in = seq_exchange(self_packed)
     streams, cotangents, enc_context, _ = lax.optimization_barrier(
         (streams, cotangents, enc_context, self_packed)
@@ -650,9 +668,7 @@
     cross_out, caption_grads = cross_attention(
         core, caption_lengths, caption_order(held), mixed, caption_kv
     )
-    near_terms[1], near_terms[3], caption_grads = lax.optimization_barrier(
-        (near_terms[1], near_terms[3], caption_grads)
-    )
+    near_terms[1], caption_grads = lax.optimization_barrier((near_terms[1], caption_grads))
     grads = tp_terms([caption_grads] * clips)
     near_terms, _ = lax.optimization_barrier((near_terms, grads[1]))
     far_terms = [other_core(x) for x in near_terms]
@@ -663,8 +679,7 @@
     self_ctx, stream_grads = unpack_self(self_back)
     taken = lax.ppermute(sent, "dp", shifts(groups, 1))
     kept, _ = lax.optimization_barrier((kept, self_ctx))
-    grad = add_taken(kept, taken)
-    weight_grad = grad.reshape(grad.shape[0], 2, local_width)
+    weight_grad = add_taken(kept, taken, 2)
     cross_ctx, stream_grads = unpack_cross(cross_back, stream_grads)
     return (self_ctx, cross_ctx, stream_grads, weight_grad)
 

time: 246 us -> 242 us (0.984)
  waiting for transfers between devices: 84.4 us -> 96.4 us
  starting transfers between devices: 55.5 us -> 44.3 us
  local copies, waits for them, and re-layouts: 16.9 us -> 13.2 us
  Pallas kernels: 85.9 us -> 83.4 us
    ppermute x6, starting transfers between devices: 14.2 us -> 2.78 us  [other_core(): lax.ppermute(x, 'seq', [(source, source ^ 1) for source in range(size)])]
    ppermute x9, waiting for transfers between devices: 29.9 us -> 39.8 us  [tp_terms(): lax.ppermute(terms[offset], 'tp', shifts(size, offset))]
    all_to_all x3, waiting for transfers between devices: 30.7 us -> 34.5 us  [seq_exchange(): return lax.all_to_all(x, 'seq', split_axis=0, concat_axis=0, tiled=True)]
    reshape x1 -> x0, local copies, waits for them, and re-layouts: 2.85 us -> none  [body(): weight_grad = grad.reshape(grad.shape[0], 2, local_width)]
    pallas_call x2, Pallas kernels: 8.12 us -> 5.51 us  [the longest x1 3.79 us: pack(): pl.pallas_call(pack_kernel, in_specs=[pl.BlockSpec(memory_space=pl.ANY)]...]
  transfers between devices with their start and end apart: 20 -> 20, of which waited for: 8 -> 8; matrix products, arithmetic and copies ran while one was open for 3% -> 2% of each run, Pallas kernels for 32% -> 33%
where the time goes in v4:
time: 242 us; the launch traced here: 239 us
  waiting for transfers between devices  96.4 us (40%)
  Pallas kernels  83.4 us (34%)
  starting transfers between devices  44.3 us (18%)
  local copies, waits for them, and re-layouts  13.2 us (5%)
    ppermute x9, waiting for transfers between devices, tp_terms(): lax.ppermute(terms[offset], 'tp', shifts(size, offset))  39.8 us
    all_to_all x3, waiting for transfers between devices, seq_exchange(): return lax.all_to_all(x, 'seq', split_axis=0, concat_axis=0, tiled=True)  34.5 us
    pallas_call x2, Pallas kernels, self_attention(): pl.pallas_call(functools.partial(self_kernel, steps=steps, per=per), grid...  34.3 us
    all_to_all x1, waiting for transfers between devices, core_exchange(): lax.all_to_all(x, 'seq', split_axis=0, concat_axis=0, tiled=True, axis_in...  22.2 us
    all_to_all x3, starting transfers between devices, seq_exchange(): return lax.all_to_all(x, 'seq', split_axis=0, concat_axis=0, tiled=True)  19.3 us
    ppermute x9, starting transfers between devices, tp_terms(): lax.ppermute(terms[offset], 'tp', shifts(size, offset))  14.1 us
    unnamed x23, local copies, waits for them, and re-layouts  13.2 us
    pallas_call x1, Pallas kernels, cross_attention(): pl.pallas_call(cross_kernel, grid=(chips // per,), in_specs=[pl.BlockSpec...  9.51 us
  transfers between devices with their start and end apart: 20, of which 8 were waited for; matrix products, arithmetic and copies ran while one was open for 2% of the time, Pallas kernels for 33%

profile of v4, /device:TPU:9, one launch (start us, length us, event | category | flops | bytes accessed | tf_op | source)
XLA Modules:
  0.0 239.0 jit_solution(2024804792936351247)
XLA Ops:
  0.6 3.8 %pack.1 = bf16[16,4,128,256]{3,2,1,0:T(8,128)(2,1)} custom-call(bf16[4,1,128,4096]{3,2,1,0:T(8,128)(2,1)} %s_ref.2, bf16[2,1,128,4096]{3,2,1,0:T(8,128)(2,1)} %c_ref.2), custom_call_target="tpu_custom_call" | custom-call | bytes 8388608 | tf_op jit(solution)/shard_map/pack/pallas_call | solution.py:218
  4.4 6.1 %all-to-all-start = ((bf16[16,4,128,256]{3,2,1,0:T(8,128)(2,1)}), bf16[16,4,128,256]{3,2,1,0:T(8,128)(2,1)}, u32[]{:S(2)}, u32[]{:S(2)}) async-start(bf16[16,4,128,256]{3,2,1,0:T(8,128)(2,1)} %pack.1), calls=%async_computation | async-start | bytes 8388608 | tf_op jit(solution)/shard_map/all_to_all | solution.py:597
  10.5 5.8 %pack_cores.1 = (bf16[8,2,128,256]{3,2,1,0:T(8,128)(2,1)}, bf16[8,2,128,256]{3,2,1,0:T(8,128)(2,1)}) custom-call(s32[1]{0:T(128)} %bitcast.4.core_ref, bf16[4,1,128,4096]{3,2,1,0:T(8,128)(2,1)} %s_ref.2, bf16[2,1,128,4096]{3,2,1,0:T(8,128)(2,1)} %c_ref.2), custom_call_target="tpu_custom_call" | custom-call | bytes 4194304 | tf_op jit(solution)/shard_map/pack_cores/pallas_call | solution.py:256
  16.6 8.2 %project.1 = (f32[32,4096]{1,0:T(8,128)}, f32[32,4096]{1,0:T(8,128)}, f32[32,4096]{1,0:T(8,128)}, f32[32,4096]{1,0:T(8,128)}) custom-call(s32[1]{0:T(128)} %bitcast.own_ref, bf16[128,1024]{1,0:T(8,128)(2,1)} %bitcast.11, bf16[1024,4096]{1,0:T(8,128)(2,1)} %w_ref.1, bf16[128,1024]{1,0:T(8,128)(2,1)} %bitcast.12), custom_call_target="tpu_custom_call" | custom-call | flops 1073741824 | bytes 8388608 | tf_op jit(solution)/shard_map/project/pallas_call | solution.py:352
  24.9 1.7 collective-permute-start
  26.5 3.3 %collective-permute-start.1 = (f32[32,4096]{1,0:T(8,128)}, f32[32,4096]{1,0:T(8,128)S(1)}, u32[]{:S(2)}, u32[]{:S(2)}) collective-permute-start(f32[32,4096]{1,0:T(8,128)} %get-tuple-element.40), channel_id=1, source_target_pairs={{0,2},{1,3},{2,0},{3,1},{4,6},{5,7},{6,4},{7,5},{8,10},{9,11},{10,... | collective-permute-start | bytes 1572872 | tf_op jit(solution)/shard_map/ppermute | solution.py:603
  30.6 5.0 %copy.15 = bf16[512,8,2,256]{3,1,2,0:T(8,128)(2,1)} copy(bf16[512,8,2,256]{3,2,1,0:T(2,128)(2,1)} %bitcast.10) | data formatting | bytes 8388608
  36.0 5.2 %collective-permute-done.refs_1_ = f32[32,4096]{1,0:T(8,128)S(1)} collective-permute-done((f32[32,4096]{1,0:T(8,128)}, f32[32,4096]{1,0:T(8,128)S(1)}, u32[]{:S(2)}, u32[]{:S(2)}) %collective-permute-start) | collective-permute-done | bytes 524320 | tf_op jit(solution)/shard_map/ppermute | solution.py:603
  41.2 12.1 %collective-permute-done.1.refs_2_ = f32[32,4096]{1,0:T(8,128)S(1)} collective-permute-done((f32[32,4096]{1,0:T(8,128)}, f32[32,4096]{1,0:T(8,128)S(1)}, u32[]{:S(2)}, u32[]{:S(2)}) %collective-permute-start.1) | collective-permute-done | bytes 524320 | tf_op jit(solution)/shard_map/ppermute | solution.py:603
  53.9 1.9 copy-done
  55.8 12.4 %all-to-all-done.q_ref.k_ref.v_ref.g_ref = bf16[16,4,128,256]{3,2,1,0:T(8,128)(2,1)} async-done(((bf16[16,4,128,256]{3,2,1,0:T(8,128)(2,1)}), bf16[16,4,128,256]{3,2,1,0:T(8,128)(2,1)}, u32[]{:S(2)}, u32[]{:S(2)}) %all-to-all-start) | async-done | bytes 4194336 | tf_op jit(solution)/shard_map/all_to_all | solution.py:597
  68.2 6.1 %all-to-all-start.1 = ((bf16[8,8,128,256]{3,2,1,0:T(8,128)(2,1)}), bf16[8,8,128,256]{3,2,1,0:T(8,128)(2,1)}, u32[]{:S(2)}, u32[]{:S(2)}) async-start(bf16[8,8,128,256]{3,2,1,0:T(8,128)(2,1)} %copy-done), calls=%async_computation.1 | async-start | bytes 8388608 | tf_op jit(solution)/shard_map/all_to_all | solution.py:610
  74.3 17.1 %self_attention.2.rest_0_ = bf16[16,4,128,256]{3,2,1,0:T(8,128)(2,1)S(1)} custom-call(bf16[16,4,128,256]{3,2,1,0:T(8,128)(2,1)} %all-to-all-done.q_ref.k_ref.v_ref.g_ref, bf16[16,4,128,256]{3,2,1,0:T(8,128)(2,1)} %all-to-all-done.q_ref.k_ref.v_ref.g_ref, bf16[16,4,128,256]{3,2,1,0:T(8,128)(2,1)} %all-to-all-done.q_ref.k_ref.v_ref.g_ref, ...), custom_call_target="tpu_custom_call" | custom-call | flops 12884901888 | bytes 4194304 | tf_op jit(solution)/shard_map/self_attention/pallas_call | solution.py:98
  91.4 17.2 %self_attention.3 = bf16[16,4,128,256]{3,2,1,0:T(8,128)(2,1)S(1)} custom-call(bf16[16,4,128,256]{3,2,1,0:T(8,128)(2,1)} %all-to-all-done.q_ref.k_ref.v_ref.g_ref, bf16[16,4,128,256]{3,2,1,0:T(8,128)(2,1)} %all-to-all-done.q_ref.k_ref.v_ref.g_ref, bf16[16,4,128,256]{3,2,1,0:T(8,128)(2,1)} %all-to-all-done.q_ref.k_ref.v_ref.g_ref, ...), custom_call_target="tpu_custom_call", output_to_operand_aliasing={{}: (4, {})} | custom-call | flops 12884901888 | bytes 4194304 | tf_op jit(solution)/shard_map/self_attention/pallas_call | solution.py:98
  108.6 2.0 copy-done.2
  110.6 22.2 %all-to-all-done.1.near_ref.x_ref = bf16[8,8,128,256]{3,2,1,0:T(8,128)(2,1)} async-done(((bf16[8,8,128,256]{3,2,1,0:T(8,128)(2,1)}), bf16[8,8,128,256]{3,2,1,0:T(8,128)(2,1)}, u32[]{:S(2)}, u32[]{:S(2)}) %all-to-all-start.1) | async-done | bytes 4194336 | tf_op jit(solution)/shard_map/all_to_all | solution.py:610
  134.1 5.0 %all-to-all-start.2 = ((bf16[16,4,128,256]{3,2,1,0:T(8,128)(2,1)}), bf16[16,4,128,256]{3,2,1,0:T(8,128)(2,1)}, u32[]{:S(2)}, u32[]{:S(2)}) async-start(bf16[16,4,128,256]{3,2,1,0:T(8,128)(2,1)} %copy-done.2), calls=%async_computation.2 | async-start | bytes 8388608 | tf_op jit(solution)/shard_map/all_to_all | solution.py:597
  139.9 2.0 split_features.1
  143.6 3.3 %collective-permute-start.6 = (bf16[256,1024]{1,0:T(8,128)(2,1)S(1)}, bf16[256,1024]{1,0:T(8,128)(2,1)S(1)}, u32[]{:S(2)}, u32[]{:S(2)}) collective-permute-start(bf16[256,1024]{1,0:T(8,128)(2,1)S(1)} %get-tuple-element.56), channel_id=1, source_target_pairs={{0,2},{1,3},{2,0},{3,1},{4,6},{5,7},{6,4},{7,5},{8,10},{9,11},{10,... | collective-permute-start | bytes 1572872 | tf_op jit(solution)/shard_map/ppermute | solution.py:603
  147.7 5.4 %caption_projection.1.k_ref.v_ref = bf16[512,512]{1,0:T(8,128)(2,1)S(1)} custom-call(bf16[8,8,128,256]{3,2,1,0:T(8,128)(2,1)} %all-to-all-done.1.near_ref.x_ref, bf16[8,8,128,256]{3,2,1,0:T(8,128)(2,1)} %collective-permute-done.4.far_ref, bf16[4096,512]{1,0:T(8,128)(2,1)S(1)} %bitcast.8), custom_call_target="tpu_custom_call" | custom-call | flops 2147483648 | bytes 12582912 | tf_op jit(solution)/shard_map/caption_projection/pallas_call | solution.py:465
  153.1 9.5 %cross_attention.1 = (bf16[16,2,128,256]{3,2,1,0:T(8,128)(2,1)S(1)}, bf16[512,512]{1,0:T(8,128)(2,1)S(1)}) custom-call(s32[1]{0:T(128)} %bitcast.4.core_ref, s32[1]{0:T(128)S(6)} %copy.19.len_ref, s32[1,512]{1,0:T(1,128)S(1)} %add.52.pos_ref, bf16[8,8,128,256]{3,2,1,0:T(8,128)(2,1)} %all-to-all-done.1.near_ref.x_ref, ...), custom_call_target="tpu_custom_call" | custom-call | flops 6000000000 | bytes 5242880 | tf_op jit(solution)/shard_map/cross_attention/pallas_call | solution.py:165
  164.8 1.9 collective-permute-start.14
  166.7 3.3 %collective-permute-done.6.refs_2_ = bf16[256,1024]{1,0:T(8,128)(2,1)S(1)} collective-permute-done((bf16[256,1024]{1,0:T(8,128)(2,1)S(1)}, bf16[256,1024]{1,0:T(8,128)(2,1)S(1)}, u32[]{:S(2)}, u32[]{:S(2)}) %collective-permute-start.6) | collective-permute-done | bytes 524320 | tf_op jit(solution)/shard_map/ppermute | solution.py:603
  170.0 13.8 %collective-permute-done.8.refs_9_ = bf16[512,512]{1,0:T(8,128)(2,1)S(1)} collective-permute-done((bf16[512,512]{1,0:T(8,128)(2,1)S(1)}, bf16[512,512]{1,0:T(8,128)(2,1)S(1)}, u32[]{:S(2)}, u32[]{:S(2)}) %collective-permute-start.8) | collective-permute-done | bytes 524320 | tf_op jit(solution)/shard_map/ppermute | solution.py:603
  185.8 5.3 %collective-permute-done.13.refs_10_ = bf16[512,512]{1,0:T(8,128)(2,1)} collective-permute-done((bf16[512,512]{1,0:T(8,128)(2,1)S(1)}, bf16[512,512]{1,0:T(8,128)(2,1)}, u32[]{:S(2)}, u32[]{:S(2)}) %collective-permute-start.13) | collective-permute-done | bytes 524320 | tf_op jit(solution)/shard_map/ppermute | solution.py:603
  192.2 4.9 %weight_terms.1 = (f32[512,512]{1,0:T(8,128)S(1)}, bf16[512,512]{1,0:T(8,128)(2,1)}) custom-call(s32[1]{0:T(128)} %bitcast.5.own_ref, bf16[256,1024]{1,0:T(8,128)(2,1)S(1)} %get-tuple-element.59.refs_0_, bf16[256,1024]{1,0:T(8,128)(2,1)S(1)} %collective-permute-done.5.refs_1_, bf16[256,1024]{1,0:T(8,128)(2,1)S(1)} %collective-permute-done.6.refs_2_, ...), custom_call_target="tpu_custom_call" | custom-call | flops 2147483648 | bytes 6291456 | tf_op jit(solution)/shard_map/weight_terms/pallas_call | solution.py:546
  198.1 2.0 collective-permute-start.15
  200.1 8.3 %all-to-all-start.3 = ((bf16[16,2,128,256]{3,2,1,0:T(8,128)(2,1)}), bf16[16,2,128,256]{3,2,1,0:T(8,128)(2,1)S(1)}, u32[]{:S(2)}, u32[]{:S(2)}) async-start(bf16[16,2,128,256]{3,2,1,0:T(8,128)(2,1)} %copy-done.3), calls=%async_computation.3 | async-start | bytes 4194304 | tf_op jit(solution)/shard_map/all_to_all | solution.py:597
  208.4 4.9 %unpack_self.1 = (bf16[1,128,4096]{2,1,0:T(8,128)(2,1)}, bf16[4,1,128,4096]{3,2,1,0:T(8,128)(2,1)}) custom-call(bf16[16,4,128,256]{3,2,1,0:T(8,128)(2,1)} %all-to-all-done.2.x_ref), custom_call_target="tpu_custom_call" | custom-call | bytes 8388608 | tf_op jit(solution)/shard_map/unpack_self/pallas_call | solution.py:285
  213.3 1.7 add_taken.1
  215.0 22.1 %all-to-all-done.3.x_ref = bf16[16,2,128,256]{3,2,1,0:T(8,128)(2,1)S(1)} async-done(((bf16[16,2,128,256]{3,2,1,0:T(8,128)(2,1)}), bf16[16,2,128,256]{3,2,1,0:T(8,128)(2,1)S(1)}, u32[]{:S(2)}, u32[]{:S(2)}) %all-to-all-start.3) | async-done | bytes 2097184 | tf_op jit(solution)/shard_map/all_to_all | solution.py:597
  237.1 1.9 unpack_cross.1
  (49 shorter events, 12.1 us)
Async XLA Ops:
  4.4 63.8 %all-to-all-start = ((bf16[16,4,128,256]{3,2,1,0:T(8,128)(2,1)}), bf16[16,4,128,256]{3,2,1,0:T(8,128)(2,1)}, u32[]{:S(2)}, u32[]{:S(2)}) async-start(bf16[16,4,128,256]{3,2,1,0:T(8,128)(2,1)} %pack.1), calls=%async_computation | async-start | bytes 8388608 | tf_op jit(solution)/shard_map/all_to_all | solution.py:597
  16.3 19.3 %collective-permute-start.3 = (bf16[8,2,128,256]{3,2,1,0:T(8,128)(2,1)}, bf16[8,2,128,256]{3,2,1,0:T(8,128)(2,1)S(1)}, u32[]{:S(2)}, u32[]{:S(2)}) collective-permute-start(bf16[8,2,128,256]{3,2,1,0:T(8,128)(2,1)} %get-tuple-element.45), channel_id=1, source_target_pairs={{0,4},{4,0},{8,12},{12,8},{16,20},{20,16},{24,28},{28,24},{32,36},... | collective-permute-start | bytes 3145736 | tf_op jit(solution)/shard_map/ppermute | solution.py:617
  24.9 16.3 %collective-permute-start = (f32[32,4096]{1,0:T(8,128)}, f32[32,4096]{1,0:T(8,128)S(1)}, u32[]{:S(2)}, u32[]{:S(2)}) collective-permute-start(f32[32,4096]{1,0:T(8,128)} %get-tuple-element.39), channel_id=1, source_target_pairs={{0,1},{1,2},{2,3},{3,0},{4,5},{5,6},{6,7},{7,4},{8,9},{9,10},{10,1... | collective-permute-start | bytes 1572872 | tf_op jit(solution)/shard_map/ppermute | solution.py:603
  26.5 26.7 %collective-permute-start.1 = (f32[32,4096]{1,0:T(8,128)}, f32[32,4096]{1,0:T(8,128)S(1)}, u32[]{:S(2)}, u32[]{:S(2)}) collective-permute-start(f32[32,4096]{1,0:T(8,128)} %get-tuple-element.40), channel_id=1, source_target_pairs={{0,2},{1,3},{2,0},{3,1},{4,6},{5,7},{6,4},{7,5},{8,10},{9,11},{10,... | collective-permute-start | bytes 1572872 | tf_op jit(solution)/shard_map/ppermute | solution.py:603
  29.8 23.4 %collective-permute-start.2 = (f32[32,4096]{1,0:T(8,128)}, f32[32,4096]{1,0:T(8,128)S(1)}, u32[]{:S(2)}, u32[]{:S(2)}) collective-permute-start(f32[32,4096]{1,0:T(8,128)} %get-tuple-element.41), channel_id=1, source_target_pairs={{0,3},{1,0},{2,1},{3,2},{4,7},{5,4},{6,5},{7,6},{8,11},{9,8},{10,9... | collective-permute-start | bytes 1572872 | tf_op jit(solution)/shard_map/ppermute | solution.py:603
  30.6 5.1 %copy-start.4 = (bf16[8,2,128,256]{3,2,1,0:T(8,128)(2,1)S(1)}, bf16[8,2,128,256]{3,2,1,0:T(8,128)(2,1)}, u32[]{:S(2)}) copy-start(bf16[8,2,128,256]{3,2,1,0:T(8,128)(2,1)} %get-tuple-element.44.own_ref) | copy-start | bytes 3145732
  35.6 17.7 %copy-start.5 = (f32[32,4096]{1,0:T(8,128)S(1)}, f32[32,4096]{1,0:T(8,128)}, u32[]{:S(2)}) copy-start(f32[32,4096]{1,0:T(8,128)} %get-tuple-element.38.refs_0_) | copy-start | bytes 1572868
  35.6 17.7 %copy-start.6 = (f32[4096]{0:T(1024)S(1)}, f32[4096]{0:T(1024)}, u32[]{:S(2)}) copy-start(f32[4096]{0:T(1024)} %param.11) | copy-start | bytes 49156
  53.9 1.9 copy-start
  68.2 64.6 %all-to-all-start.1 = ((bf16[8,8,128,256]{3,2,1,0:T(8,128)(2,1)}), bf16[8,8,128,256]{3,2,1,0:T(8,128)(2,1)}, u32[]{:S(2)}, u32[]{:S(2)}) async-start(bf16[8,8,128,256]{3,2,1,0:T(8,128)(2,1)} %copy-done), calls=%async_computation.1 | async-start | bytes 8388608 | tf_op jit(solution)/shard_map/all_to_all | solution.py:610
  108.6 2.0 copy-start.2
  132.7 14.9 %collective-permute-start.4 = (bf16[8,8,128,256]{3,2,1,0:T(8,128)(2,1)}, bf16[8,8,128,256]{3,2,1,0:T(8,128)(2,1)}, u32[]{:S(2)}, u32[]{:S(2)}) collective-permute-start(bf16[8,8,128,256]{3,2,1,0:T(8,128)(2,1)} %all-to-all-done.1.near_ref.x_ref), channel_id=1, source_target_pairs={{0,4},{4,0},{8,12},{12,8},{16,20},{20,16},{24,28},{28,24},{32,36},... | collective-permute-start | bytes 12582920 | tf_op jit(solution)/shard_map/ppermute | solution.py:617
  134.1 66.0 %all-to-all-start.2 = ((bf16[16,4,128,256]{3,2,1,0:T(8,128)(2,1)}), bf16[16,4,128,256]{3,2,1,0:T(8,128)(2,1)}, u32[]{:S(2)}, u32[]{:S(2)}) async-start(bf16[16,4,128,256]{3,2,1,0:T(8,128)(2,1)} %copy-done.2), calls=%async_computation.2 | async-start | bytes 8388608 | tf_op jit(solution)/shard_map/all_to_all | solution.py:597
  139.9 7.8 %copy-start.1 = (bf16[512,8,2,256]{3,1,2,0:T(8,128)(2,1)S(1)}, bf16[512,8,2,256]{3,1,2,0:T(8,128)(2,1)}, u32[]{:S(2)}) copy-start(bf16[512,8,2,256]{3,1,2,0:T(8,128)(2,1)} %copy.15) | copy-start | bytes 12582916
  142.0 22.0 %collective-permute-start.5 = (bf16[256,1024]{1,0:T(8,128)(2,1)S(1)}, bf16[256,1024]{1,0:T(8,128)(2,1)S(1)}, u32[]{:S(2)}, u32[]{:S(2)}) collective-permute-start(bf16[256,1024]{1,0:T(8,128)(2,1)S(1)} %get-tuple-element.53), channel_id=1, source_target_pairs={{0,1},{1,2},{2,3},{3,0},{4,5},{5,6},{6,7},{7,4},{8,9},{9,10},{10,1... | collective-permute-start | bytes 1572872 | tf_op jit(solution)/shard_map/ppermute | solution.py:603
  143.6 26.4 %collective-permute-start.6 = (bf16[256,1024]{1,0:T(8,128)(2,1)S(1)}, bf16[256,1024]{1,0:T(8,128)(2,1)S(1)}, u32[]{:S(2)}, u32[]{:S(2)}) collective-permute-start(bf16[256,1024]{1,0:T(8,128)(2,1)S(1)} %get-tuple-element.56), channel_id=1, source_target_pairs={{0,2},{1,3},{2,0},{3,1},{4,6},{5,7},{6,4},{7,5},{8,10},{9,11},{10,... | collective-permute-start | bytes 1572872 | tf_op jit(solution)/shard_map/ppermute | solution.py:603
  147.0 23.1 %collective-permute-start.7 = (bf16[256,1024]{1,0:T(8,128)(2,1)S(1)}, bf16[256,1024]{1,0:T(8,128)(2,1)S(1)}, u32[]{:S(2)}, u32[]{:S(2)}) collective-permute-start(bf16[256,1024]{1,0:T(8,128)(2,1)S(1)} %get-tuple-element.57), channel_id=1, source_target_pairs={{0,3},{1,0},{2,1},{3,2},{4,7},{5,4},{6,5},{7,6},{8,11},{9,8},{10,9... | collective-permute-start | bytes 1572872 | tf_op jit(solution)/shard_map/ppermute | solution.py:603
  162.6 1.4 copy-start.3
  164.0 19.8 %collective-permute-start.8 = (bf16[512,512]{1,0:T(8,128)(2,1)S(1)}, bf16[512,512]{1,0:T(8,128)(2,1)S(1)}, u32[]{:S(2)}, u32[]{:S(2)}) collective-permute-start(bf16[512,512]{1,0:T(8,128)(2,1)S(1)} %get-tuple-element.58.refs_8_), channel_id=1, source_target_pairs={{0,1},{1,2},{2,3},{3,0},{4,5},{5,6},{6,7},{7,4},{8,9},{9,10},{10,1... | collective-permute-start | bytes 1572872 | tf_op jit(solution)/shard_map/ppermute | solution.py:603
  164.8 20.2 %collective-permute-start.14 = (bf16[512,512]{1,0:T(8,128)(2,1)S(1)}, bf16[512,512]{1,0:T(8,128)(2,1)S(1)}, u32[]{:S(2)}, u32[]{:S(2)}) collective-permute-start(bf16[512,512]{1,0:T(8,128)(2,1)S(1)} %get-tuple-element.58.refs_8_), channel_id=1, source_target_pairs={{0,3},{1,0},{2,1},{3,2},{4,7},{5,4},{6,5},{7,6},{8,11},{9,8},{10,9... | collective-permute-start | bytes 1572872 | tf_op jit(solution)/shard_map/ppermute | solution.py:603
  166.7 24.4 %collective-permute-start.13 = (bf16[512,512]{1,0:T(8,128)(2,1)S(1)}, bf16[512,512]{1,0:T(8,128)(2,1)}, u32[]{:S(2)}, u32[]{:S(2)}) collective-permute-start(bf16[512,512]{1,0:T(8,128)(2,1)S(1)} %get-tuple-element.58.refs_8_), channel_id=1, source_target_pairs={{0,2},{1,3},{2,0},{3,1},{4,6},{5,7},{6,4},{7,5},{8,10},{9,11},{10,... | collective-permute-start | bytes 1572872 | tf_op jit(solution)/shard_map/ppermute | solution.py:603
  183.9 7.3 %collective-permute-start.9 = (bf16[256,1024]{1,0:T(8,128)(2,1)S(1)}, bf16[256,1024]{1,0:T(8,128)(2,1)}, u32[]{:S(2)}, u32[]{:S(2)}) collective-permute-start(bf16[256,1024]{1,0:T(8,128)(2,1)S(1)} %get-tuple-element.59.refs_0_), channel_id=1, source_target_pairs={{0,4},{4,0},{8,12},{12,8},{16,20},{20,16},{24,28},{28,24},{32,36},... | collective-permute-start | bytes 1572872 | tf_op jit(solution)/shard_map/ppermute | solution.py:617
  184.5 6.7 %collective-permute-start.10 = (bf16[256,1024]{1,0:T(8,128)(2,1)S(1)}, bf16[256,1024]{1,0:T(8,128)(2,1)}, u32[]{:S(2)}, u32[]{:S(2)}) collective-permute-start(bf16[256,1024]{1,0:T(8,128)(2,1)S(1)} %collective-permute-done.5.refs_1_), channel_id=1, source_target_pairs={{0,4},{4,0},{8,12},{12,8},{16,20},{20,16},{24,28},{28,24},{32,36},... | collective-permute-start | bytes 1572872 | tf_op jit(solution)/shard_map/ppermute | solution.py:617
  184.5 6.7 %collective-permute-start.11 = (bf16[256,1024]{1,0:T(8,128)(2,1)S(1)}, bf16[256,1024]{1,0:T(8,128)(2,1)}, u32[]{:S(2)}, u32[]{:S(2)}) collective-permute-start(bf16[256,1024]{1,0:T(8,128)(2,1)S(1)} %collective-permute-done.6.refs_2_), channel_id=1, source_target_pairs={{0,4},{4,0},{8,12},{12,8},{16,20},{20,16},{24,28},{28,24},{32,36},... | collective-permute-start | bytes 1572872 | tf_op jit(solution)/shard_map/ppermute | solution.py:617
  185.0 0.8 copy-start.7
  185.8 5.4 %collective-permute-start.12 = (bf16[256,1024]{1,0:T(8,128)(2,1)S(1)}, bf16[256,1024]{1,0:T(8,128)(2,1)}, u32[]{:S(2)}, u32[]{:S(2)}) collective-permute-start(bf16[256,1024]{1,0:T(8,128)(2,1)S(1)} %collective-permute-done.7.refs_3_), channel_id=1, source_target_pairs={{0,4},{4,0},{8,12},{12,8},{16,20},{20,16},{24,28},{28,24},{32,36},... | collective-permute-start | bytes 1572872 | tf_op jit(solution)/shard_map/ppermute | solution.py:617
  191.1 1.0 copy-start.8
  197.1 1.0 copy-start.9
  198.1 15.2 %collective-permute-start.15 = (bf16[512,512]{1,0:T(8,128)(2,1)}, bf16[512,512]{1,0:T(8,128)(2,1)S(1)}, u32[]{:S(2)}, u32[]{:S(2)}) collective-permute-start(bf16[512,512]{1,0:T(8,128)(2,1)} %get-tuple-element.63), channel_id=1, source_target_pairs={{0,64},{64,0},{1,65},{65,1},{2,66},{66,2},{3,67},{67,3},{4,68},{68... | collective-permute-start | bytes 1572872 | tf_op jit(solution)/shard_map/ppermute | solution.py:680
  200.1 37.0 %all-to-all-start.3 = ((bf16[16,2,128,256]{3,2,1,0:T(8,128)(2,1)}), bf16[16,2,128,256]{3,2,1,0:T(8,128)(2,1)S(1)}, u32[]{:S(2)}, u32[]{:S(2)}) async-start(bf16[16,2,128,256]{3,2,1,0:T(8,128)(2,1)} %copy-done.3), calls=%async_computation.3 | async-start | bytes 4194304 | tf_op jit(solution)/shard_map/all_to_all | solution.py:597
  208.4 5.0 %copy-start.10 = (f32[512,512]{1,0:T(8,128)S(1)}, f32[512,512]{1,0:T(8,128)}, u32[]{:S(2)}) copy-start(f32[512,512]{1,0:T(8,128)} %copy-done.9) | copy-start | bytes 3145732

commit v5 on v4

--- a/solution.py
+++ b/solution.py
@@ -19,6 +19,13 @@
 ADD_COST = 2 * 10**10
 CROSS_COST = 6 * 10**9
 CORES = 2
+SELF_CHIPS = (0, 2, 5, 7, 1, 3, 4, 6)
+CROSS_CHIPS = (0, 4, 5, 1, 2, 6, 7, 3)
+
+
+def devices(chips):
+    return [CORES * chip + core for chip in chips for core in range(CORES)]
+
 
 NT = (((1,), (1,)), ((), ()))
 NN = (((1,), (0,)), ((), ()))
@@ -192,7 +199,7 @@
     )(core, lengths, positions.reshape(1, captions), x, kv, kv)
 
 
-def pack_kernel(s_ref, c_ref, x_ref, held, in_sems, out_sems):
+def pack_kernel(s_ref, c_ref, x_ref, held, in_sems, out_sems, *, order):
     parts, count, _, width = x_ref.shape
     fetches, stores = [], []
     for which in range(count):
@@ -202,7 +209,7 @@
     for which in range(count):
         fetches[which].wait()
         for part in range(parts):
-            cols = pl.ds(part * width, width)
+            cols = pl.ds(order[part] * width, width)
             stores.append(
                 pltpu.make_async_copy(
                     held.at[which, :, cols], x_ref.at[part, which], out_sems.at[part, which]
@@ -213,10 +220,11 @@
         store.wait()
 
 
-def pack(streams, cotangents, count, parts):
+def pack(streams, cotangents, count, order):
+    parts = len(order)
     tokens, width = streams.shape[2], streams.shape[3] // parts
     return pl.pallas_call(
-        pack_kernel,
+        functools.partial(pack_kernel, order=order),
         in_specs=[pl.BlockSpec(memory_space=pl.ANY)] * 2,
         out_specs=pl.BlockSpec(memory_space=pl.ANY),
         out_shape=jax.ShapeDtypeStruct((parts, count + 1, tokens, width), jnp.bfloat16),
@@ -233,102 +241,106 @@
     )(streams, cotangents)
 
 
-def pack_cores_kernel(core_ref, s_ref, c_ref, keep_ref, give_ref):
+def pack_cores_kernel(core_ref, s_ref, c_ref, keep_ref, give_ref, *, order):
     width = keep_ref.shape[3]
-    for core in range(CORES):
-        cols = slice(core * width, (core + 1) * width)
-
-        @pl.when(core_ref[0] == core)
-        def _():
-            keep_ref[0, 0] = s_ref[0, 0, :, cols]
-            keep_ref[0, 1] = c_ref[0, 0, :, cols]
-
-        @pl.when(core_ref[0] != core)
-        def _():
-            give_ref[0, 0] = s_ref[0, 0, :, cols]
-            give_ref[0, 1] = c_ref[0, 0, :, cols]
-
-
-def pack_cores(core, streams, cotangents, stream, cot, parts):
-    tokens, width = streams.shape[2], streams.shape[3] // parts
-    chips = parts // CORES
-    slab = pl.BlockSpec((1, 2, tokens, width), lambda j: (j, 0, 0, 0))
-    return pl.pallas_call(
-        pack_cores_kernel,
-        grid=(chips,),
+    for at, chip in enumerate(order):
+        for core in range(CORES):
+            place = CORES * chip + core
+            cols = slice(place * width, (place + 1) * width)
+
+            @pl.when(core_ref[0] == core)
+            def _():
+                keep_ref[at, 0] = s_ref[0, 0, :, cols]
+                keep_ref[at, 1] = c_ref[0, 0, :, cols]
+
+            @pl.when(core_ref[0] != core)
+            def _():
+                give_ref[at, 0] = s_ref[0, 0, :, cols]
+                give_ref[at, 1] = c_ref[0, 0, :, cols]
+
+
+def pack_cores(core, streams, cotangents, stream, cot, order):
+    chips = len(order)
+    tokens, columns = streams.shape[2:]
+    width = columns // (CORES * chips)
+    rows = 32
+    slab = pl.BlockSpec((chips, 2, rows, width), lambda j: (0, 0, j, 0))
+    return pl.pallas_call(
+        functools.partial(pack_cores_kernel, order=order),
+        grid=(tokens // rows,),
         in_specs=[
             pl.BlockSpec(memory_space=pltpu.SMEM),
-            pl.BlockSpec((1, 1, tokens, CORES * width), lambda j: (stream, 0, 0, j)),
-            pl.BlockSpec((1, 1, tokens, CORES * width), lambda j: (cot, 0, 0, j)),
+            pl.BlockSpec((1, 1, rows, columns), lambda j: (stream, 0, j, 0)),
+            pl.BlockSpec((1, 1, rows, columns), lambda j: (cot, 0, j, 0)),
         ],
         out_specs=[slab, slab],
         out_shape=[jax.ShapeDtypeStruct((chips, 2, tokens, width), jnp.bfloat16)] * 2,
         compiler_params=pltpu.CompilerParams(vmem_limit_bytes=VMEM),
         cost_estimate=pl.CostEstimate(
-            flops=0, bytes_accessed=8 * tokens * width * parts, transcendentals=0
+            flops=0, bytes_accessed=8 * tokens * columns, transcendentals=0
         ),
         name="pack_cores",
     )(core, streams, cotangents)
 
 
-def unpack_self_kernel(x_ref, ctx_ref, grads_ref):
+def unpack_self_kernel(x_ref, ctx_ref, grads_ref, *, order):
     width = x_ref.shape[3]
-    for part in range(x_ref.shape[0]):
-        cols = slice(part * width, (part + 1) * width)
-        ctx_ref[0, :, cols] = x_ref[part, 0]
-        grads_ref[:, 0, :, cols] = x_ref[part, 1:]
-
-
-def unpack_self(x):
+    for at, place in enumerate(order):
+        cols = slice(place * width, (place + 1) * width)
+        ctx_ref[0, :, cols] = x_ref[at, 0]
+        grads_ref[:, 0, :, cols] = x_ref[at, 1:]
+
+
+def unpack_self(x, order):
     parts, _, tokens, width = x.shape
-    per = 4
-    return pl.pallas_call(
-        unpack_self_kernel,
-        grid=(parts // per,),
-        in_specs=[pl.BlockSpec((per, 4, tokens, width), lambda j: (j, 0, 0, 0))],
+    rows = 32
+    return pl.pallas_call(
+        functools.partial(unpack_self_kernel, order=order),
+        grid=(tokens // rows,),
+        in_specs=[pl.BlockSpec((parts, 4, rows, width), lambda j: (0, 0, j, 0))],
         out_specs=[
-            pl.BlockSpec((1, tokens, per * width), lambda j: (0, 0, j)),
-            pl.BlockSpec((3, 1, tokens, per * width), lambda j: (0, 0, 0, j)),
+            pl.BlockSpec((1, rows, parts * width), lambda j: (0, j, 0)),
+            pl.BlockSpec((3, 1, rows, parts * width), lambda j: (0, 0, j, 0)),
         ],
         out_shape=[
             jax.ShapeDtypeStruct((1, tokens, parts * width), jnp.bfloat16),
             jax.ShapeDtypeStruct((4, 1, tokens, parts * width), jnp.bfloat16),
         ],
+        compiler_params=pltpu.CompilerParams(vmem_limit_bytes=SMALL),
         cost_estimate=pl.CostEstimate(flops=0, bytes_accessed=4 * x.size, transcendentals=0),
-        compiler_params=pltpu.CompilerParams(vmem_limit_bytes=SMALL),
         name="unpack_self",
     )(x)
 
 
-def unpack_cross_kernel(x_ref, _, ctx_ref, grads_ref):
+def unpack_cross_kernel(x_ref, _, ctx_ref, grads_ref, *, order):
     width = x_ref.shape[3]
-    for part in range(x_ref.shape[0]):
-        cols = slice(part * width, (part + 1) * width)
-        ctx_ref[0, :, cols] = x_ref[part, 0]
-        grads_ref[0, 0, :, cols] = x_ref[part, 1]
-
-
-def unpack_cross(x, grads):
+    for at, place in enumerate(order):
+        cols = slice(place * width, (place + 1) * width)
+        ctx_ref[0, :, cols] = x_ref[at, 0]
+        grads_ref[0, 0, :, cols] = x_ref[at, 1]
+
+
+def unpack_cross(x, grads, order):
     parts, _, tokens, width = x.shape
-    per = 4
-    return pl.pallas_call(
-        unpack_cross_kernel,
-        grid=(parts // per,),
+    rows = 32
+    return pl.pallas_call(
+        functools.partial(unpack_cross_kernel, order=order),
+        grid=(tokens // rows,),
         in_specs=[
-            pl.BlockSpec((per, 2, tokens, width), lambda j: (j, 0, 0, 0)),
+            pl.BlockSpec((parts, 2, rows, width), lambda j: (0, 0, j, 0)),
             pl.BlockSpec(memory_space=pl.ANY),
         ],
         out_specs=[
-            pl.BlockSpec((1, tokens, per * width), lambda j: (0, 0, j)),
-            pl.BlockSpec((1, 1, tokens, per * width), lambda j: (3, 0, 0, j)),
+            pl.BlockSpec((1, rows, parts * width), lambda j: (0, j, 0)),
+            pl.BlockSpec((1, 1, rows, parts * width), lambda j: (3, 0, j, 0)),
         ],
         out_shape=[
             jax.ShapeDtypeStruct((1, tokens, parts * width), jnp.bfloat16),
             jax.ShapeDtypeStruct(grads.shape, jnp.bfloat16),
         ],
         input_output_aliases={1: 1},
+        compiler_params=pltpu.CompilerParams(vmem_limit_bytes=SMALL),
         cost_estimate=pl.CostEstimate(flops=0, bytes_accessed=4 * x.size, transcendentals=0),
-        compiler_params=pltpu.CompilerParams(vmem_limit_bytes=SMALL),
         name="unpack_cross",
     )(x, grads)
 
@@ -593,8 +605,10 @@
     return [(at, (at + offset) % size) for at in range(size)]
 
 
-def seq_exchange(x):
-    return lax.all_to_all(x, "seq", split_axis=0, concat_axis=0, tiled=True)
+def seq_exchange(x, order):
+    return lax.all_to_all(
+        x, "seq", split_axis=0, concat_axis=0, tiled=True, axis_index_groups=[order]
+    )
 
 
 def tp_terms(terms):
@@ -605,8 +619,7 @@
 
 
 def core_exchange(x):
-    size = lax.axis_size("seq")
-    groups = [list(range(core, size, CORES)) for core in range(CORES)]
+    groups = [[CORES * chip + core for chip in CROSS_CHIPS] for core in range(CORES)]
     return lax.all_to_all(
         x, "seq", split_axis=0, concat_axis=0, tiled=True, axis_index_groups=groups
     )
@@ -618,8 +631,8 @@
 
 
 def caption_order(rows):
-    size, core = lax.axis_size("seq"), lax.axis_index("seq") % CORES
-    chips = jnp.arange(0, size, CORES, dtype=jnp.int32)
+    core = lax.axis_index("seq") % CORES
+    chips = CORES * jnp.asarray(CROSS_CHIPS, jnp.int32)
     places = jnp.concatenate([chips + core, chips + (1 - core)])
     return (places[:, None] * rows + jnp.arange(rows, dtype=jnp.int32)[None, :]).reshape(-1)
 
@@ -634,20 +647,19 @@
     streams,
     cotangents,
 ):
-    parts = lax.axis_size("seq")
     groups, clips = lax.axis_size("dp"), lax.axis_size("tp")
     local_width = kv_weight.shape[2]
 
     held = enc_context.shape[1]
     core = (lax.axis_index("seq") % CORES).astype(jnp.int32).reshape(1)
 
-    self_packed = pack(streams, cotangents, 3, parts)
-    self_in = seq_exchange(self_packed)
+    self_packed = pack(streams, cotangents, 3, devices(SELF_CHIPS))
+    self_in = seq_exchange(self_packed, devices(SELF_CHIPS))
     streams, cotangents, enc_context, _ = lax.optimization_barrier(
         (streams, cotangents, enc_context, self_packed)
     )
     terms = tp_terms(project(enc_context, out_weight, enc_residual))
-    keep, give = pack_cores(core, streams, cotangents, 3, 1, parts)
+    keep, give = pack_cores(core, streams, cotangents, 3, 1, CROSS_CHIPS)
     blocks = terms[0].size // (keep.shape[2] * keep.shape[3])
     packed = join_cores(keep, other_core(give), blocks)
     kv_flat = kv_weight.reshape(kv_weight.shape[0], 2 * local_width)
@@ -660,7 +672,7 @@
         self_out = self_attention(self_in, head, self_out)
 
     self_out, mixed = lax.optimization_barrier((self_out, mixed))
-    self_back = seq_exchange(self_out)
+    self_back = seq_exchange(self_out, devices(SELF_CHIPS))
     skip = 2 * CORES
     near_terms = tp_terms(split_features(mixed, skip, groups, clips, held))
     far = other_core(mixed)
@@ -675,12 +687,12 @@
     kept, sent = weight_terms(near_terms, far_terms, grads, groups)
 
     cross_out, _, _ = lax.optimization_barrier((cross_out, self_back, sent))
-    cross_back = seq_exchange(cross_out)
-    self_ctx, stream_grads = unpack_self(self_back)
+    cross_back = seq_exchange(cross_out, devices(CROSS_CHIPS))
+    self_ctx, stream_grads = unpack_self(self_back, devices(SELF_CHIPS))
     taken = lax.ppermute(sent, "dp", shifts(groups, 1))
     kept, _ = lax.optimization_barrier((kept, self_ctx))
     weight_grad = add_taken(kept, taken, 2)
-    cross_ctx, stream_grads = unpack_cross(cross_back, stream_grads)
+    cross_ctx, stream_grads = unpack_cross(cross_back, stream_grads, devices(CROSS_CHIPS))
     return (self_ctx, cross_ctx, stream_grads, weight_grad)
 
 

time: 242 us -> 227 us (0.938)
  waiting for transfers between devices: 96.4 us -> 83.7 us
    all_to_all x1, waiting for transfers between devices: 22.2 us -> 12.1 us  [core_exchange(): lax.all_to_all(x, 'seq', split_axis=0, concat_axis=0, tiled=True, axis_in...]
    all_to_all x3, waiting for transfers between devices: 34.5 us -> 31.9 us  [seq_exchange(): lax.all_to_all(x, 'seq', split_axis=0, concat_axis=0, tiled=True, axis_in...]
    unnamed x23 -> x25, local copies, waits for them, and re-layouts: 13.2 us -> 13.2 us
  transfers between devices with their start and end apart: 20 -> 20, of which waited for: 8 -> 8; matrix products, arithmetic and copies ran while one was open for 2% -> 2% of each run, Pallas kernels for 33% -> 34%
where the time goes in v5:
time: 227 us; the launch traced here: 223 us
  waiting for transfers between devices  83.7 us (37%)
  Pallas kernels  81.9 us (36%)
  starting transfers between devices  42.4 us (19%)
  local copies, waits for them, and re-layouts  13.2 us (6%)
    ppermute x9, waiting for transfers between devices, tp_terms(): lax.ppermute(terms[offset], 'tp', shifts(size, offset))  39.7 us
    pallas_call x2, Pallas kernels, self_attention(): pl.pallas_call(functools.partial(self_kernel, steps=steps, per=per), grid...  34.3 us
    all_to_all x3, waiting for transfers between devices, seq_exchange(): lax.all_to_all(x, 'seq', split_axis=0, concat_axis=0, tiled=True, axis_in...  31.9 us
    all_to_all x3, starting transfers between devices, seq_exchange(): lax.all_to_all(x, 'seq', split_axis=0, concat_axis=0, tiled=True, axis_in...  18.1 us
    ppermute x9, starting transfers between devices, tp_terms(): lax.ppermute(terms[offset], 'tp', shifts(size, offset))  14.1 us
    unnamed x25, local copies, waits for them, and re-layouts  13.2 us
    all_to_all x1, waiting for transfers between devices, core_exchange(): lax.all_to_all(x, 'seq', split_axis=0, concat_axis=0, tiled=True, axis_in...  12.1 us
    pallas_call x1, Pallas kernels, cross_attention(): pl.pallas_call(cross_kernel, grid=(chips // per,), in_specs=[pl.BlockSpec...  9.51 us
  transfers between devices with their start and end apart: 20, of which 8 were waited for; matrix products, arithmetic and copies ran while one was open for 2% of the time, Pallas kernels for 34%

profile of v5, /device:TPU:9, one launch (start us, length us, event | category | flops | bytes accessed | tf_op | source)
XLA Modules:
  0.0 222.8 jit_solution(18318405863167746757)
XLA Ops:
  0.6 3.8 %pack.1 = bf16[16,4,128,256]{3,2,1,0:T(8,128)(2,1)} custom-call(bf16[4,1,128,4096]{3,2,1,0:T(8,128)(2,1)} %s_ref.2, bf16[2,1,128,4096]{3,2,1,0:T(8,128)(2,1)} %c_ref.2), custom_call_target="tpu_custom_call" | custom-call | bytes 8388608 | tf_op jit(solution)/shard_map/pack/pallas_call | solution.py:226
  4.4 6.1 %all-to-all-start = ((bf16[16,4,128,256]{3,2,1,0:T(8,128)(2,1)}), bf16[16,4,128,256]{3,2,1,0:T(8,128)(2,1)}, u32[]{:S(2)}, u32[]{:S(2)}) async-start(bf16[16,4,128,256]{3,2,1,0:T(8,128)(2,1)} %pack.1), calls=%async_computation | async-start | bytes 8388608 | tf_op jit(solution)/shard_map/all_to_all | solution.py:609
  10.5 4.2 %pack_cores.1 = (bf16[8,2,128,256]{3,2,1,0:T(8,128)(2,1)}, bf16[8,2,128,256]{3,2,1,0:T(8,128)(2,1)}) custom-call(s32[1]{0:T(128)} %bitcast.4.core_ref, bf16[4,1,128,4096]{3,2,1,0:T(8,128)(2,1)} %s_ref.2, bf16[2,1,128,4096]{3,2,1,0:T(8,128)(2,1)} %c_ref.2), custom_call_target="tpu_custom_call" | custom-call | bytes 4194304 | tf_op jit(solution)/shard_map/pack_cores/pallas_call | solution.py:268
  15.1 8.2 %project.1 = (f32[32,4096]{1,0:T(8,128)}, f32[32,4096]{1,0:T(8,128)}, f32[32,4096]{1,0:T(8,128)}, f32[32,4096]{1,0:T(8,128)}) custom-call(s32[1]{0:T(128)} %bitcast.own_ref, bf16[128,1024]{1,0:T(8,128)(2,1)} %bitcast.11, bf16[1024,4096]{1,0:T(8,128)(2,1)} %w_ref.1, bf16[128,1024]{1,0:T(8,128)(2,1)} %bitcast.12), custom_call_target="tpu_custom_call" | custom-call | flops 1073741824 | bytes 8388608 | tf_op jit(solution)/shard_map/project/pallas_call | solution.py:364
  23.3 1.7 collective-permute-start
  25.0 3.3 %collective-permute-start.1 = (f32[32,4096]{1,0:T(8,128)}, f32[32,4096]{1,0:T(8,128)S(1)}, u32[]{:S(2)}, u32[]{:S(2)}) collective-permute-start(f32[32,4096]{1,0:T(8,128)} %get-tuple-element.40), channel_id=1, source_target_pairs={{0,2},{1,3},{2,0},{3,1},{4,6},{5,7},{6,4},{7,5},{8,10},{9,11},{10,... | collective-permute-start | bytes 1572872 | tf_op jit(solution)/shard_map/ppermute | solution.py:617
  29.0 5.0 %copy.16 = bf16[512,8,2,256]{3,1,2,0:T(8,128)(2,1)} copy(bf16[512,8,2,256]{3,2,1,0:T(2,128)(2,1)} %bitcast.10) | data formatting | bytes 8388608
  34.4 5.2 %collective-permute-done.refs_1_ = f32[32,4096]{1,0:T(8,128)S(1)} collective-permute-done((f32[32,4096]{1,0:T(8,128)}, f32[32,4096]{1,0:T(8,128)S(1)}, u32[]{:S(2)}, u32[]{:S(2)}) %collective-permute-start) | collective-permute-done | bytes 524320 | tf_op jit(solution)/shard_map/ppermute | solution.py:617
  39.6 12.0 %collective-permute-done.1.refs_2_ = f32[32,4096]{1,0:T(8,128)S(1)} collective-permute-done((f32[32,4096]{1,0:T(8,128)}, f32[32,4096]{1,0:T(8,128)S(1)}, u32[]{:S(2)}, u32[]{:S(2)}) %collective-permute-start.1) | collective-permute-done | bytes 524320 | tf_op jit(solution)/shard_map/ppermute | solution.py:617
  52.2 1.9 copy-done
  54.1 9.8 %all-to-all-done.q_ref.k_ref.v_ref.g_ref = bf16[16,4,128,256]{3,2,1,0:T(8,128)(2,1)} async-done(((bf16[16,4,128,256]{3,2,1,0:T(8,128)(2,1)}), bf16[16,4,128,256]{3,2,1,0:T(8,128)(2,1)}, u32[]{:S(2)}, u32[]{:S(2)}) %all-to-all-start) | async-done | bytes 4194336 | tf_op jit(solution)/shard_map/all_to_all | solution.py:609
  63.9 5.5 %all-to-all-start.1 = ((bf16[8,8,128,256]{3,2,1,0:T(8,128)(2,1)}), bf16[8,8,128,256]{3,2,1,0:T(8,128)(2,1)}, u32[]{:S(2)}, u32[]{:S(2)}) async-start(bf16[8,8,128,256]{3,2,1,0:T(8,128)(2,1)} %copy-done), calls=%async_computation.1 | async-start | bytes 8388608 | tf_op jit(solution)/shard_map/all_to_all | solution.py:623
  69.5 17.1 %self_attention.2.rest_0_ = bf16[16,4,128,256]{3,2,1,0:T(8,128)(2,1)S(1)} custom-call(bf16[16,4,128,256]{3,2,1,0:T(8,128)(2,1)} %all-to-all-done.q_ref.k_ref.v_ref.g_ref, bf16[16,4,128,256]{3,2,1,0:T(8,128)(2,1)} %all-to-all-done.q_ref.k_ref.v_ref.g_ref, bf16[16,4,128,256]{3,2,1,0:T(8,128)(2,1)} %all-to-all-done.q_ref.k_ref.v_ref.g_ref, ...), custom_call_target="tpu_custom_call" | custom-call | flops 12884901888 | bytes 4194304 | tf_op jit(solution)/shard_map/self_attention/pallas_call | solution.py:105
  86.6 17.1 %self_attention.3 = bf16[16,4,128,256]{3,2,1,0:T(8,128)(2,1)S(1)} custom-call(bf16[16,4,128,256]{3,2,1,0:T(8,128)(2,1)} %all-to-all-done.q_ref.k_ref.v_ref.g_ref, bf16[16,4,128,256]{3,2,1,0:T(8,128)(2,1)} %all-to-all-done.q_ref.k_ref.v_ref.g_ref, bf16[16,4,128,256]{3,2,1,0:T(8,128)(2,1)} %all-to-all-done.q_ref.k_ref.v_ref.g_ref, ...), custom_call_target="tpu_custom_call", output_to_operand_aliasing={{}: (4, {})} | custom-call | flops 12884901888 | bytes 4194304 | tf_op jit(solution)/shard_map/self_attention/pallas_call | solution.py:105
  103.8 2.0 copy-done.2
  105.8 12.1 %all-to-all-done.1.near_ref.x_ref = bf16[8,8,128,256]{3,2,1,0:T(8,128)(2,1)} async-done(((bf16[8,8,128,256]{3,2,1,0:T(8,128)(2,1)}), bf16[8,8,128,256]{3,2,1,0:T(8,128)(2,1)}, u32[]{:S(2)}, u32[]{:S(2)}) %all-to-all-start.1) | async-done | bytes 4194336 | tf_op jit(solution)/shard_map/all_to_all | solution.py:623
  119.2 4.5 %all-to-all-start.2 = ((bf16[16,4,128,256]{3,2,1,0:T(8,128)(2,1)}), bf16[16,4,128,256]{3,2,1,0:T(8,128)(2,1)}, u32[]{:S(2)}, u32[]{:S(2)}) async-start(bf16[16,4,128,256]{3,2,1,0:T(8,128)(2,1)} %copy-done.2), calls=%async_computation.2 | async-start | bytes 8388608 | tf_op jit(solution)/shard_map/all_to_all | solution.py:609
  124.6 2.0 split_features.1
  128.3 3.3 %collective-permute-start.6 = (bf16[256,1024]{1,0:T(8,128)(2,1)S(1)}, bf16[256,1024]{1,0:T(8,128)(2,1)S(1)}, u32[]{:S(2)}, u32[]{:S(2)}) collective-permute-start(bf16[256,1024]{1,0:T(8,128)(2,1)S(1)} %get-tuple-element.56), channel_id=1, source_target_pairs={{0,2},{1,3},{2,0},{3,1},{4,6},{5,7},{6,4},{7,5},{8,10},{9,11},{10,... | collective-permute-start | bytes 1572872 | tf_op jit(solution)/shard_map/ppermute | solution.py:617
  132.3 5.4 %caption_projection.1.k_ref.v_ref = bf16[512,512]{1,0:T(8,128)(2,1)S(1)} custom-call(bf16[8,8,128,256]{3,2,1,0:T(8,128)(2,1)} %all-to-all-done.1.near_ref.x_ref, bf16[8,8,128,256]{3,2,1,0:T(8,128)(2,1)} %collective-permute-done.4.far_ref, bf16[4096,512]{1,0:T(8,128)(2,1)S(1)} %bitcast.8), custom_call_target="tpu_custom_call" | custom-call | flops 2147483648 | bytes 12582912 | tf_op jit(solution)/shard_map/caption_projection/pallas_call | solution.py:477
  137.7 9.5 %cross_attention.1 = (bf16[16,2,128,256]{3,2,1,0:T(8,128)(2,1)S(1)}, bf16[512,512]{1,0:T(8,128)(2,1)S(1)}) custom-call(s32[1]{0:T(128)} %bitcast.4.core_ref, s32[1]{0:T(128)S(6)} %copy.20.len_ref, s32[1,512]{1,0:T(1,128)S(1)} %add.48.pos_ref, bf16[8,8,128,256]{3,2,1,0:T(8,128)(2,1)} %all-to-all-done.1.near_ref.x_ref, ...), custom_call_target="tpu_custom_call" | custom-call | flops 6000000000 | bytes 5242880 | tf_op jit(solution)/shard_map/cross_attention/pallas_call | solution.py:172
  149.4 1.9 collective-permute-start.14
  151.3 3.7 %collective-permute-done.6.refs_2_ = bf16[256,1024]{1,0:T(8,128)(2,1)S(1)} collective-permute-done((bf16[256,1024]{1,0:T(8,128)(2,1)S(1)}, bf16[256,1024]{1,0:T(8,128)(2,1)S(1)}, u32[]{:S(2)}, u32[]{:S(2)}) %collective-permute-start.6) | collective-permute-done | bytes 524320 | tf_op jit(solution)/shard_map/ppermute | solution.py:617
  155.1 13.6 %collective-permute-done.8.refs_9_ = bf16[512,512]{1,0:T(8,128)(2,1)S(1)} collective-permute-done((bf16[512,512]{1,0:T(8,128)(2,1)S(1)}, bf16[512,512]{1,0:T(8,128)(2,1)S(1)}, u32[]{:S(2)}, u32[]{:S(2)}) %collective-permute-start.8) | collective-permute-done | bytes 524320 | tf_op jit(solution)/shard_map/ppermute | solution.py:617
  170.5 5.2 %collective-permute-done.13.refs_10_ = bf16[512,512]{1,0:T(8,128)(2,1)} collective-permute-done((bf16[512,512]{1,0:T(8,128)(2,1)S(1)}, bf16[512,512]{1,0:T(8,128)(2,1)}, u32[]{:S(2)}, u32[]{:S(2)}) %collective-permute-start.13) | collective-permute-done | bytes 524320 | tf_op jit(solution)/shard_map/ppermute | solution.py:617
  176.7 4.9 %weight_terms.1 = (f32[512,512]{1,0:T(8,128)S(1)}, bf16[512,512]{1,0:T(8,128)(2,1)}) custom-call(s32[1]{0:T(128)} %bitcast.5.own_ref, bf16[256,1024]{1,0:T(8,128)(2,1)S(1)} %get-tuple-element.59.refs_0_, bf16[256,1024]{1,0:T(8,128)(2,1)S(1)} %collective-permute-done.5.refs_1_, bf16[256,1024]{1,0:T(8,128)(2,1)S(1)} %collective-permute-done.6.refs_2_, ...), custom_call_target="tpu_custom_call" | custom-call | flops 2147483648 | bytes 6291456 | tf_op jit(solution)/shard_map/weight_terms/pallas_call | solution.py:558
  182.6 2.0 collective-permute-start.15
  184.6 7.5 %all-to-all-start.3 = ((bf16[16,2,128,256]{3,2,1,0:T(8,128)(2,1)}), bf16[16,2,128,256]{3,2,1,0:T(8,128)(2,1)S(1)}, u32[]{:S(2)}, u32[]{:S(2)}) async-start(bf16[16,2,128,256]{3,2,1,0:T(8,128)(2,1)} %copy-done.3), calls=%async_computation.3 | async-start | bytes 4194304 | tf_op jit(solution)/shard_map/all_to_all | solution.py:609
  192.1 4.9 %unpack_self.1 = (bf16[1,128,4096]{2,1,0:T(8,128)(2,1)}, bf16[4,1,128,4096]{3,2,1,0:T(8,128)(2,1)}) custom-call(bf16[16,4,128,256]{3,2,1,0:T(8,128)(2,1)} %all-to-all-done.2.x_ref), custom_call_target="tpu_custom_call" | custom-call | bytes 8388608 | tf_op jit(solution)/shard_map/unpack_self/pallas_call | solution.py:297
  197.0 1.7 add_taken.1
  198.7 22.1 %all-to-all-done.3.x_ref = bf16[16,2,128,256]{3,2,1,0:T(8,128)(2,1)S(1)} async-done(((bf16[16,2,128,256]{3,2,1,0:T(8,128)(2,1)}), bf16[16,2,128,256]{3,2,1,0:T(8,128)(2,1)S(1)}, u32[]{:S(2)}, u32[]{:S(2)}) %all-to-all-start.3) | async-done | bytes 2097184 | tf_op jit(solution)/shard_map/all_to_all | solution.py:609
  220.9 2.0 unpack_cross.1
  (51 shorter events, 12.0 us)
Async XLA Ops:
  4.4 59.5 %all-to-all-start = ((bf16[16,4,128,256]{3,2,1,0:T(8,128)(2,1)}), bf16[16,4,128,256]{3,2,1,0:T(8,128)(2,1)}, u32[]{:S(2)}, u32[]{:S(2)}) async-start(bf16[16,4,128,256]{3,2,1,0:T(8,128)(2,1)} %pack.1), calls=%async_computation | async-start | bytes 8388608 | tf_op jit(solution)/shard_map/all_to_all | solution.py:609
  14.7 19.3 %collective-permute-start.3 = (bf16[8,2,128,256]{3,2,1,0:T(8,128)(2,1)}, bf16[8,2,128,256]{3,2,1,0:T(8,128)(2,1)S(1)}, u32[]{:S(2)}, u32[]{:S(2)}) collective-permute-start(bf16[8,2,128,256]{3,2,1,0:T(8,128)(2,1)} %get-tuple-element.45), channel_id=1, source_target_pairs={{0,4},{4,0},{8,12},{12,8},{16,20},{20,16},{24,28},{28,24},{32,36},... | collective-permute-start | bytes 3145736 | tf_op jit(solution)/shard_map/ppermute | solution.py:630
  23.3 16.3 %collective-permute-start = (f32[32,4096]{1,0:T(8,128)}, f32[32,4096]{1,0:T(8,128)S(1)}, u32[]{:S(2)}, u32[]{:S(2)}) collective-permute-start(f32[32,4096]{1,0:T(8,128)} %get-tuple-element.39), channel_id=1, source_target_pairs={{0,1},{1,2},{2,3},{3,0},{4,5},{5,6},{6,7},{7,4},{8,9},{9,10},{10,1... | collective-permute-start | bytes 1572872 | tf_op jit(solution)/shard_map/ppermute | solution.py:617
  25.0 26.6 %collective-permute-start.1 = (f32[32,4096]{1,0:T(8,128)}, f32[32,4096]{1,0:T(8,128)S(1)}, u32[]{:S(2)}, u32[]{:S(2)}) collective-permute-start(f32[32,4096]{1,0:T(8,128)} %get-tuple-element.40), channel_id=1, source_target_pairs={{0,2},{1,3},{2,0},{3,1},{4,6},{5,7},{6,4},{7,5},{8,10},{9,11},{10,... | collective-permute-start | bytes 1572872 | tf_op jit(solution)/shard_map/ppermute | solution.py:617
  28.3 23.3 %collective-permute-start.2 = (f32[32,4096]{1,0:T(8,128)}, f32[32,4096]{1,0:T(8,128)S(1)}, u32[]{:S(2)}, u32[]{:S(2)}) collective-permute-start(f32[32,4096]{1,0:T(8,128)} %get-tuple-element.41), channel_id=1, source_target_pairs={{0,3},{1,0},{2,1},{3,2},{4,7},{5,4},{6,5},{7,6},{8,11},{9,8},{10,9... | collective-permute-start | bytes 1572872 | tf_op jit(solution)/shard_map/ppermute | solution.py:617
  29.0 5.1 %copy-start.4 = (bf16[8,2,128,256]{3,2,1,0:T(8,128)(2,1)S(1)}, bf16[8,2,128,256]{3,2,1,0:T(8,128)(2,1)}, u32[]{:S(2)}) copy-start(bf16[8,2,128,256]{3,2,1,0:T(8,128)(2,1)} %get-tuple-element.44.own_ref) | copy-start | bytes 3145732
  34.0 17.6 %copy-start.5 = (f32[32,4096]{1,0:T(8,128)S(1)}, f32[32,4096]{1,0:T(8,128)}, u32[]{:S(2)}) copy-start(f32[32,4096]{1,0:T(8,128)} %get-tuple-element.38.refs_0_) | copy-start | bytes 1572868
  34.0 17.6 %copy-start.6 = (f32[4096]{0:T(1024)S(1)}, f32[4096]{0:T(1024)}, u32[]{:S(2)}) copy-start(f32[4096]{0:T(1024)} %param.12) | copy-start | bytes 49156
  52.2 1.9 copy-start
  63.9 54.0 %all-to-all-start.1 = ((bf16[8,8,128,256]{3,2,1,0:T(8,128)(2,1)}), bf16[8,8,128,256]{3,2,1,0:T(8,128)(2,1)}, u32[]{:S(2)}, u32[]{:S(2)}) async-start(bf16[8,8,128,256]{3,2,1,0:T(8,128)(2,1)} %copy-done), calls=%async_computation.1 | async-start | bytes 8388608 | tf_op jit(solution)/shard_map/all_to_all | solution.py:623
  103.8 2.0 copy-start.2
  105.8 18.5 %copy-start.11 = (s32[8]{0:T(128)S(1)}, s32[8]{0:T(128)}, u32[]{:S(2)}) copy-start(s32[8]{0:T(128)} %constant.40) | copy-start | bytes 100
  117.9 14.4 %collective-permute-start.4 = (bf16[8,8,128,256]{3,2,1,0:T(8,128)(2,1)}, bf16[8,8,128,256]{3,2,1,0:T(8,128)(2,1)}, u32[]{:S(2)}, u32[]{:S(2)}) collective-permute-start(bf16[8,8,128,256]{3,2,1,0:T(8,128)(2,1)} %all-to-all-done.1.near_ref.x_ref), channel_id=1, source_target_pairs={{0,4},{4,0},{8,12},{12,8},{16,20},{20,16},{24,28},{28,24},{32,36},... | collective-permute-start | bytes 12582920 | tf_op jit(solution)/shard_map/ppermute | solution.py:630
  119.2 65.4 %all-to-all-start.2 = ((bf16[16,4,128,256]{3,2,1,0:T(8,128)(2,1)}), bf16[16,4,128,256]{3,2,1,0:T(8,128)(2,1)}, u32[]{:S(2)}, u32[]{:S(2)}) async-start(bf16[16,4,128,256]{3,2,1,0:T(8,128)(2,1)} %copy-done.2), calls=%async_computation.2 | async-start | bytes 8388608 | tf_op jit(solution)/shard_map/all_to_all | solution.py:609
  124.6 7.8 %copy-start.1 = (bf16[512,8,2,256]{3,1,2,0:T(8,128)(2,1)S(1)}, bf16[512,8,2,256]{3,1,2,0:T(8,128)(2,1)}, u32[]{:S(2)}) copy-start(bf16[512,8,2,256]{3,1,2,0:T(8,128)(2,1)} %copy.16) | copy-start | bytes 12582916
  126.6 22.1 %collective-permute-start.5 = (bf16[256,1024]{1,0:T(8,128)(2,1)S(1)}, bf16[256,1024]{1,0:T(8,128)(2,1)S(1)}, u32[]{:S(2)}, u32[]{:S(2)}) collective-permute-start(bf16[256,1024]{1,0:T(8,128)(2,1)S(1)} %get-tuple-element.53), channel_id=1, source_target_pairs={{0,1},{1,2},{2,3},{3,0},{4,5},{5,6},{6,7},{7,4},{8,9},{9,10},{10,1... | collective-permute-start | bytes 1572872 | tf_op jit(solution)/shard_map/ppermute | solution.py:617
  128.3 26.8 %collective-permute-start.6 = (bf16[256,1024]{1,0:T(8,128)(2,1)S(1)}, bf16[256,1024]{1,0:T(8,128)(2,1)S(1)}, u32[]{:S(2)}, u32[]{:S(2)}) collective-permute-start(bf16[256,1024]{1,0:T(8,128)(2,1)S(1)} %get-tuple-element.56), channel_id=1, source_target_pairs={{0,2},{1,3},{2,0},{3,1},{4,6},{5,7},{6,4},{7,5},{8,10},{9,11},{10,... | collective-permute-start | bytes 1572872 | tf_op jit(solution)/shard_map/ppermute | solution.py:617
  131.6 23.5 %collective-permute-start.7 = (bf16[256,1024]{1,0:T(8,128)(2,1)S(1)}, bf16[256,1024]{1,0:T(8,128)(2,1)S(1)}, u32[]{:S(2)}, u32[]{:S(2)}) collective-permute-start(bf16[256,1024]{1,0:T(8,128)(2,1)S(1)} %get-tuple-element.57), channel_id=1, source_target_pairs={{0,3},{1,0},{2,1},{3,2},{4,7},{5,4},{6,5},{7,6},{8,11},{9,8},{10,9... | collective-permute-start | bytes 1572872 | tf_op jit(solution)/shard_map/ppermute | solution.py:617
  147.3 1.4 copy-start.3
  148.7 20.0 %collective-permute-start.8 = (bf16[512,512]{1,0:T(8,128)(2,1)S(1)}, bf16[512,512]{1,0:T(8,128)(2,1)S(1)}, u32[]{:S(2)}, u32[]{:S(2)}) collective-permute-start(bf16[512,512]{1,0:T(8,128)(2,1)S(1)} %get-tuple-element.58.refs_8_), channel_id=1, source_target_pairs={{0,1},{1,2},{2,3},{3,0},{4,5},{5,6},{6,7},{7,4},{8,9},{9,10},{10,1... | collective-permute-start | bytes 1572872 | tf_op jit(solution)/shard_map/ppermute | solution.py:617
  149.4 20.3 %collective-permute-start.14 = (bf16[512,512]{1,0:T(8,128)(2,1)S(1)}, bf16[512,512]{1,0:T(8,128)(2,1)S(1)}, u32[]{:S(2)}, u32[]{:S(2)}) collective-permute-start(bf16[512,512]{1,0:T(8,128)(2,1)S(1)} %get-tuple-element.58.refs_8_), channel_id=1, source_target_pairs={{0,3},{1,0},{2,1},{3,2},{4,7},{5,4},{6,5},{7,6},{8,11},{9,8},{10,9... | collective-permute-start | bytes 1572872 | tf_op jit(solution)/shard_map/ppermute | solution.py:617
  151.3 24.3 %collective-permute-start.13 = (bf16[512,512]{1,0:T(8,128)(2,1)S(1)}, bf16[512,512]{1,0:T(8,128)(2,1)}, u32[]{:S(2)}, u32[]{:S(2)}) collective-permute-start(bf16[512,512]{1,0:T(8,128)(2,1)S(1)} %get-tuple-element.58.refs_8_), channel_id=1, source_target_pairs={{0,2},{1,3},{2,0},{3,1},{4,6},{5,7},{6,4},{7,5},{8,10},{9,11},{10,... | collective-permute-start | bytes 1572872 | tf_op jit(solution)/shard_map/ppermute | solution.py:617
  168.7 7.0 %collective-permute-start.9 = (bf16[256,1024]{1,0:T(8,128)(2,1)S(1)}, bf16[256,1024]{1,0:T(8,128)(2,1)}, u32[]{:S(2)}, u32[]{:S(2)}) collective-permute-start(bf16[256,1024]{1,0:T(8,128)(2,1)S(1)} %get-tuple-element.59.refs_0_), channel_id=1, source_target_pairs={{0,4},{4,0},{8,12},{12,8},{16,20},{20,16},{24,28},{28,24},{32,36},... | collective-permute-start | bytes 1572872 | tf_op jit(solution)/shard_map/ppermute | solution.py:630
  169.2 6.5 %collective-permute-start.10 = (bf16[256,1024]{1,0:T(8,128)(2,1)S(1)}, bf16[256,1024]{1,0:T(8,128)(2,1)}, u32[]{:S(2)}, u32[]{:S(2)}) collective-permute-start(bf16[256,1024]{1,0:T(8,128)(2,1)S(1)} %collective-permute-done.5.refs_1_), channel_id=1, source_target_pairs={{0,4},{4,0},{8,12},{12,8},{16,20},{20,16},{24,28},{28,24},{32,36},... | collective-permute-start | bytes 1572872 | tf_op jit(solution)/shard_map/ppermute | solution.py:630
  169.2 6.5 %collective-permute-start.11 = (bf16[256,1024]{1,0:T(8,128)(2,1)S(1)}, bf16[256,1024]{1,0:T(8,128)(2,1)}, u32[]{:S(2)}, u32[]{:S(2)}) collective-permute-start(bf16[256,1024]{1,0:T(8,128)(2,1)S(1)} %collective-permute-done.6.refs_2_), channel_id=1, source_target_pairs={{0,4},{4,0},{8,12},{12,8},{16,20},{20,16},{24,28},{28,24},{32,36},... | collective-permute-start | bytes 1572872 | tf_op jit(solution)/shard_map/ppermute | solution.py:630
  169.7 0.8 copy-start.7
  170.5 5.2 %collective-permute-start.12 = (bf16[256,1024]{1,0:T(8,128)(2,1)S(1)}, bf16[256,1024]{1,0:T(8,128)(2,1)}, u32[]{:S(2)}, u32[]{:S(2)}) collective-permute-start(bf16[256,1024]{1,0:T(8,128)(2,1)S(1)} %collective-permute-done.7.refs_3_), channel_id=1, source_target_pairs={{0,4},{4,0},{8,12},{12,8},{16,20},{20,16},{24,28},{28,24},{32,36},... | collective-permute-start | bytes 1572872 | tf_op jit(solution)/shard_map/ppermute | solution.py:630
  175.7 1.0 copy-start.8
  181.6 1.0 copy-start.9
  182.6 14.4 %collective-permute-start.15 = (bf16[512,512]{1,0:T(8,128)(2,1)}, bf16[512,512]{1,0:T(8,128)(2,1)S(1)}, u32[]{:S(2)}, u32[]{:S(2)}) collective-permute-start(bf16[512,512]{1,0:T(8,128)(2,1)} %get-tuple-element.63), channel_id=1, source_target_pairs={{0,64},{64,0},{1,65},{65,1},{2,66},{66,2},{3,67},{67,3},{4,68},{68... | collective-permute-start | bytes 1572872 | tf_op jit(solution)/shard_map/ppermute | solution.py:692
  184.6 36.2 %all-to-all-start.3 = ((bf16[16,2,128,256]{3,2,1,0:T(8,128)(2,1)}), bf16[16,2,128,256]{3,2,1,0:T(8,128)(2,1)S(1)}, u32[]{:S(2)}, u32[]{:S(2)}) async-start(bf16[16,2,128,256]{3,2,1,0:T(8,128)(2,1)} %copy-done.3), calls=%async_computation.3 | async-start | bytes 4194304 | tf_op jit(solution)/shard_map/all_to_all | solution.py:609
  192.1 4.9 %copy-start.10 = (f32[512,512]{1,0:T(8,128)S(1)}, f32[512,512]{1,0:T(8,128)}, u32[]{:S(2)}) copy-start(f32[512,512]{1,0:T(8,128)} %copy-done.9) | copy-start | bytes 3145732
